TPU v7x, 256 devices: a whole 4x4x8 slice. The times are simulated.
256 devices in a mesh: space: 64 (over x, z_lo, y), chan: 4 (over z_hi, core).
Axes of the slice: x: 4, y: 4, z: 8 (z_hi: 2, z_lo: 4; z = z_hi * 4 + z_lo), core: 2. Of those that a mesh axis runs over, the one named last changes fastest.
Arguments:
- inputs: float32 [128, 8, 128, 128], P('chan', None, 'space'), may hold values from -6 to 6
- out_grad: float32 [128, 8, 128, 128], P('chan', None, 'space'), may hold values from -6 to 6
- weights: float32 [3, 3, 3, 128, 128], P(None, None, None, 'chan'), may hold values from -0.109375 to 0.109375
Outputs:
- input_grad: float32 [128, 8, 128, 128], P('chan', None, 'space')
- weight_grad: float32 [3, 3, 3, 128, 128], P(None, None, None, 'chan')
All inputs are finite; a program needn't handle non-finite values.
Results may differ from a plain program's by a relative error of at most 0.00025.
Values sent between devices are 32-bit elements; how exact they have to be, the bound alone decides.
No kernel may reach another device: no remote copies, remote signals or barrier semaphores. Data moves between devices by JAX's collectives and lax.ppermute only.
A program may use at most 192 MiB of HBM per device.

v0:
```python
import math

import jax
import jax.numpy as jnp
from jax import lax
from jax.sharding import PartitionSpec as P


def with_halo(value, sides, width):
    for axis, dim in sides:
        peers, length = (lax.axis_size(axis), value.shape[dim])
        up = [(i, (i + 1) % peers) for i in range(peers - 1)]
        down = [(j, i) for i, j in up]
        last = lax.slice_in_dim(value, length - width, length, axis=dim)
        initial = lax.slice_in_dim(value, 0, width, axis=dim)
        before = lax.ppermute(last, axis, up)
        after = lax.ppermute(initial, axis, down)
        value = jnp.concatenate([before, value, after], axis=dim)
    return value


def pad_planes(volume):
    return jnp.pad(volume, ((0, 0), (1, 1), (0, 0), (1, 1)))


def transposed_part(grad_rim, kernel):
    padded = pad_planes(grad_rim)
    plane_count = grad_rim.shape[1]
    row_count = grad_rim.shape[2] - 2
    col_count = grad_rim.shape[3]
    accumulated = jnp.zeros((kernel.shape[3], plane_count, row_count, col_count), jnp.float32)
    for depth_tap in range(3):
        plane_slab = padded[:, 2 - depth_tap : 2 - depth_tap + plane_count]
        for height_tap in range(3):
            products = jnp.einsum(
                "acf,fzhw->aczhw",
                kernel[depth_tap, height_tap],
                plane_slab,
                precision=lax.Precision.HIGHEST,
            )
            for width_tap in range(3):
                accumulated = (
                    accumulated
                    + products[
                        width_tap,
                        :,
                        :,
                        2 - height_tap : 2 - height_tap + row_count,
                        2 - width_tap : 2 - width_tap + col_count,
                    ]
                )
    return accumulated


def weight_part(grad_rim, input_rim):
    grad_core = grad_rim[:, :, 1:-1, :]
    padded = pad_planes(input_rim)
    plane_count = grad_core.shape[1]
    row_count = grad_core.shape[2]
    col_count = grad_core.shape[3]
    collected = []
    for depth_tap in range(3):
        for height_tap in range(3):
            shifted = jnp.stack(
                [
                    padded[
                        :,
                        depth_tap : depth_tap + plane_count,
                        height_tap : height_tap + row_count,
                        width_tap : width_tap + col_count,
                    ]
                    for width_tap in range(3)
                ]
            )
            collected.append(
                jnp.einsum("fzhw,aczhw->acf", grad_core, shifted, precision=lax.Precision.HIGHEST)
            )
    stacked = jnp.stack(collected)
    return stacked.reshape((3, 3, 3, input_rim.shape[0], grad_core.shape[0]))


def per_device(inputs, out_grad, weights):
    input_rim = with_halo(inputs, (("space", 2),), 1)
    grad_rim = with_halo(out_grad, (("space", 2),), 1)
    cell_total = inputs.shape[1] * inputs.shape[2] * lax.axis_size("space") * inputs.shape[3]
    normalizer = 1.0 / math.sqrt(cell_total)
    segment = lax.all_gather(grad_rim, "chan", axis=0, tiled=True)
    grad_total = transposed_part(segment, weights)
    rows_block = weight_part(segment, input_rim)
    weight_table = rows_block
    input_grad, weight_table = (grad_total, weight_table)
    weight_grad = lax.psum(weight_table, "space") * normalizer
    return (input_grad, weight_grad)


def solution(mesh):
    return jax.shard_map(
        per_device,
        mesh=mesh,
        in_specs=(
            P("chan", None, "space", None),
            P("chan", None, "space", None),
            P(None, None, None, "chan", None),
        ),
        out_specs=(P("chan", None, "space", None), P(None, None, None, "chan", None)),
        check_vma=False,
    )
```

profile of v0, /device:TPU:32, one launch (start us, length us, event | category | flops | bytes accessed | tf_op | source)
XLA Modules:
  0.0 828.0 jit_solution(308277940260453446)
XLA Ops:
  7.2 0.0 copy-start.25
  7.2 0.0 all-gather.2.cloned.1.call-start
  7.2 1.0 copy.30
  8.3 3.5 collective-permute-start
  11.7 4.5 collective-permute-start.1
  16.2 1.3 collective-permute-done
  17.5 1.2 collective-permute-done.1
  18.7 0.8 pad_maximum_fusion
  19.6 0.0 all-gather.2.cloned.1.call-update
  19.6 0.0 all-reduce.4.cloned.1.call-start
  19.6 0.0 copy-done.25
  19.6 0.1 copy.121
  19.8 3.4 collective-permute-start.2
  23.2 5.0 collective-permute-start.3
  28.2 1.0 collective-permute-done.2
  29.2 1.5 collective-permute-done.3
  30.7 0.8 fusion.98
  31.5 0.3 select_maximum_fusion
  31.8 1.2 slice_bitcast_fusion
  33.0 2.9 slice_bitcast_fusion.2
  35.9 32.3 %all-gather.2.cloned.1.call-done = f32[128,8,4,128]{3,1,2,0:T(8,128)} async-done(((f32[32,8,4,128]{3,1,2,0:T(8,128)}), f32[128,8,4,128]{3,1,2,0:T(8,128)}) %all-gather.2.cloned.1.call-update) | async-done | bytes 2097168 | tf_op jit(solution)/shard_map/all_gather | solution.py:87
  68.2 2.5 copy.33
  70.7 0.0 copy-start.23
  70.8 6.7 convolution_bitcast_fusion
  77.5 0.0 copy-done.23
  77.5 5.9 convolution_bitcast_fusion.1
  83.4 5.9 convolution_bitcast_fusion.2
  89.3 5.9 convolution_bitcast_fusion.3
  95.2 6.1 convolution_bitcast_fusion.4
  101.2 5.9 convolution_bitcast_fusion.5
  107.1 6.1 fusion.11
  113.2 6.3 fusion.14
  119.5 0.0 copy-done
  119.6 0.0 copy-start.12
  119.6 0.0 copy-start.19
  119.6 0.0 copy-start.20
  119.6 0.1 slice.320
  119.7 0.8 copy-done.16
  120.5 0.1 copy-done.17
  120.6 0.1 copy-done.18
  120.7 1.3 fusion.34
  121.9 0.0 copy-start.11
  122.0 0.0 copy-start.22
  122.0 0.0 copy-done.12
  122.0 0.0 copy-done.19
  122.0 0.0 copy-done.20
  122.0 1.3 fusion.33
  123.3 1.3 fusion.32
  124.7 1.3 fusion.31
  126.0 1.3 fusion.30
  127.3 1.3 fusion.29
  128.6 0.0 copy-done.3
  128.6 1.3 fusion.28
  129.9 0.0 copy-done.1
  129.9 1.3 fusion.27
  131.2 1.3 fusion.26
  132.5 0.0 copy-start.24
  132.5 0.8 copy-done.24
  133.2 0.0 all-reduce.4.cloned.1.call-update
  133.3 5.6 fusion.8
  138.8 5.3 fusion.100
  144.2 0.9 copy.47
  145.1 673.9 %all-reduce.4.cloned.1.call-done = f32[3,3,3,32,128]{4,3,2,1,0:T(8,128)} async-done(((f32[3,3,3,32,128]{4,3,2,1,0:T(8,128)}), f32[3,3,3,32,128]{4,3,2,1,0:T(8,128)}) %all-reduce.4.cloned.1.call-update) | async-done | bytes 442384 | tf_op jit(solution)/shard_map/psum | solution.py:92
  819.0 1.8 broadcast_multiply_fusion
  (34 shorter events, 0.1 us)
Async XLA Ops:
  7.2 12.5 %copy-start.25 = (f32[32,8,2,128]{3,2,1,0:T(2,128)S(1)}, f32[32,8,2,128]{3,2,1,0:T(2,128)}, u32[]{:S(2)}) copy-start(f32[32,8,2,128]{3,2,1,0:T(2,128)} %param.3) | copy-start | bytes 786436
  7.2 61.0 %all-gather.2.cloned.1.call-start = ((), (), s32[]{:S(2)}) async-start(), calls=%async_computation | async-start | bytes 2621440 | tf_op jit(solution)/shard_map/all_gather | solution.py:87
  8.3 9.2 %collective-permute-start = (f32[32,8,1,128]{3,1,2,0:T(8,128)S(1)}, f32[32,8,1,128]{3,1,2,0:T(8,128)S(1)}, u32[]{:S(2)}, u32[]{:S(2)}) collective-permute-start(f32[32,8,1,128]{3,1,2,0:T(8,128)S(1)} %get-tuple-element.36), channel_id=1, source_target_pairs={{0,4},{4,8},{8,12},{12,16},{16,20},{20,24},{24,28},{28,32},{32,36}... | collective-permute-start | bytes 393224 | tf_op jit(solution)/shard_map/ppermute | solution.py:16
  11.7 7.0 collective-permute-start.1
  19.6 799.4 %all-reduce.4.cloned.1.call-start = ((), (), s32[]{:S(2)}) async-start(), calls=%async_computation.1 | async-start | bytes 884736 | tf_op jit(solution)/shard_map/psum | solution.py:92
  19.8 9.4 %collective-permute-start.2 = (f32[32,8,1,128]{3,0,1,2:T(8,128)S(1)}, f32[32,8,1,128]{3,0,1,2:T(8,128)S(1)}, u32[]{:S(2)}, u32[]{:S(2)}) collective-permute-start(f32[32,8,1,128]{3,0,1,2:T(8,128)S(1)} %get-tuple-element.34), channel_id=1, source_target_pairs={{0,4},{4,8},{8,12},{12,16},{16,20},{20,24},{24,28},{28,32},{32,36}... | collective-permute-start | bytes 393224 | tf_op jit(solution)/shard_map/ppermute | solution.py:16
  23.2 7.5 collective-permute-start.3
  70.7 6.7 copy-start.23
  113.2 6.3 copy-start
  119.5 1.0 copy-start.16
  119.6 1.0 copy-start.17
  119.6 1.1 copy-start.18
  119.6 2.4 copy-start.12
  119.6 2.4 copy-start.19
  119.6 2.4 copy-start.20
  119.7 3.6 copy-start.13
  119.7 3.6 copy-start.14
  119.7 3.6 copy-start.15
  121.9 2.7 copy-start.10
  121.9 2.7 copy-start.11
  122.0 2.7 copy-start.22
  123.3 2.7 copy-start.8
  123.3 2.7 copy-start.9
  124.6 2.7 copy-start.6
  124.6 2.7 copy-start.7
  124.6 2.7 copy-start.21
  125.9 2.7 copy-start.3
  125.9 2.7 copy-start.4
  126.0 2.7 copy-start.5
  127.3 2.6 copy-start.1
  127.3 2.6 copy-start.2
  132.5 0.8 copy-start.24
Sparse Core Ops, SparseCore 0:
  19.7 48.4 all-gather.1
  133.4 685.6 all-reduce.3
where the time goes:
time: 834 us; the launch traced here: 828 us
  waiting for transfers between devices  711 us (85%)
  matrix products  65.8 us (8%)
  starting transfers between devices  16.4 us (2%)
  between operations  14.7 us (2%)
  local copies, waits for them, and re-layouts  10.5 us (1%)
  other arithmetic  9.17 us (1%)
    psum x1, waiting for transfers between devices, per_device(): weight_grad = lax.psum(weight_table, 'space') * normalizer  674 us
    dot_general x9, matrix products, transposed_part(): jnp.einsum('acf,fzhw->aczhw', kernel[depth_tap, height_tap], plane_slab,...  54.4 us
    all_gather x1, waiting for transfers between devices, per_device(): segment = lax.all_gather(grad_rim, 'chan', axis=0, tiled=True)  32.3 us
  transfers between devices with their start and end apart: 6, of which 6 were waited for; matrix products, arithmetic and copies ran while one was open for 2% of the time, Pallas kernels for 0%

commit v1 on v0

v1 whole, which is shorter than its diff:
```python
import math

import jax
import jax.numpy as jnp
from jax import lax
from jax.experimental import pallas as pl
from jax.experimental.pallas import tpu as pltpu
from jax.sharding import PartitionSpec as P

BF = jnp.bfloat16
F32 = jnp.float32


def split(value):
    high = value.astype(BF)
    return high, (value - high.astype(F32)).astype(BF)


def shifted(value, step):
    lanes = value.shape[1]
    lane = lax.broadcasted_iota(jnp.int32, value.shape, 1)
    edge = lanes - 1 if step > 0 else 0
    return jnp.where(lane == edge, 0.0, pltpu.roll(value, (-step) % lanes, 1))


def load_grads(parts, grads, chan):
    filters = grads.shape[0] // 2
    count = filters // len(parts)
    pairs = parts[0].shape[0] // count
    for j, part in enumerate(parts):
        start = pl.multiple_of((chan ^ j) * count, count)
        for r in range(pairs):
            high, low = split(part[pl.ds(r, count, stride=pairs), :])
            grads[pl.ds(start, count), r * 128 : (r + 1) * 128] = high
            grads[pl.ds(filters + start, count), r * 128 : (r + 1) * 128] = low


def weight_kernel(scale, planes, x, above, below, g0, g1, g2, g3, out, cells, grads):
    chan = lax.axis_index("chan")
    load_grads((g0, g1, g2, g3), grads, chan)
    count = x.shape[0] // (2 * planes)
    filters = grads.shape[0] // 2
    cells[:, : 4 * 128] = jnp.zeros((cells.shape[0], 4 * 128), BF)
    cells[:, (planes + 1) * 512 :] = jnp.zeros((cells.shape[0], 512), BF)
    for d in range(planes):
        for r in range(4):
            if r == 0:
                value = above[pl.ds(d, count, stride=planes), :]
            elif r == 3:
                value = below[pl.ds(d, count, stride=planes), :]
            else:
                value = x[pl.ds(2 * d + r - 1, count, stride=2 * planes), :]
            at = ((d + 1) * 4 + r) * 128
            for kw in range(3):
                moved = value if kw == 1 else shifted(value, kw - 1)
                high, low = split(moved)
                cells[kw * 2 * count : (kw * 2 + 1) * count, at : at + 128] = high
                cells[(kw * 2 + 1) * count : (kw * 2 + 2) * count, at : at + 128] = low
    for kd in range(3):
        for kh in range(3):
            left = jnp.concatenate(
                [
                    cells[:, ((d + kd) * 4 + kh) * 128 : ((d + kd) * 4 + kh) * 128 + 256]
                    for d in range(planes)
                ],
                axis=1,
            )
            full = lax.dot_general(
                left, grads[...], (((1,), (1,)), ((), ())), preferred_element_type=F32
            )
            for kw in range(3):
                high = full[kw * 2 * count : (kw * 2 + 1) * count]
                low = full[(kw * 2 + 1) * count : (kw * 2 + 2) * count]
                total = high[:, :filters] + (high[:, filters:] + low[:, :filters])
                tap = (kd * 3 + kh) * 3 + kw
                out[tap * count : (tap + 1) * count, :] = total * scale


def input_kernel(planes, w, g0, g1, g2, g3, out, above, below, left, grads):
    chan = lax.axis_index("chan")
    load_grads((g0, g1, g2, g3), grads, chan)
    count = w.shape[0] // 27
    filters = grads.shape[0] // 2
    block = 9 * count
    for kd in range(3):
        high, low = split(w[kd * block : (kd + 1) * block, :])
        left[:, (kd * 3) * filters : (kd * 3 + 1) * filters] = high
        left[:, (kd * 3 + 1) * filters : (kd * 3 + 2) * filters] = low
        left[:, (kd * 3 + 2) * filters : (kd * 3 + 3) * filters] = high
    for q in range(planes):
        taps = [kd for kd in range(3) if 0 <= q - kd + 1 < planes]
        right = []
        for kd in taps:
            d = q - kd + 1
            high = grads[:filters, d * 256 : (d + 1) * 256]
            right += [high, high, grads[filters:, d * 256 : (d + 1) * 256]]
        full = jnp.dot(
            left[:, taps[0] * 3 * filters : (taps[-1] + 1) * 3 * filters],
            jnp.concatenate(right, axis=0),
            preferred_element_type=F32,
        )

        def term(kh, kw, h):
            at = (kh * 3 + kw) * count
            return full[at : at + count, h * 128 : (h + 1) * 128]

        def row(pairs):
            sums = []
            for kw in range(3):
                values = [term(kh, kw, h) for kh, h in pairs]
                sums.append(sum(values[1:], values[0]))
            return shifted(sums[0], 1) + sums[1] + shifted(sums[2], -1)

        out[pl.ds(2 * q, count, stride=2 * planes), :] = row([(1, 0), (0, 1)])
        out[pl.ds(2 * q + 1, count, stride=2 * planes), :] = row([(2, 0), (1, 1)])
        above[pl.ds(q, count, stride=planes), :] = row([(0, 0)])
        below[pl.ds(q, count, stride=planes), :] = row([(2, 1)])


AXES = 4


def place(deltas):
    pairs = []
    for i in range(AXES**3):
        x, z, y = i // (AXES * AXES), (i // AXES) % AXES, i % AXES
        pairs.append((i, ((x ^ deltas[0]) * AXES + (z ^ deltas[1])) * AXES + (y ^ deltas[2])))
    return pairs


def toward(axis, step):
    deltas = [0, 0, 0]
    deltas[axis] = step
    return place(deltas)


def sum_over_space(value):
    me = lax.axis_index("space")
    last = me % AXES
    length = value.shape[0] // AXES

    def piece(index):
        return lax.dynamic_slice_in_dim(value, index * length, length, 0)

    total = piece(last)
    for k in (1, 2, 3):
        total = total + lax.ppermute(piece(last ^ k), "space", toward(2, k))
    for axis in (0, 1):
        held = total
        for k in (1, 2, 3):
            total = total + lax.ppermute(held, "space", toward(axis, k))
    parts = [total] + [lax.ppermute(total, "space", toward(2, k)) for k in (1, 2, 3)]
    result = jnp.zeros(value.shape, value.dtype)
    for k in range(4):
        result = lax.dynamic_update_slice_in_dim(result, parts[k], (last ^ k) * length, 0)
    return result


def per_device(inputs, out_grad, weights):
    channels, planes, rows, cols = inputs.shape
    filters = weights.shape[4]
    cell_total = planes * rows * lax.axis_size("space") * cols
    scale = 1.0 / math.sqrt(cell_total)
    x = inputs.reshape(-1, cols)
    g0 = out_grad.reshape(-1, cols)
    w = weights.reshape(-1, filters)
    peers = lax.axis_size("space")
    up = [(i, i + 1) for i in range(peers - 1)]
    down = [(j, i) for i, j in up]
    g2 = lax.ppermute(g0, "chan", [(i, i ^ 2) for i in range(4)])
    g1 = lax.ppermute(g0, "chan", [(i, i ^ 1) for i in range(4)])
    above = lax.ppermute(inputs[:, :, 1, :].reshape(-1, cols), "space", up)
    below = lax.ppermute(inputs[:, :, 0, :].reshape(-1, cols), "space", down)
    g3 = lax.ppermute(g2, "chan", [(i, i ^ 1) for i in range(4)])
    cells = planes * rows * cols

    def vmem(n):
        return [pl.BlockSpec(memory_space=pltpu.VMEM)] * n

    partial = pl.pallas_call(
        lambda *refs: weight_kernel(scale, planes, *refs),
        out_shape=jax.ShapeDtypeStruct((27 * channels, filters), F32),
        in_specs=vmem(7),
        out_specs=vmem(1)[0],
        scratch_shapes=[
            pltpu.VMEM((6 * channels, (planes + 2) * 4 * cols), BF),
            pltpu.VMEM((2 * filters, cells), BF),
        ],
        compiler_params=pltpu.CompilerParams(vmem_limit_bytes=48 * 1024 * 1024),
        cost_estimate=pl.CostEstimate(
            flops=6 * 27 * channels * filters * cells, bytes_accessed=2**21, transcendentals=0
        ),
        name="weight_kernel",
    )(x, above, below, g0, g1, g2, g3)
    halo = jax.ShapeDtypeStruct((channels * planes, cols), F32)
    core, to_above, to_below = pl.pallas_call(
        lambda *refs: input_kernel(planes, *refs),
        out_shape=(jax.ShapeDtypeStruct(x.shape, F32), halo, halo),
        in_specs=vmem(5),
        out_specs=tuple(vmem(3)),
        scratch_shapes=[
            pltpu.VMEM((9 * channels, 9 * filters), BF),
            pltpu.VMEM((2 * filters, cells), BF),
        ],
        compiler_params=pltpu.CompilerParams(vmem_limit_bytes=48 * 1024 * 1024),
        cost_estimate=pl.CostEstimate(
            flops=6 * 27 * channels * filters * cells, bytes_accessed=2**21, transcendentals=0
        ),
        name="input_kernel",
    )(w, g0, g1, g2, g3)
    from_above = lax.ppermute(to_below, "space", up).reshape(channels, planes, cols)
    from_below = lax.ppermute(to_above, "space", down).reshape(channels, planes, cols)
    input_grad = core.reshape(inputs.shape) + jnp.stack([from_above, from_below], axis=2)
    weight_grad = sum_over_space(partial).reshape(3, 3, 3, channels, filters)
    return (input_grad, weight_grad)


def solution(mesh):
    return jax.shard_map(
        per_device,
        mesh=mesh,
        in_specs=(
            P("chan", None, "space", None),
            P("chan", None, "space", None),
            P(None, None, None, "chan", None),
        ),
        out_specs=(P("chan", None, "space", None), P(None, None, None, "chan", None)),
        check_vma=False,
    )
```

time: 834 us -> 87.6 us (0.11)
  the two profiles are of different devices: /device:TPU:32 before, /device:TPU:248 now
where the time goes in v1:
time: 87.6 us; the launch traced here: 87.4 us
  waiting for transfers between devices  48.6 us (55%)
  starting transfers between devices  28.9 us (33%)
  Pallas kernels  5.8 us (7%)
  local copies, waits for them, and re-layouts  2.13 us (2%)
  other arithmetic  1.11 us (1%)
    ppermute x1, waiting for transfers between devices, per_device(): g2 = lax.ppermute(g0, 'chan', [(i, i ^ 2) for i in range(4)])  13.8 us
    ppermute x1, waiting for transfers between devices, per_device(): below = lax.ppermute(inputs[:, :, 0, :].reshape(-1, cols), 'space', down)  8.92 us
    ppermute x6, starting transfers between devices, sum_over_space(): total = total + lax.ppermute(held, 'space', toward(axis, k))  8.63 us
    ppermute x1, waiting for transfers between devices, per_device(): lax.ppermute(to_above, 'space', down).reshape(channels, planes, cols)  7.85 us
    ppermute x3, waiting for transfers between devices, sum_over_space(): lax.ppermute(total, 'space', toward(2, k))  7.1 us
    ppermute x1, starting transfers between devices, per_device(): above = lax.ppermute(inputs[:, :, 1, :].reshape(-1, cols), 'space', up)  6.3 us
    ppermute x6, waiting for transfers between devices, sum_over_space(): total = total + lax.ppermute(held, 'space', toward(axis, k))  4.53 us
    ppermute x3, starting transfers between devices, sum_over_space(): total = total + lax.ppermute(piece(last ^ k), 'space', toward(2, k))  4.17 us
  transfers between devices with their start and end apart: 19, of which 11 were waited for; matrix products, arithmetic and copies ran while one was open for 3% of the time, Pallas kernels for 2%

profile of v1, /device:TPU:248, one launch (start us, length us, event | category | flops | bytes accessed | tf_op | source)
XLA Modules:
  0.0 87.4 jit_solution(18232120709547842465)
XLA Ops:
  0.6 0.0 copy-start
  0.6 0.0 copy-start.2
  0.6 1.5 %collective-permute-start.1 = (f32[512,128]{1,0:T(8,128)}, f32[512,128]{1,0:T(8,128)S(1)}, u32[]{:S(2)}, u32[]{:S(2)}) collective-permute-start(f32[512,128]{1,0:T(8,128)} %bitcast.16), channel_id=1, source_target_pairs={{0,2},{1,3},{2,0},{3,1},{4,6},{5,7},{6,4},{7,5},{8,10},{9,11},{10,... | collective-permute-start | bytes 786440 | tf_op jit(solution)/shard_map/ppermute | solution.py:170
  2.2 0.0 collective-permute-start
  2.2 13.8 %collective-permute-done.1.refs_3_.refs_5_ = f32[512,128]{1,0:T(8,128)S(1)} collective-permute-done((f32[512,128]{1,0:T(8,128)}, f32[512,128]{1,0:T(8,128)S(1)}, u32[]{:S(2)}, u32[]{:S(2)}) %collective-permute-start.1) | collective-permute-done | bytes 262176 | tf_op jit(solution)/shard_map/ppermute | solution.py:170
  16.0 0.0 collective-permute-start.2
  16.0 1.3 %fusion = (f32[32,8,1,128]{3,2,1,0:T(1,128)S(1)}, f32[32,8,1,128]{3,2,1,0:T(1,128)S(1)}) fusion(f32[32,8,2,128]{3,2,1,0:T(2,128)} %param.3), kind=kLoop, calls=%fused_computation.11 | loop fusion | bytes 524288 | tf_op jit(solution)/shard_map/slice | solution.py:173
  17.2 6.3 %collective-permute-start.5 = (f32[256,128]{1,0:T(8,128)S(1)}, f32[256,128]{1,0:T(8,128)S(1)}, u32[]{:S(2)}, u32[]{:S(2)}) collective-permute-start(f32[256,128]{1,0:T(8,128)S(1)} %bitcast.22), channel_id=1, source_target_pairs={{0,4},{4,8},{8,12},{12,16},{16,20},{20,24},{24,28},{28,32},{32,36}... | collective-permute-start | bytes 393224 | tf_op jit(solution)/shard_map/ppermute | solution.py:172
  23.5 1.9 %collective-permute-start.6 = (f32[256,128]{1,0:T(8,128)S(1)}, f32[256,128]{1,0:T(8,128)S(1)}, u32[]{:S(2)}, u32[]{:S(2)}) collective-permute-start(f32[256,128]{1,0:T(8,128)S(1)} %bitcast.21), channel_id=1, source_target_pairs={{4,0},{8,4},{12,8},{16,12},{20,16},{24,20},{28,24},{32,28},{36,32}... | collective-permute-start | bytes 393224 | tf_op jit(solution)/shard_map/ppermute | solution.py:173
  25.5 1.4 %collective-permute-done.5.refs_1_ = f32[256,128]{1,0:T(8,128)S(1)} collective-permute-done((f32[256,128]{1,0:T(8,128)S(1)}, f32[256,128]{1,0:T(8,128)S(1)}, u32[]{:S(2)}, u32[]{:S(2)}) %collective-permute-start.5) | collective-permute-done | bytes 131104 | tf_op jit(solution)/shard_map/ppermute | solution.py:172
  26.9 8.9 %collective-permute-done.6.refs_2_ = f32[256,128]{1,0:T(8,128)S(1)} collective-permute-done((f32[256,128]{1,0:T(8,128)S(1)}, f32[256,128]{1,0:T(8,128)S(1)}, u32[]{:S(2)}, u32[]{:S(2)}) %collective-permute-start.6) | collective-permute-done | bytes 131104 | tf_op jit(solution)/shard_map/ppermute | solution.py:173
  35.9 0.0 collective-permute-done.refs_2_.refs_4_
  35.9 0.0 collective-permute-done.2.refs_4_.refs_6_
  35.9 0.0 copy-done
  35.9 0.0 copy-done.2
  35.9 3.7 %weight_kernel.1 = f32[864,128]{1,0:T(8,128)S(1)} custom-call(f32[512,128]{1,0:T(8,128)S(1)} %bitcast.14, f32[256,128]{1,0:T(8,128)S(1)} %collective-permute-done.5.refs_1_, f32[256,128]{1,0:T(8,128)S(1)} %collective-permute-done.6.refs_2_, f32[512,128]{1,0:T(8,128)S(1)} %bitcast.18, f32[512,128]{1,0:T(8,128)S(1)} %collective-permute-done.refs_2_.refs_4_, ...), custom_call_target="tpu_custom_call" | custom-call | flops 1358954496 | bytes 2097152 | tf_op jit(solution)/shard_map/weight_kernel/pallas_call | solution.py:180
  39.7 0.1 collective-permute-start.7
  39.8 0.1 collective-permute-start.9
  39.9 4.0 %collective-permute-start.8 = (f32[216,128]{1,0:T(8,128)S(1)}, f32[216,128]{1,0:T(8,128)S(1)}, u32[]{:S(2)}, u32[]{:S(2)}) collective-permute-start(f32[216,128]{1,0:T(8,128)S(1)} %get-tuple-element.12), channel_id=1, source_target_pairs={{0,8},{4,12},{8,0},{12,4},{16,24},{20,28},{24,16},{28,20},{32,40},... | collective-permute-start | bytes 331784 | tf_op jit(solution)/shard_map/ppermute | solution.py:147
  43.9 0.0 copy-start.1
  43.9 1.5 %collective-permute-done.7 = f32[216,128]{1,0:T(8,128)S(1)} collective-permute-done((f32[216,128]{1,0:T(8,128)S(1)}, f32[216,128]{1,0:T(8,128)S(1)}, u32[]{:S(2)}, u32[]{:S(2)}) %collective-permute-start.7) | collective-permute-done | bytes 110624 | tf_op jit(solution)/shard_map/ppermute | solution.py:147
  45.4 2.4 %collective-permute-done.9 = f32[216,128]{1,0:T(8,128)S(1)} collective-permute-done((f32[216,128]{1,0:T(8,128)S(1)}, f32[216,128]{1,0:T(8,128)S(1)}, u32[]{:S(2)}, u32[]{:S(2)}) %collective-permute-start.9) | collective-permute-done | bytes 110624 | tf_op jit(solution)/shard_map/ppermute | solution.py:147
  47.8 0.0 collective-permute-done.8
  47.8 0.1 collective-permute-start.12
  47.9 3.5 %collective-permute-start.11 = (f32[216,128]{1,0:T(8,128)S(1)}, f32[216,128]{1,0:T(8,128)S(1)}, u32[]{:S(2)}, u32[]{:S(2)}) collective-permute-start(f32[216,128]{1,0:T(8,128)S(1)} %add_add_fusion.2), channel_id=1, source_target_pairs={{0,128},{4,132},{8,136},{12,140},{16,144},{20,148},{24,152},{28,15... | collective-permute-start | bytes 331784 | tf_op jit(solution)/shard_map/ppermute | solution.py:151
  51.5 0.5 collective-permute-start.10
  52.0 3.9 %collective-permute-done.12 = f32[216,128]{1,0:T(8,128)S(1)} collective-permute-done((f32[216,128]{1,0:T(8,128)S(1)}, f32[216,128]{1,0:T(8,128)S(1)}, u32[]{:S(2)}, u32[]{:S(2)}) %collective-permute-start.12) | collective-permute-done | bytes 110624 | tf_op jit(solution)/shard_map/ppermute | solution.py:151
  55.9 0.0 collective-permute-done.11
  55.9 0.6 collective-permute-done.10
  56.6 0.1 collective-permute-start.15
  56.7 0.1 collective-permute-start.14
  56.8 4.3 %collective-permute-start.13 = (f32[216,128]{1,0:T(8,128)S(1)}, f32[216,128]{1,0:T(8,128)S(1)}, u32[]{:S(2)}, u32[]{:S(2)}) collective-permute-start(f32[216,128]{1,0:T(8,128)S(1)} %add_add_fusion.1), channel_id=1, source_target_pairs={{0,16},{4,20},{8,24},{12,28},{16,0},{20,4},{24,8},{28,12},{32,48},... | collective-permute-start | bytes 331784 | tf_op jit(solution)/shard_map/ppermute | solution.py:151
  61.1 0.0 copy-done.1
  61.1 2.1 %input_kernel.1 = (f32[512,128]{1,0:T(8,128)S(1)}, f32[256,128]{1,0:T(8,128)S(1)}, f32[256,128]{1,0:T(8,128)S(1)}) custom-call(f32[864,128]{1,0:T(8,128)S(1)} %bitcast.15, f32[512,128]{1,0:T(8,128)S(1)} %bitcast.19, f32[512,128]{1,0:T(8,128)S(1)} %collective-permute-done.refs_2_.refs_4_, f32[512,128]{1,0:T(8,128)S(1)} %collective-permute-done.1.refs_3_.refs_5_, ...), custom_call_target="tpu_custom_call" | custom-call | flops 1358954496 | bytes 2097152 | tf_op jit(solution)/shard_map/input_kernel/pallas_call | solution.py:196
  63.1 3.7 %collective-permute-start.3 = (f32[256,128]{1,0:T(8,128)S(1)}, f32[256,128]{1,0:T(8,128)S(1)}, u32[]{:S(2)}, u32[]{:S(2)}) collective-permute-start(f32[256,128]{1,0:T(8,128)S(1)} %get-tuple-element.6), channel_id=1, source_target_pairs={{0,4},{4,8},{8,12},{12,16},{16,20},{20,24},{24,28},{28,32},{32,36}... | collective-permute-start | bytes 393224 | tf_op jit(solution)/shard_map/ppermute | solution.py:211
  66.8 2.1 %collective-permute-start.4 = (f32[256,128]{1,0:T(8,128)S(1)}, f32[256,128]{1,0:T(8,128)S(1)}, u32[]{:S(2)}, u32[]{:S(2)}) collective-permute-start(f32[256,128]{1,0:T(8,128)S(1)} %get-tuple-element.7), channel_id=1, source_target_pairs={{4,0},{8,4},{12,8},{16,12},{20,16},{24,20},{28,24},{32,28},{36,32}... | collective-permute-start | bytes 393224 | tf_op jit(solution)/shard_map/ppermute | solution.py:212
  69.0 0.0 collective-permute-done.15
  69.0 0.0 collective-permute-done.14
  69.0 0.0 collective-permute-done.13
  69.1 0.5 collective-permute-start.16
  69.6 1.0 %collective-permute-done.3 = f32[256,128]{1,0:T(8,128)S(1)} collective-permute-done((f32[256,128]{1,0:T(8,128)S(1)}, f32[256,128]{1,0:T(8,128)S(1)}, u32[]{:S(2)}, u32[]{:S(2)}) %collective-permute-start.3) | collective-permute-done | bytes 131104 | tf_op jit(solution)/shard_map/ppermute | solution.py:211
  70.7 7.8 %collective-permute-done.4 = f32[256,128]{1,0:T(8,128)S(1)} collective-permute-done((f32[256,128]{1,0:T(8,128)S(1)}, f32[256,128]{1,0:T(8,128)S(1)}, u32[]{:S(2)}, u32[]{:S(2)}) %collective-permute-start.4) | collective-permute-done | bytes 131104 | tf_op jit(solution)/shard_map/ppermute | solution.py:212
  78.5 1.0 %maximum_add_fusion = f32[32,8,2,128]{3,2,1,0:T(2,128)} fusion(f32[32,8,2,128]{3,2,1,0:T(2,128)S(1)} %bitcast.13, f32[32,8,1,128]{3,2,1,0:T(1,128)S(1)} %bitcast.24, f32[32,8,1,128]{3,2,1,0:T(1,128)S(1)} %bitcast.23), kind=kLoop, calls=%fused_computation | loop fusion | flops 131072 | bytes 786432 | tf_op jit(solution)/shard_map/add | solution.py:213
  79.5 0.0 collective-permute-start.17
  79.5 0.0 collective-permute-start.18
  79.5 0.0 collective-permute-done.16
  79.5 6.3 %collective-permute-done.17 = f32[216,128]{1,0:T(8,128)S(1)} collective-permute-done((f32[216,128]{1,0:T(8,128)S(1)}, f32[216,128]{1,0:T(8,128)S(1)}, u32[]{:S(2)}, u32[]{:S(2)}) %collective-permute-start.17) | collective-permute-done | bytes 110624 | tf_op jit(solution)/shard_map/ppermute | solution.py:152
  85.9 0.8 collective-permute-done.18
  86.7 0.0 copy-start.3
  86.7 0.8 copy-done.3
  (8 shorter events, 0.2 us)
Async XLA Ops:
  0.6 35.2 %copy-start = (f32[32,8,2,128]{3,2,1,0:T(2,128)S(1)}, f32[32,8,2,128]{3,2,1,0:T(2,128)}, u32[]{:S(2)}) copy-start(f32[32,8,2,128]{3,2,1,0:T(2,128)} %param.3) | copy-start | bytes 786436
  0.6 35.2 %copy-start.2 = (f32[32,8,2,128]{3,2,1,0:T(2,128)S(1)}, f32[32,8,2,128]{3,2,1,0:T(2,128)}, u32[]{:S(2)}) copy-start(f32[32,8,2,128]{3,2,1,0:T(2,128)} %param.4) | copy-start | bytes 786436
  0.6 15.3 %collective-permute-start.1 = (f32[512,128]{1,0:T(8,128)}, f32[512,128]{1,0:T(8,128)S(1)}, u32[]{:S(2)}, u32[]{:S(2)}) collective-permute-start(f32[512,128]{1,0:T(8,128)} %bitcast.16), channel_id=1, source_target_pairs={{0,2},{1,3},{2,0},{3,1},{4,6},{5,7},{6,4},{7,5},{8,10},{9,11},{10,... | collective-permute-start | bytes 786440 | tf_op jit(solution)/shard_map/ppermute | solution.py:170
  2.2 33.7 %collective-permute-start = (f32[512,128]{1,0:T(8,128)}, f32[512,128]{1,0:T(8,128)S(1)}, u32[]{:S(2)}, u32[]{:S(2)}) collective-permute-start(f32[512,128]{1,0:T(8,128)} %bitcast.17), channel_id=1, source_target_pairs={{0,1},{1,0},{2,3},{3,2},{4,5},{5,4},{6,7},{7,6},{8,9},{9,8},{10,11... | collective-permute-start | bytes 786440 | tf_op jit(solution)/shard_map/ppermute | solution.py:171
  16.0 19.9 %collective-permute-start.2 = (f32[512,128]{1,0:T(8,128)S(1)}, f32[512,128]{1,0:T(8,128)S(1)}, u32[]{:S(2)}, u32[]{:S(2)}) collective-permute-start(f32[512,128]{1,0:T(8,128)S(1)} %collective-permute-done.1.refs_3_.refs_5_), channel_id=1, source_target_pairs={{0,1},{1,0},{2,3},{3,2},{4,5},{5,4},{6,7},{7,6},{8,9},{9,8},{10,11... | collective-permute-start | bytes 786440 | tf_op jit(solution)/shard_map/ppermute | solution.py:174
  17.2 9.7 %collective-permute-start.5 = (f32[256,128]{1,0:T(8,128)S(1)}, f32[256,128]{1,0:T(8,128)S(1)}, u32[]{:S(2)}, u32[]{:S(2)}) collective-permute-start(f32[256,128]{1,0:T(8,128)S(1)} %bitcast.22), channel_id=1, source_target_pairs={{0,4},{4,8},{8,12},{12,16},{16,20},{20,24},{24,28},{28,32},{32,36}... | collective-permute-start | bytes 393224 | tf_op jit(solution)/shard_map/ppermute | solution.py:172
  23.5 12.3 %collective-permute-start.6 = (f32[256,128]{1,0:T(8,128)S(1)}, f32[256,128]{1,0:T(8,128)S(1)}, u32[]{:S(2)}, u32[]{:S(2)}) collective-permute-start(f32[256,128]{1,0:T(8,128)S(1)} %bitcast.21), channel_id=1, source_target_pairs={{4,0},{8,4},{12,8},{16,12},{20,16},{24,20},{28,24},{32,28},{36,32}... | collective-permute-start | bytes 393224 | tf_op jit(solution)/shard_map/ppermute | solution.py:173
  39.7 5.7 %collective-permute-start.7 = (f32[216,128]{1,0:T(8,128)S(1)}, f32[216,128]{1,0:T(8,128)S(1)}, u32[]{:S(2)}, u32[]{:S(2)}) collective-permute-start(f32[216,128]{1,0:T(8,128)S(1)} %get-tuple-element.10), channel_id=1, source_target_pairs={{0,4},{4,0},{8,12},{12,8},{16,20},{20,16},{24,28},{28,24},{32,36},... | collective-permute-start | bytes 331784 | tf_op jit(solution)/shard_map/ppermute | solution.py:147
  39.8 8.0 %collective-permute-start.9 = (f32[216,128]{1,0:T(8,128)S(1)}, f32[216,128]{1,0:T(8,128)S(1)}, u32[]{:S(2)}, u32[]{:S(2)}) collective-permute-start(f32[216,128]{1,0:T(8,128)S(1)} %get-tuple-element.11), channel_id=1, source_target_pairs={{0,12},{4,8},{8,4},{12,0},{16,28},{20,24},{24,20},{28,16},{32,44},... | collective-permute-start | bytes 331784 | tf_op jit(solution)/shard_map/ppermute | solution.py:147
  39.9 7.9 %collective-permute-start.8 = (f32[216,128]{1,0:T(8,128)S(1)}, f32[216,128]{1,0:T(8,128)S(1)}, u32[]{:S(2)}, u32[]{:S(2)}) collective-permute-start(f32[216,128]{1,0:T(8,128)S(1)} %get-tuple-element.12), channel_id=1, source_target_pairs={{0,8},{4,12},{8,0},{12,4},{16,24},{20,28},{24,16},{28,20},{32,40},... | collective-permute-start | bytes 331784 | tf_op jit(solution)/shard_map/ppermute | solution.py:147
  43.9 17.2 %copy-start.1 = (f32[3,3,3,32,128]{4,3,2,1,0:T(8,128)S(1)}, f32[3,3,3,32,128]{4,3,2,1,0:T(8,128)}, u32[]{:S(2)}) copy-start(f32[3,3,3,32,128]{4,3,2,1,0:T(8,128)} %param.5) | copy-start | bytes 1327108
  47.8 8.1 %collective-permute-start.12 = (f32[216,128]{1,0:T(8,128)S(1)}, f32[216,128]{1,0:T(8,128)S(1)}, u32[]{:S(2)}, u32[]{:S(2)}) collective-permute-start(f32[216,128]{1,0:T(8,128)S(1)} %add_add_fusion.2), channel_id=1, source_target_pairs={{0,192},{4,196},{8,200},{12,204},{16,208},{20,212},{24,216},{28,22... | collective-permute-start | bytes 331784 | tf_op jit(solution)/shard_map/ppermute | solution.py:151
  47.9 8.0 %collective-permute-start.11 = (f32[216,128]{1,0:T(8,128)S(1)}, f32[216,128]{1,0:T(8,128)S(1)}, u32[]{:S(2)}, u32[]{:S(2)}) collective-permute-start(f32[216,128]{1,0:T(8,128)S(1)} %add_add_fusion.2), channel_id=1, source_target_pairs={{0,128},{4,132},{8,136},{12,140},{16,144},{20,148},{24,152},{28,15... | collective-permute-start | bytes 331784 | tf_op jit(solution)/shard_map/ppermute | solution.py:151
  51.5 5.1 %collective-permute-start.10 = (f32[216,128]{1,0:T(8,128)S(1)}, f32[216,128]{1,0:T(8,128)S(1)}, u32[]{:S(2)}, u32[]{:S(2)}) collective-permute-start(f32[216,128]{1,0:T(8,128)S(1)} %add_add_fusion.2), channel_id=1, source_target_pairs={{0,64},{4,68},{8,72},{12,76},{16,80},{20,84},{24,88},{28,92},{32,9... | collective-permute-start | bytes 331784 | tf_op jit(solution)/shard_map/ppermute | solution.py:151
  56.6 12.4 %collective-permute-start.15 = (f32[216,128]{1,0:T(8,128)S(1)}, f32[216,128]{1,0:T(8,128)S(1)}, u32[]{:S(2)}, u32[]{:S(2)}) collective-permute-start(f32[216,128]{1,0:T(8,128)S(1)} %add_add_fusion.1), channel_id=1, source_target_pairs={{0,48},{4,52},{8,56},{12,60},{16,32},{20,36},{24,40},{28,44},{32,1... | collective-permute-start | bytes 331784 | tf_op jit(solution)/shard_map/ppermute | solution.py:151
  56.7 12.3 %collective-permute-start.14 = (f32[216,128]{1,0:T(8,128)S(1)}, f32[216,128]{1,0:T(8,128)S(1)}, u32[]{:S(2)}, u32[]{:S(2)}) collective-permute-start(f32[216,128]{1,0:T(8,128)S(1)} %add_add_fusion.1), channel_id=1, source_target_pairs={{0,32},{4,36},{8,40},{12,44},{16,48},{20,52},{24,56},{28,60},{32,0... | collective-permute-start | bytes 331784 | tf_op jit(solution)/shard_map/ppermute | solution.py:151
  56.8 12.2 %collective-permute-start.13 = (f32[216,128]{1,0:T(8,128)S(1)}, f32[216,128]{1,0:T(8,128)S(1)}, u32[]{:S(2)}, u32[]{:S(2)}) collective-permute-start(f32[216,128]{1,0:T(8,128)S(1)} %add_add_fusion.1), channel_id=1, source_target_pairs={{0,16},{4,20},{8,24},{12,28},{16,0},{20,4},{24,8},{28,12},{32,48},... | collective-permute-start | bytes 331784 | tf_op jit(solution)/shard_map/ppermute | solution.py:151
  63.1 7.5 %collective-permute-start.3 = (f32[256,128]{1,0:T(8,128)S(1)}, f32[256,128]{1,0:T(8,128)S(1)}, u32[]{:S(2)}, u32[]{:S(2)}) collective-permute-start(f32[256,128]{1,0:T(8,128)S(1)} %get-tuple-element.6), channel_id=1, source_target_pairs={{0,4},{4,8},{8,12},{12,16},{16,20},{20,24},{24,28},{28,32},{32,36}... | collective-permute-start | bytes 393224 | tf_op jit(solution)/shard_map/ppermute | solution.py:211
  66.8 11.7 %collective-permute-start.4 = (f32[256,128]{1,0:T(8,128)S(1)}, f32[256,128]{1,0:T(8,128)S(1)}, u32[]{:S(2)}, u32[]{:S(2)}) collective-permute-start(f32[256,128]{1,0:T(8,128)S(1)} %get-tuple-element.7), channel_id=1, source_target_pairs={{4,0},{8,4},{12,8},{16,12},{20,16},{24,20},{28,24},{32,28},{36,32}... | collective-permute-start | bytes 393224 | tf_op jit(solution)/shard_map/ppermute | solution.py:212
  69.1 10.4 %collective-permute-start.16 = (f32[216,128]{1,0:T(8,128)S(1)}, f32[216,128]{1,0:T(8,128)S(1)}, u32[]{:S(2)}, u32[]{:S(2)}) collective-permute-start(f32[216,128]{1,0:T(8,128)S(1)} %get-tuple-element.9), channel_id=1, source_target_pairs={{0,4},{4,0},{8,12},{12,8},{16,20},{20,16},{24,28},{28,24},{32,36},... | collective-permute-start | bytes 331784 | tf_op jit(solution)/shard_map/ppermute | solution.py:152
  79.5 6.4 %collective-permute-start.17 = (f32[216,128]{1,0:T(8,128)S(1)}, f32[216,128]{1,0:T(8,128)S(1)}, u32[]{:S(2)}, u32[]{:S(2)}) collective-permute-start(f32[216,128]{1,0:T(8,128)S(1)} %get-tuple-element.9), channel_id=1, source_target_pairs={{0,8},{4,12},{8,0},{12,4},{16,24},{20,28},{24,16},{28,20},{32,40},... | collective-permute-start | bytes 331784 | tf_op jit(solution)/shard_map/ppermute | solution.py:152
  79.5 7.1 %collective-permute-start.18 = (f32[216,128]{1,0:T(8,128)S(1)}, f32[216,128]{1,0:T(8,128)S(1)}, u32[]{:S(2)}, u32[]{:S(2)}) collective-permute-start(f32[216,128]{1,0:T(8,128)S(1)} %get-tuple-element.9), channel_id=1, source_target_pairs={{0,12},{4,8},{8,4},{12,0},{16,28},{20,24},{24,20},{28,16},{32,44},... | collective-permute-start | bytes 331784 | tf_op jit(solution)/shard_map/ppermute | solution.py:152
  86.7 0.8 copy-start.3

commit v2 on v1

--- a/solution.py
+++ b/solution.py
@@ -35,19 +35,20 @@
             grads[pl.ds(filters + start, count), r * 128 : (r + 1) * 128] = low
 
 
-def weight_kernel(scale, planes, x, above, below, g0, g1, g2, g3, out, cells, grads):
+def weight_kernel(scale, planes, x, near, far, g0, g1, g2, g3, out, cells, grads):
     chan = lax.axis_index("chan")
     load_grads((g0, g1, g2, g3), grads, chan)
     count = x.shape[0] // (2 * planes)
     filters = grads.shape[0] // 2
     cells[:, : 4 * 128] = jnp.zeros((cells.shape[0], 4 * 128), BF)
     cells[:, (planes + 1) * 512 :] = jnp.zeros((cells.shape[0], 512), BF)
+    odd = lax.axis_index("space") % 2 == 1
     for d in range(planes):
         for r in range(4):
-            if r == 0:
-                value = above[pl.ds(d, count, stride=planes), :]
-            elif r == 3:
-                value = below[pl.ds(d, count, stride=planes), :]
+            if r in (0, 3):
+                inner = near[pl.ds(d, count, stride=planes), :]
+                outer = far[pl.ds(d, count, stride=planes), :]
+                value = jnp.where(odd, inner, outer) if r == 0 else jnp.where(odd, outer, inner)
             else:
                 value = x[pl.ds(2 * d + r - 1, count, stride=2 * planes), :]
             at = ((d + 1) * 4 + r) * 128
@@ -120,40 +121,41 @@
 AXES = 4
 
 
-def place(deltas):
-    pairs = []
-    for i in range(AXES**3):
-        x, z, y = i // (AXES * AXES), (i // AXES) % AXES, i % AXES
-        pairs.append((i, ((x ^ deltas[0]) * AXES + (z ^ deltas[1])) * AXES + (y ^ deltas[2])))
-    return pairs
-
-
-def toward(axis, step):
-    deltas = [0, 0, 0]
-    deltas[axis] = step
-    return place(deltas)
-
-
-def sum_over_space(value):
-    me = lax.axis_index("space")
-    last = me % AXES
-    length = value.shape[0] // AXES
-
-    def piece(index):
-        return lax.dynamic_slice_in_dim(value, index * length, length, 0)
-
-    total = piece(last)
-    for k in (1, 2, 3):
-        total = total + lax.ppermute(piece(last ^ k), "space", toward(2, k))
-    for axis in (0, 1):
-        held = total
-        for k in (1, 2, 3):
-            total = total + lax.ppermute(held, "space", toward(axis, k))
-    parts = [total] + [lax.ppermute(total, "space", toward(2, k)) for k in (1, 2, 3)]
-    result = jnp.zeros(value.shape, value.dtype)
-    for k in range(4):
-        result = lax.dynamic_update_slice_in_dim(result, parts[k], (last ^ k) * length, 0)
-    return result
+def groups_over_xy():
+    return [
+        [(x * AXES + z) * AXES + y for x in range(AXES) for y in range(AXES)] for z in range(AXES)
+    ]
+
+
+def z_pairs(step):
+    return [(i, i ^ (step * AXES)) for i in range(AXES**3)]
+
+
+def scattered(value):
+    return lax.all_to_all(value, "space", 0, 0, axis_index_groups=groups_over_xy()).sum(axis=0)
+
+
+def summed_over_z(value):
+    total = value
+    for step in (1, 2, 3):
+        total = total + lax.ppermute(value, "space", z_pairs(step))
+    return total
+
+
+def gathered(value):
+    pieces = jnp.broadcast_to(value[None], (AXES * AXES,) + value.shape)
+    return lax.all_to_all(pieces, "space", 0, 0, axis_index_groups=groups_over_xy())
+
+
+def swap_halo(first, last):
+    count = lax.axis_size("space")
+    odd = lax.axis_index("space") % 2 == 1
+    inner = [(i, i ^ 1) for i in range(count)]
+    outer = [(i, i + 1) for i in range(1, count - 1, 2)]
+    outer = outer + [(j, i) for i, j in outer]
+    a = lax.ppermute(jnp.where(odd, first, last), "space", inner)
+    b = lax.ppermute(jnp.where(odd, last, first), "space", outer)
+    return a, b, odd
 
 
 def per_device(inputs, out_grad, weights):
@@ -164,14 +166,15 @@
     x = inputs.reshape(-1, cols)
     g0 = out_grad.reshape(-1, cols)
     w = weights.reshape(-1, filters)
-    peers = lax.axis_size("space")
-    up = [(i, i + 1) for i in range(peers - 1)]
-    down = [(j, i) for i, j in up]
-    g2 = lax.ppermute(g0, "chan", [(i, i ^ 2) for i in range(4)])
-    g1 = lax.ppermute(g0, "chan", [(i, i ^ 1) for i in range(4)])
-    above = lax.ppermute(inputs[:, :, 1, :].reshape(-1, cols), "space", up)
-    below = lax.ppermute(inputs[:, :, 0, :].reshape(-1, cols), "space", down)
-    g3 = lax.ppermute(g2, "chan", [(i, i ^ 1) for i in range(4)])
+    across = [(i, i ^ 2) for i in range(4)]
+    beside = [(i, i ^ 1) for i in range(4)]
+    g2 = lax.ppermute(g0, "chan", across)
+    g1 = lax.ppermute(g0, "chan", beside)
+    near, far, odd = swap_halo(
+        inputs[:, :, 0, :].reshape(-1, cols), inputs[:, :, 1, :].reshape(-1, cols)
+    )
+    g1, g2, near, far = lax.optimization_barrier((g1, g2, near, far))
+    g3 = lax.ppermute(g2, "chan", beside)
     cells = planes * rows * cols
 
     def vmem(n):
@@ -191,7 +194,9 @@
             flops=6 * 27 * channels * filters * cells, bytes_accessed=2**21, transcendentals=0
         ),
         name="weight_kernel",
-    )(x, above, below, g0, g1, g2, g3)
+    )(x, near, far, g0, g1, g2, g3)
+    partial, w, g0, g1, g2, g3 = lax.optimization_barrier((partial, w, g0, g1, g2, g3))
+    piece = scattered(partial.reshape(AXES * AXES, -1, 2, filters))
     halo = jax.ShapeDtypeStruct((channels * planes, cols), F32)
     core, to_above, to_below = pl.pallas_call(
         lambda *refs: input_kernel(planes, *refs),
@@ -208,10 +213,13 @@
         ),
         name="input_kernel",
     )(w, g0, g1, g2, g3)
-    from_above = lax.ppermute(to_below, "space", up).reshape(channels, planes, cols)
-    from_below = lax.ppermute(to_above, "space", down).reshape(channels, planes, cols)
-    input_grad = core.reshape(inputs.shape) + jnp.stack([from_above, from_below], axis=2)
-    weight_grad = sum_over_space(partial).reshape(3, 3, 3, channels, filters)
+    near, far, odd = swap_halo(to_above, to_below)
+    weight_grad = gathered(summed_over_z(piece))
+    near = near.reshape(channels, planes, cols)
+    far = far.reshape(channels, planes, cols)
+    rims = jnp.stack([jnp.where(odd, near, far), jnp.where(odd, far, near)], axis=2)
+    input_grad = core.reshape(inputs.shape) + rims
+    weight_grad = weight_grad.reshape(3, 3, 3, channels, filters)
     return (input_grad, weight_grad)
 
 

time: 87.6 us -> 71.1 us (0.81)
  the two profiles are of different devices: /device:TPU:248 before, /device:TPU:32 now
where the time goes in v2:
time: 71.1 us; the launch traced here: 70.1 us
  starting transfers between devices  30.3 us (43%)
  waiting for transfers between devices  28.2 us (40%)
  Pallas kernels  6.57 us (9%)
  other arithmetic  2.53 us (4%)
  local copies, waits for them, and re-layouts  1.65 us (2%)
  between operations  0.76 us (1%)
    ppermute x2, waiting for transfers between devices, swap_halo(): b = lax.ppermute(jnp.where(odd, last, first), 'space', outer)  9.85 us
    ppermute x2, starting transfers between devices, swap_halo(): b = lax.ppermute(jnp.where(odd, last, first), 'space', outer)  9.36 us
    all_to_all x1, waiting for transfers between devices, scattered(): lax.all_to_all(value, 'space', 0, 0, axis_index_groups=groups_over_xy())  8.54 us
    all_to_all x1, waiting for transfers between devices, gathered(): lax.all_to_all(pieces, 'space', 0, 0, axis_index_groups=groups_over_xy())  8.31 us
    ppermute x1, starting transfers between devices, per_device(): g2 = lax.ppermute(g0, 'chan', across)  6.38 us
    all_to_all x1, starting transfers between devices, scattered(): lax.all_to_all(value, 'space', 0, 0, axis_index_groups=groups_over_xy())  4.54 us
    pallas_call x1, Pallas kernels, per_device(): pl.pallas_call(lambda *refs: weight_kernel(scale, planes, *refs), out_sha...  4.52 us
    ppermute x3, starting transfers between devices, summed_over_z(): total = total + lax.ppermute(value, 'space', z_pairs(step))  4.29 us
  transfers between devices with their start and end apart: 12, of which 4 were waited for; matrix products, arithmetic and copies ran while one was open for 5% of the time, Pallas kernels for 3%

profile of v2, /device:TPU:32, one launch (start us, length us, event | category | flops | bytes accessed | tf_op | source)
XLA Modules:
  0.0 70.1 jit_solution(14031786464200446808)
XLA Ops:
  0.6 6.4 %collective-permute-start.1 = (f32[512,128]{1,0:T(8,128)}, f32[512,128]{1,0:T(8,128)S(1)}, u32[]{:S(2)}, u32[]{:S(2)}) collective-permute-start(f32[512,128]{1,0:T(8,128)} %bitcast.17), channel_id=1, source_target_pairs={{0,2},{1,3},{2,0},{3,1},{4,6},{5,7},{6,4},{7,5},{8,10},{9,11},{10,... | collective-permute-start | bytes 786440 | tf_op jit(solution)/shard_map/ppermute | solution.py:171
  7.0 0.0 collective-permute-start
  7.0 0.0 copy-start
  7.0 0.0 copy-start.2
  7.0 1.3 %broadcast_select_fusion = (f32[32,8,1,128]{3,2,1,0:T(1,128)S(1)}, f32[32,8,1,128]{3,2,1,0:T(1,128)S(1)}) fusion(pred[]{:T(512)S(6)} %eq.7, f32[32,8,2,128]{3,2,1,0:T(2,128)} %param.3), kind=kLoop, calls=%fused_computation.1 | loop fusion | flops 65536 | bytes 524289 | tf_op jit(solution)/shard_map/jit(_where)/select_n | solution.py:157
  8.3 1.7 %collective-permute-start.2 = (f32[256,128]{1,0:T(8,128)S(1)}, f32[256,128]{1,0:T(8,128)S(1)}, u32[]{:S(2)}, u32[]{:S(2)}) collective-permute-start(f32[256,128]{1,0:T(8,128)S(1)} %bitcast.25), channel_id=1, source_target_pairs={{0,4},{4,0},{8,12},{12,8},{16,20},{20,16},{24,28},{28,24},{32,36},... | collective-permute-start | bytes 393224 | tf_op jit(solution)/shard_map/ppermute | solution.py:156
  10.0 4.5 %collective-permute-start.3 = (f32[256,128]{1,0:T(8,128)S(1)}, f32[256,128]{1,0:T(8,128)S(1)}, u32[]{:S(2)}, u32[]{:S(2)}) collective-permute-start(f32[256,128]{1,0:T(8,128)S(1)} %bitcast.24), channel_id=1, source_target_pairs={{4,8},{12,16},{20,24},{28,32},{36,40},{44,48},{52,56},{60,64},{68,... | collective-permute-start | bytes 393224 | tf_op jit(solution)/shard_map/ppermute | solution.py:157
  14.5 0.0 collective-permute-done.2.refs_1_
  14.5 9.8 %collective-permute-done.3.refs_2_ = f32[256,128]{1,0:T(8,128)S(1)} collective-permute-done((f32[256,128]{1,0:T(8,128)S(1)}, f32[256,128]{1,0:T(8,128)S(1)}, u32[]{:S(2)}, u32[]{:S(2)}) %collective-permute-start.3) | collective-permute-done | bytes 131104 | tf_op jit(solution)/shard_map/ppermute | solution.py:157
  24.4 0.0 collective-permute-done.1.refs_5_.refs_3_
  24.4 0.0 collective-permute-done.refs_4_.refs_2_
  24.4 0.0 collective-permute-start.4
  24.4 1.5 %collective-permute-done.4.refs_6_.refs_4_ = f32[512,128]{1,0:T(8,128)S(1)} collective-permute-done((f32[512,128]{1,0:T(8,128)S(1)}, f32[512,128]{1,0:T(8,128)S(1)}, u32[]{:S(2)}, u32[]{:S(2)}) %collective-permute-start.4) | collective-permute-done | bytes 262176 | tf_op jit(solution)/shard_map/ppermute | solution.py:177
  25.9 0.0 copy-done
  25.9 0.0 copy-done.2
  25.9 4.5 %weight_kernel.1 = f32[864,128]{1,0:T(8,128)} custom-call(f32[512,128]{1,0:T(8,128)S(1)} %bitcast.15, f32[256,128]{1,0:T(8,128)S(1)} %collective-permute-done.2.refs_1_, f32[256,128]{1,0:T(8,128)S(1)} %collective-permute-done.3.refs_2_, f32[512,128]{1,0:T(8,128)S(1)} %bitcast.19, f32[512,128]{1,0:T(8,128)S(1)} %collective-permute-done.refs_4_.refs_2_, ...), custom_call_target="tpu_custom_call" | custom-call | flops 1358954496 | bytes 2097152 | tf_op jit(solution)/shard_map/weight_kernel/pallas_call | solution.py:183
  30.5 0.0 copy-start.1
  30.5 4.5 %all-to-all-start = ((f32[16,27,2,128]{3,2,1,0:T(2,128)}), f32[16,27,2,128]{3,2,1,0:T(2,128)S(1)}, u32[]{:S(2)}, u32[]{:S(2)}) async-start(f32[16,27,2,128]{3,2,1,0:T(2,128)} %bitcast.10), calls=%async_computation | async-start | bytes 884736 | tf_op jit(solution)/shard_map/all_to_all | solution.py:135
  35.0 0.0 copy-done.1
  35.0 2.1 %input_kernel.1 = (f32[512,128]{1,0:T(8,128)S(1)}, f32[256,128]{1,0:T(8,128)S(1)}, f32[256,128]{1,0:T(8,128)S(1)}) custom-call(f32[864,128]{1,0:T(8,128)S(1)} %bitcast.16, f32[512,128]{1,0:T(8,128)S(1)} %bitcast.20, f32[512,128]{1,0:T(8,128)S(1)} %collective-permute-done.refs_4_.refs_2_, f32[512,128]{1,0:T(8,128)S(1)} %collective-permute-done.1.refs_5_.refs_3_, ...), custom_call_target="tpu_custom_call" | custom-call | flops 1358954496 | bytes 2097152 | tf_op jit(solution)/shard_map/input_kernel/pallas_call | solution.py:201
  37.1 8.5 %all-to-all-done = f32[16,27,2,128]{3,2,1,0:T(2,128)S(1)} async-done(((f32[16,27,2,128]{3,2,1,0:T(2,128)}), f32[16,27,2,128]{3,2,1,0:T(2,128)S(1)}, u32[]{:S(2)}, u32[]{:S(2)}) %all-to-all-start) | async-done | bytes 442400 | tf_op jit(solution)/shard_map/all_to_all | solution.py:135
  45.6 0.1 reduce_sum.9
  45.8 1.6 %collective-permute-start.9 = (f32[27,2,128]{2,1,0:T(2,128)S(1)}, f32[27,2,128]{2,1,0:T(2,128)S(1)}, u32[]{:S(2)}, u32[]{:S(2)}) collective-permute-start(f32[27,2,128]{2,1,0:T(2,128)S(1)} %reduce_sum.9), channel_id=1, source_target_pairs={{0,48},{4,52},{8,56},{12,60},{16,32},{20,36},{24,40},{28,44},{32,1... | collective-permute-start | bytes 82952 | tf_op jit(solution)/shard_map/ppermute | solution.py:141
  47.4 2.5 %collective-permute-start.8 = (f32[27,2,128]{2,1,0:T(2,128)S(1)}, f32[27,2,128]{2,1,0:T(2,128)S(1)}, u32[]{:S(2)}, u32[]{:S(2)}) collective-permute-start(f32[27,2,128]{2,1,0:T(2,128)S(1)} %reduce_sum.9), channel_id=1, source_target_pairs={{0,32},{4,36},{8,40},{12,44},{16,48},{20,52},{24,56},{28,60},{32,0... | collective-permute-start | bytes 82952 | tf_op jit(solution)/shard_map/ppermute | solution.py:141
  49.9 0.2 collective-permute-start.7
  50.1 0.5 collective-permute-start.5
  50.5 4.8 %collective-permute-start.6 = (f32[256,128]{1,0:T(8,128)S(1)}, f32[256,128]{1,0:T(8,128)S(1)}, u32[]{:S(2)}, u32[]{:S(2)}) collective-permute-start(f32[256,128]{1,0:T(8,128)S(1)} %get-tuple-element.31), channel_id=1, source_target_pairs={{4,8},{12,16},{20,24},{28,32},{36,40},{44,48},{52,56},{60,64},{68,... | collective-permute-start | bytes 393224 | tf_op jit(solution)/shard_map/ppermute | solution.py:157
  55.4 0.0 collective-permute-done.9
  55.4 0.0 collective-permute-done.8
  55.4 0.0 collective-permute-done.7
  55.4 0.9 %broadcast_in_dim.2 = f32[16,27,2,128]{3,2,1,0:T(2,128)} broadcast(f32[27,2,128]{2,1,0:T(2,128)S(1)} %add_add_fusion), dimensions={1,2,3} | broadcast | bytes 470016 | tf_op jit(solution)/shard_map/broadcast_in_dim | solution.py:146
  56.3 3.6 %all-to-all-start.1 = ((f32[16,27,2,128]{3,2,1,0:T(2,128)}), f32[16,27,2,128]{3,2,1,0:T(2,128)S(1)}, u32[]{:S(2)}, u32[]{:S(2)}) async-start(f32[16,27,2,128]{3,2,1,0:T(2,128)} %broadcast_in_dim.2), calls=%async_computation.1 | async-start | bytes 884736 | tf_op jit(solution)/shard_map/all_to_all | solution.py:147
  60.0 0.0 collective-permute-done.5
  60.0 0.0 collective-permute-done.6
  60.0 1.0 %maximum_add_fusion = f32[32,8,2,128]{3,2,1,0:T(2,128)} fusion(f32[32,8,2,128]{3,2,1,0:T(2,128)S(1)} %bitcast.14, f32[32,8,1,128]{3,2,1,0:T(1,128)S(1)} %bitcast.23, f32[32,8,1,128]{3,2,1,0:T(1,128)S(1)} %bitcast.22), kind=kLoop, calls=%fused_computation | loop fusion | flops 131072 | bytes 786432 | tf_op jit(solution)/shard_map/add | solution.py:221
  61.0 8.3 %all-to-all-done.1 = f32[16,27,2,128]{3,2,1,0:T(2,128)S(1)} async-done(((f32[16,27,2,128]{3,2,1,0:T(2,128)}), f32[16,27,2,128]{3,2,1,0:T(2,128)S(1)}, u32[]{:S(2)}, u32[]{:S(2)}) %all-to-all-start.1) | async-done | bytes 442400 | tf_op jit(solution)/shard_map/all_to_all | solution.py:147
  69.3 0.8 %copy.8 = f32[3,3,3,32,128]{4,3,2,1,0:T(8,128)} copy(f32[3,3,3,32,128]{4,3,2,1,0:T(8,128)S(1)} %bitcast.21) | data formatting | bytes 884736
  (3 shorter events, 0.1 us)
Async XLA Ops:
  0.6 23.8 %collective-permute-start.1 = (f32[512,128]{1,0:T(8,128)}, f32[512,128]{1,0:T(8,128)S(1)}, u32[]{:S(2)}, u32[]{:S(2)}) collective-permute-start(f32[512,128]{1,0:T(8,128)} %bitcast.17), channel_id=1, source_target_pairs={{0,2},{1,3},{2,0},{3,1},{4,6},{5,7},{6,4},{7,5},{8,10},{9,11},{10,... | collective-permute-start | bytes 786440 | tf_op jit(solution)/shard_map/ppermute | solution.py:171
  7.0 17.4 %collective-permute-start = (f32[512,128]{1,0:T(8,128)}, f32[512,128]{1,0:T(8,128)S(1)}, u32[]{:S(2)}, u32[]{:S(2)}) collective-permute-start(f32[512,128]{1,0:T(8,128)} %bitcast.18), channel_id=1, source_target_pairs={{0,1},{1,0},{2,3},{3,2},{4,5},{5,4},{6,7},{7,6},{8,9},{9,8},{10,11... | collective-permute-start | bytes 786440 | tf_op jit(solution)/shard_map/ppermute | solution.py:172
  7.0 18.9 %copy-start = (f32[32,8,2,128]{3,2,1,0:T(2,128)S(1)}, f32[32,8,2,128]{3,2,1,0:T(2,128)}, u32[]{:S(2)}) copy-start(f32[32,8,2,128]{3,2,1,0:T(2,128)} %param.3) | copy-start | bytes 786436
  7.0 18.9 %copy-start.2 = (f32[32,8,2,128]{3,2,1,0:T(2,128)S(1)}, f32[32,8,2,128]{3,2,1,0:T(2,128)}, u32[]{:S(2)}) copy-start(f32[32,8,2,128]{3,2,1,0:T(2,128)} %param.4) | copy-start | bytes 786436
  8.3 6.2 %collective-permute-start.2 = (f32[256,128]{1,0:T(8,128)S(1)}, f32[256,128]{1,0:T(8,128)S(1)}, u32[]{:S(2)}, u32[]{:S(2)}) collective-permute-start(f32[256,128]{1,0:T(8,128)S(1)} %bitcast.25), channel_id=1, source_target_pairs={{0,4},{4,0},{8,12},{12,8},{16,20},{20,16},{24,28},{28,24},{32,36},... | collective-permute-start | bytes 393224 | tf_op jit(solution)/shard_map/ppermute | solution.py:156
  10.0 14.4 %collective-permute-start.3 = (f32[256,128]{1,0:T(8,128)S(1)}, f32[256,128]{1,0:T(8,128)S(1)}, u32[]{:S(2)}, u32[]{:S(2)}) collective-permute-start(f32[256,128]{1,0:T(8,128)S(1)} %bitcast.24), channel_id=1, source_target_pairs={{4,8},{12,16},{20,24},{28,32},{36,40},{44,48},{52,56},{60,64},{68,... | collective-permute-start | bytes 393224 | tf_op jit(solution)/shard_map/ppermute | solution.py:157
  24.4 1.5 %collective-permute-start.4 = (f32[512,128]{1,0:T(8,128)S(1)}, f32[512,128]{1,0:T(8,128)S(1)}, u32[]{:S(2)}, u32[]{:S(2)}) collective-permute-start(f32[512,128]{1,0:T(8,128)S(1)} %collective-permute-done.1.refs_5_.refs_3_), channel_id=1, source_target_pairs={{0,1},{1,0},{2,3},{3,2},{4,5},{5,4},{6,7},{7,6},{8,9},{9,8},{10,11... | collective-permute-start | bytes 786440 | tf_op jit(solution)/shard_map/ppermute | solution.py:177
  30.5 4.6 %copy-start.1 = (f32[3,3,3,32,128]{4,3,2,1,0:T(8,128)S(1)}, f32[3,3,3,32,128]{4,3,2,1,0:T(8,128)}, u32[]{:S(2)}) copy-start(f32[3,3,3,32,128]{4,3,2,1,0:T(8,128)} %param.5) | copy-start | bytes 1327108
  30.5 15.2 %all-to-all-start = ((f32[16,27,2,128]{3,2,1,0:T(2,128)}), f32[16,27,2,128]{3,2,1,0:T(2,128)S(1)}, u32[]{:S(2)}, u32[]{:S(2)}) async-start(f32[16,27,2,128]{3,2,1,0:T(2,128)} %bitcast.10), calls=%async_computation | async-start | bytes 884736 | tf_op jit(solution)/shard_map/all_to_all | solution.py:135
  45.8 9.6 %collective-permute-start.9 = (f32[27,2,128]{2,1,0:T(2,128)S(1)}, f32[27,2,128]{2,1,0:T(2,128)S(1)}, u32[]{:S(2)}, u32[]{:S(2)}) collective-permute-start(f32[27,2,128]{2,1,0:T(2,128)S(1)} %reduce_sum.9), channel_id=1, source_target_pairs={{0,48},{4,52},{8,56},{12,60},{16,32},{20,36},{24,40},{28,44},{32,1... | collective-permute-start | bytes 82952 | tf_op jit(solution)/shard_map/ppermute | solution.py:141
  47.4 8.0 %collective-permute-start.8 = (f32[27,2,128]{2,1,0:T(2,128)S(1)}, f32[27,2,128]{2,1,0:T(2,128)S(1)}, u32[]{:S(2)}, u32[]{:S(2)}) collective-permute-start(f32[27,2,128]{2,1,0:T(2,128)S(1)} %reduce_sum.9), channel_id=1, source_target_pairs={{0,32},{4,36},{8,40},{12,44},{16,48},{20,52},{24,56},{28,60},{32,0... | collective-permute-start | bytes 82952 | tf_op jit(solution)/shard_map/ppermute | solution.py:141
  49.9 5.5 %collective-permute-start.7 = (f32[27,2,128]{2,1,0:T(2,128)S(1)}, f32[27,2,128]{2,1,0:T(2,128)S(1)}, u32[]{:S(2)}, u32[]{:S(2)}) collective-permute-start(f32[27,2,128]{2,1,0:T(2,128)S(1)} %reduce_sum.9), channel_id=1, source_target_pairs={{0,16},{4,20},{8,24},{12,28},{16,0},{20,4},{24,8},{28,12},{32,48},... | collective-permute-start | bytes 82952 | tf_op jit(solution)/shard_map/ppermute | solution.py:141
  50.1 9.9 %collective-permute-start.5 = (f32[256,128]{1,0:T(8,128)S(1)}, f32[256,128]{1,0:T(8,128)S(1)}, u32[]{:S(2)}, u32[]{:S(2)}) collective-permute-start(f32[256,128]{1,0:T(8,128)S(1)} %get-tuple-element.30), channel_id=1, source_target_pairs={{0,4},{4,0},{8,12},{12,8},{16,20},{20,16},{24,28},{28,24},{32,36},... | collective-permute-start | bytes 393224 | tf_op jit(solution)/shard_map/ppermute | solution.py:156
  50.5 9.4 %collective-permute-start.6 = (f32[256,128]{1,0:T(8,128)S(1)}, f32[256,128]{1,0:T(8,128)S(1)}, u32[]{:S(2)}, u32[]{:S(2)}) collective-permute-start(f32[256,128]{1,0:T(8,128)S(1)} %get-tuple-element.31), channel_id=1, source_target_pairs={{4,8},{12,16},{20,24},{28,32},{36,40},{44,48},{52,56},{60,64},{68,... | collective-permute-start | bytes 393224 | tf_op jit(solution)/shard_map/ppermute | solution.py:157
  56.3 13.0 %all-to-all-start.1 = ((f32[16,27,2,128]{3,2,1,0:T(2,128)}), f32[16,27,2,128]{3,2,1,0:T(2,128)S(1)}, u32[]{:S(2)}, u32[]{:S(2)}) async-start(f32[16,27,2,128]{3,2,1,0:T(2,128)} %broadcast_in_dim.2), calls=%async_computation.1 | async-start | bytes 884736 | tf_op jit(solution)/shard_map/all_to_all | solution.py:147

commit v3 on v2

--- a/solution.py
+++ b/solution.py
@@ -57,21 +57,22 @@
                 high, low = split(moved)
                 cells[kw * 2 * count : (kw * 2 + 1) * count, at : at + 128] = high
                 cells[(kw * 2 + 1) * count : (kw * 2 + 2) * count, at : at + 128] = low
-    for kd in range(3):
-        for kh in range(3):
-            left = jnp.concatenate(
-                [
-                    cells[:, ((d + kd) * 4 + kh) * 128 : ((d + kd) * 4 + kh) * 128 + 256]
-                    for d in range(planes)
-                ],
-                axis=1,
-            )
-            full = lax.dot_general(
-                left, grads[...], (((1,), (1,)), ((), ())), preferred_element_type=F32
-            )
+    for kh in range(3):
+        stripes = []
+        for kd in range(3):
+            starts = [((d + kd) * 4 + kh) * 128 for d in range(planes)]
+            stripes.append(jnp.concatenate([cells[:, i : i + 256] for i in starts], axis=1))
+        full = lax.dot_general(
+            jnp.concatenate(stripes, axis=0),
+            grads[...],
+            (((1,), (1,)), ((), ())),
+            preferred_element_type=F32,
+        )
+        for kd in range(3):
             for kw in range(3):
-                high = full[kw * 2 * count : (kw * 2 + 1) * count]
-                low = full[(kw * 2 + 1) * count : (kw * 2 + 2) * count]
+                at = (kd * 3 + kw) * 2 * count
+                high = full[at : at + count]
+                low = full[at + count : at + 2 * count]
                 total = high[:, :filters] + (high[:, filters:] + low[:, :filters])
                 tap = (kd * 3 + kh) * 3 + kw
                 out[tap * count : (tap + 1) * count, :] = total * scale
@@ -135,15 +136,23 @@
     return lax.all_to_all(value, "space", 0, 0, axis_index_groups=groups_over_xy()).sum(axis=0)
 
 
-def summed_over_z(value):
-    total = value
-    for step in (1, 2, 3):
-        total = total + lax.ppermute(value, "space", z_pairs(step))
-    return total
+def spread_kernel(a, b, c, d, out):
+    total = (a[...] + b[...]) + (c[...] + d[...])
+    for i in range(out.shape[0]):
+        out[i] = total
 
 
 def gathered(value):
-    pieces = jnp.broadcast_to(value[None], (AXES * AXES,) + value.shape)
+    parts = [value] + [lax.ppermute(value, "space", z_pairs(step)) for step in (1, 2, 3)]
+    pieces = pl.pallas_call(
+        spread_kernel,
+        out_shape=jax.ShapeDtypeStruct((AXES * AXES,) + value.shape, F32),
+        in_specs=[pl.BlockSpec(memory_space=pltpu.VMEM)] * 4,
+        out_specs=pl.BlockSpec(memory_space=pltpu.VMEM),
+        compiler_params=pltpu.CompilerParams(vmem_limit_bytes=2 * 1024 * 1024),
+        cost_estimate=pl.CostEstimate(flops=2**16, bytes_accessed=2**19, transcendentals=0),
+        name="spread_kernel",
+    )(*parts)
     return lax.all_to_all(pieces, "space", 0, 0, axis_index_groups=groups_over_xy())
 
 
@@ -214,7 +223,7 @@
         name="input_kernel",
     )(w, g0, g1, g2, g3)
     near, far, odd = swap_halo(to_above, to_below)
-    weight_grad = gathered(summed_over_z(piece))
+    weight_grad = gathered(piece)
     near = near.reshape(channels, planes, cols)
     far = far.reshape(channels, planes, cols)
     rims = jnp.stack([jnp.where(odd, near, far), jnp.where(odd, far, near)], axis=2)

time: 71.1 us -> 67.8 us (0.954)
  waiting for transfers between devices: 28.2 us -> 24.8 us
  starting transfers between devices: 30.3 us -> 32.3 us
  local copies, waits for them, and re-layouts: 1.65 us -> 0.77 us
    all_to_all x1, waiting for transfers between devices: 8.54 us -> 1.78 us  [scattered(): lax.all_to_all(value, 'space', 0, 0, axis_index_groups=groups_over_xy())]
    ppermute x3, waiting for transfers between devices: 0.01 us -> 3.34 us  [gathered(): lax.ppermute(value, 'space', z_pairs(step))]
    ppermute x2, starting transfers between devices: 2.12 us -> 3.67 us  [swap_halo(): a = lax.ppermute(jnp.where(odd, first, last), 'space', inner)]
    pallas_call x1, Pallas kernels: 4.52 us -> 3.34 us  [per_device(): pl.pallas_call(lambda *refs: weight_kernel(scale, planes, *refs), out_sha...]
    pallas_call x0 -> x1, Pallas kernels: none -> 0.88 us  [gathered(): pl.pallas_call(spread_kernel, out_shape=jax.ShapeDtypeStruct((AXES * AXES...]
    broadcast_in_dim x1 -> x0, local copies, waits for them, and re-layouts: 0.88 us -> none  [gathered(): pieces = jnp.broadcast_to(value[None], (AXES * AXES,) + value.shape)]
  transfers between devices with their start and end apart: 12 -> 12, of which waited for: 4 -> 6; matrix products, arithmetic and copies ran while one was open for 5% -> 4% of each run, Pallas kernels for 3% -> 4%
where the time goes in v3:
time: 67.8 us; the launch traced here: 67.4 us
  starting transfers between devices  32.3 us (48%)
  waiting for transfers between devices  24.8 us (37%)
  Pallas kernels  6.28 us (9%)
  other arithmetic  2.5 us (4%)
  local copies, waits for them, and re-layouts  0.77 us (1%)
  between operations  0.74 us (1%)
    ppermute x2, waiting for transfers between devices, swap_halo(): b = lax.ppermute(jnp.where(odd, last, first), 'space', outer)  9.85 us
    ppermute x2, starting transfers between devices, swap_halo(): b = lax.ppermute(jnp.where(odd, last, first), 'space', outer)  9.59 us
    all_to_all x1, waiting for transfers between devices, gathered(): lax.all_to_all(pieces, 'space', 0, 0, axis_index_groups=groups_over_xy())  8.31 us
    ppermute x1, starting transfers between devices, per_device(): g2 = lax.ppermute(g0, 'chan', across)  6.38 us
    all_to_all x1, starting transfers between devices, scattered(): lax.all_to_all(value, 'space', 0, 0, axis_index_groups=groups_over_xy())  4.54 us
    ppermute x3, starting transfers between devices, gathered(): lax.ppermute(value, 'space', z_pairs(step))  4.29 us
    all_to_all x1, starting transfers between devices, gathered(): lax.all_to_all(pieces, 'space', 0, 0, axis_index_groups=groups_over_xy())  3.8 us
    ppermute x2, starting transfers between devices, swap_halo(): a = lax.ppermute(jnp.where(odd, first, last), 'space', inner)  3.67 us
  transfers between devices with their start and end apart: 12, of which 6 were waited for; matrix products, arithmetic and copies ran while one was open for 4% of the time, Pallas kernels for 4%

profile of v3, /device:TPU:32, one launch (start us, length us, event | category | flops | bytes accessed | tf_op | source)
XLA Modules:
  0.0 67.4 jit_solution(2896972728943902964)
XLA Ops:
  0.6 6.4 %collective-permute-start.1 = (f32[512,128]{1,0:T(8,128)}, f32[512,128]{1,0:T(8,128)S(1)}, u32[]{:S(2)}, u32[]{:S(2)}) collective-permute-start(f32[512,128]{1,0:T(8,128)} %bitcast.17), channel_id=1, source_target_pairs={{0,2},{1,3},{2,0},{3,1},{4,6},{5,7},{6,4},{7,5},{8,10},{9,11},{10,... | collective-permute-start | bytes 786440 | tf_op jit(solution)/shard_map/ppermute | solution.py:180
  7.0 0.0 collective-permute-start
  7.0 0.0 copy-start
  7.0 0.0 copy-start.2
  7.0 1.3 %broadcast_select_fusion = (f32[32,8,1,128]{3,2,1,0:T(1,128)S(1)}, f32[32,8,1,128]{3,2,1,0:T(1,128)S(1)}) fusion(pred[]{:T(512)S(6)} %eq.7, f32[32,8,2,128]{3,2,1,0:T(2,128)} %param.3), kind=kLoop, calls=%fused_computation.1 | loop fusion | flops 65536 | bytes 524289 | tf_op jit(solution)/shard_map/jit(_where)/select_n | solution.py:166
  8.3 1.7 %collective-permute-start.2 = (f32[256,128]{1,0:T(8,128)S(1)}, f32[256,128]{1,0:T(8,128)S(1)}, u32[]{:S(2)}, u32[]{:S(2)}) collective-permute-start(f32[256,128]{1,0:T(8,128)S(1)} %bitcast.25), channel_id=1, source_target_pairs={{0,4},{4,0},{8,12},{12,8},{16,20},{20,16},{24,28},{28,24},{32,36},... | collective-permute-start | bytes 393224 | tf_op jit(solution)/shard_map/ppermute | solution.py:165
  10.0 4.5 %collective-permute-start.3 = (f32[256,128]{1,0:T(8,128)S(1)}, f32[256,128]{1,0:T(8,128)S(1)}, u32[]{:S(2)}, u32[]{:S(2)}) collective-permute-start(f32[256,128]{1,0:T(8,128)S(1)} %bitcast.24), channel_id=1, source_target_pairs={{4,8},{12,16},{20,24},{28,32},{36,40},{44,48},{52,56},{60,64},{68,... | collective-permute-start | bytes 393224 | tf_op jit(solution)/shard_map/ppermute | solution.py:166
  14.5 0.0 collective-permute-done.2.refs_1_
  14.5 9.8 %collective-permute-done.3.refs_2_ = f32[256,128]{1,0:T(8,128)S(1)} collective-permute-done((f32[256,128]{1,0:T(8,128)S(1)}, f32[256,128]{1,0:T(8,128)S(1)}, u32[]{:S(2)}, u32[]{:S(2)}) %collective-permute-start.3) | collective-permute-done | bytes 131104 | tf_op jit(solution)/shard_map/ppermute | solution.py:166
  24.4 0.0 collective-permute-done.1.refs_5_.refs_3_
  24.4 0.0 collective-permute-done.refs_4_.refs_2_
  24.4 0.0 collective-permute-start.4
  24.4 1.5 %collective-permute-done.4.refs_6_.refs_4_ = f32[512,128]{1,0:T(8,128)S(1)} collective-permute-done((f32[512,128]{1,0:T(8,128)S(1)}, f32[512,128]{1,0:T(8,128)S(1)}, u32[]{:S(2)}, u32[]{:S(2)}) %collective-permute-start.4) | collective-permute-done | bytes 262176 | tf_op jit(solution)/shard_map/ppermute | solution.py:186
  25.9 0.0 copy-done
  25.9 0.0 copy-done.2
  25.9 3.3 %weight_kernel.1 = f32[864,128]{1,0:T(8,128)} custom-call(f32[512,128]{1,0:T(8,128)S(1)} %bitcast.15, f32[256,128]{1,0:T(8,128)S(1)} %collective-permute-done.2.refs_1_, f32[256,128]{1,0:T(8,128)S(1)} %collective-permute-done.3.refs_2_, f32[512,128]{1,0:T(8,128)S(1)} %bitcast.19, f32[512,128]{1,0:T(8,128)S(1)} %collective-permute-done.refs_4_.refs_2_, ...), custom_call_target="tpu_custom_call" | custom-call | flops 1358954496 | bytes 2097152 | tf_op jit(solution)/shard_map/weight_kernel/pallas_call | solution.py:192
  29.3 0.0 copy-start.1
  29.3 4.5 %all-to-all-start = ((f32[16,27,2,128]{3,2,1,0:T(2,128)}), f32[16,27,2,128]{3,2,1,0:T(2,128)S(1)}, u32[]{:S(2)}, u32[]{:S(2)}) async-start(f32[16,27,2,128]{3,2,1,0:T(2,128)} %bitcast.10), calls=%async_computation | async-start | bytes 884736 | tf_op jit(solution)/shard_map/all_to_all | solution.py:136
  33.8 0.0 copy-done.1
  33.8 2.1 %input_kernel.1 = (f32[512,128]{1,0:T(8,128)S(1)}, f32[256,128]{1,0:T(8,128)S(1)}, f32[256,128]{1,0:T(8,128)S(1)}) custom-call(f32[864,128]{1,0:T(8,128)S(1)} %bitcast.16, f32[512,128]{1,0:T(8,128)S(1)} %bitcast.20, f32[512,128]{1,0:T(8,128)S(1)} %collective-permute-done.refs_4_.refs_2_, f32[512,128]{1,0:T(8,128)S(1)} %collective-permute-done.1.refs_5_.refs_3_, ...), custom_call_target="tpu_custom_call" | custom-call | flops 1358954496 | bytes 2097152 | tf_op jit(solution)/shard_map/input_kernel/pallas_call | solution.py:210
  35.9 2.0 %collective-permute-start.5 = (f32[256,128]{1,0:T(8,128)S(1)}, f32[256,128]{1,0:T(8,128)S(1)}, u32[]{:S(2)}, u32[]{:S(2)}) collective-permute-start(f32[256,128]{1,0:T(8,128)S(1)} %get-tuple-element.30), channel_id=1, source_target_pairs={{0,4},{4,0},{8,12},{12,8},{16,20},{20,16},{24,28},{28,24},{32,36},... | collective-permute-start | bytes 393224 | tf_op jit(solution)/shard_map/ppermute | solution.py:165
  37.9 5.1 %collective-permute-start.6 = (f32[256,128]{1,0:T(8,128)S(1)}, f32[256,128]{1,0:T(8,128)S(1)}, u32[]{:S(2)}, u32[]{:S(2)}) collective-permute-start(f32[256,128]{1,0:T(8,128)S(1)} %get-tuple-element.31), channel_id=1, source_target_pairs={{4,8},{12,16},{20,24},{28,32},{36,40},{44,48},{52,56},{60,64},{68,... | collective-permute-start | bytes 393224 | tf_op jit(solution)/shard_map/ppermute | solution.py:166
  43.0 1.8 %all-to-all-done = f32[16,27,2,128]{3,2,1,0:T(2,128)S(1)} async-done(((f32[16,27,2,128]{3,2,1,0:T(2,128)}), f32[16,27,2,128]{3,2,1,0:T(2,128)S(1)}, u32[]{:S(2)}, u32[]{:S(2)}) %all-to-all-start) | async-done | bytes 442400 | tf_op jit(solution)/shard_map/all_to_all | solution.py:136
  44.8 0.1 reduce_sum.9.a
  44.9 1.6 %collective-permute-start.9 = (f32[27,2,128]{2,1,0:T(2,128)S(1)}, f32[27,2,128]{2,1,0:T(2,128)S(1)}, u32[]{:S(2)}, u32[]{:S(2)}) collective-permute-start(f32[27,2,128]{2,1,0:T(2,128)S(1)} %reduce_sum.9.a), channel_id=1, source_target_pairs={{0,48},{4,52},{8,56},{12,60},{16,32},{20,36},{24,40},{28,44},{32,1... | collective-permute-start | bytes 82952 | tf_op jit(solution)/shard_map/ppermute | solution.py:146
  46.5 2.2 %collective-permute-start.8 = (f32[27,2,128]{2,1,0:T(2,128)S(1)}, f32[27,2,128]{2,1,0:T(2,128)S(1)}, u32[]{:S(2)}, u32[]{:S(2)}) collective-permute-start(f32[27,2,128]{2,1,0:T(2,128)S(1)} %reduce_sum.9.a), channel_id=1, source_target_pairs={{0,32},{4,36},{8,40},{12,44},{16,48},{20,52},{24,56},{28,60},{32,0... | collective-permute-start | bytes 82952 | tf_op jit(solution)/shard_map/ppermute | solution.py:146
  48.7 0.5 collective-permute-start.7
  49.2 0.0 collective-permute-done.9.d
  49.2 2.1 %collective-permute-done.8.c = f32[27,2,128]{2,1,0:T(2,128)S(1)} collective-permute-done((f32[27,2,128]{2,1,0:T(2,128)S(1)}, f32[27,2,128]{2,1,0:T(2,128)S(1)}, u32[]{:S(2)}, u32[]{:S(2)}) %collective-permute-start.8) | collective-permute-done | bytes 27680 | tf_op jit(solution)/shard_map/ppermute | solution.py:146
  51.3 1.2 %collective-permute-done.7.b = f32[27,2,128]{2,1,0:T(2,128)S(1)} collective-permute-done((f32[27,2,128]{2,1,0:T(2,128)S(1)}, f32[27,2,128]{2,1,0:T(2,128)S(1)}, u32[]{:S(2)}, u32[]{:S(2)}) %collective-permute-start.7) | collective-permute-done | bytes 27680 | tf_op jit(solution)/shard_map/ppermute | solution.py:146
  52.6 0.9 %spread_kernel.1 = f32[16,27,2,128]{3,2,1,0:T(2,128)} custom-call(f32[27,2,128]{2,1,0:T(2,128)S(1)} %reduce_sum.9.a, f32[27,2,128]{2,1,0:T(2,128)S(1)} %collective-permute-done.7.b, f32[27,2,128]{2,1,0:T(2,128)S(1)} %collective-permute-done.8.c, f32[27,2,128]{2,1,0:T(2,128)S(1)} %collective-permute-done.9.d), custom_call_target="tpu_custom_call" | custom-call | flops 65536 | bytes 524288 | tf_op jit(solution)/shard_map/spread_kernel/pallas_call | solution.py:147
  53.4 3.8 %all-to-all-start.1 = ((f32[16,27,2,128]{3,2,1,0:T(2,128)}), f32[16,27,2,128]{3,2,1,0:T(2,128)S(1)}, u32[]{:S(2)}, u32[]{:S(2)}) async-start(f32[16,27,2,128]{3,2,1,0:T(2,128)} %spread_kernel.1), calls=%async_computation.1 | async-start | bytes 884736 | tf_op jit(solution)/shard_map/all_to_all | solution.py:156
  57.2 0.0 collective-permute-done.5
  57.3 0.0 collective-permute-done.6
  57.3 1.0 %maximum_add_fusion = f32[32,8,2,128]{3,2,1,0:T(2,128)} fusion(f32[32,8,2,128]{3,2,1,0:T(2,128)S(1)} %bitcast.14, f32[32,8,1,128]{3,2,1,0:T(1,128)S(1)} %bitcast.23, f32[32,8,1,128]{3,2,1,0:T(1,128)S(1)} %bitcast.22), kind=kLoop, calls=%fused_computation | loop fusion | flops 131072 | bytes 786432 | tf_op jit(solution)/shard_map/add | solution.py:230
  58.3 8.3 %all-to-all-done.1 = f32[16,27,2,128]{3,2,1,0:T(2,128)S(1)} async-done(((f32[16,27,2,128]{3,2,1,0:T(2,128)}), f32[16,27,2,128]{3,2,1,0:T(2,128)S(1)}, u32[]{:S(2)}, u32[]{:S(2)}) %all-to-all-start.1) | async-done | bytes 442400 | tf_op jit(solution)/shard_map/all_to_all | solution.py:156
  66.6 0.8 %copy.8 = f32[3,3,3,32,128]{4,3,2,1,0:T(8,128)} copy(f32[3,3,3,32,128]{4,3,2,1,0:T(8,128)S(1)} %bitcast.21) | data formatting | bytes 884736
  (2 shorter events, 0.0 us)
Async XLA Ops:
  0.6 23.8 %collective-permute-start.1 = (f32[512,128]{1,0:T(8,128)}, f32[512,128]{1,0:T(8,128)S(1)}, u32[]{:S(2)}, u32[]{:S(2)}) collective-permute-start(f32[512,128]{1,0:T(8,128)} %bitcast.17), channel_id=1, source_target_pairs={{0,2},{1,3},{2,0},{3,1},{4,6},{5,7},{6,4},{7,5},{8,10},{9,11},{10,... | collective-permute-start | bytes 786440 | tf_op jit(solution)/shard_map/ppermute | solution.py:180
  7.0 17.4 %collective-permute-start = (f32[512,128]{1,0:T(8,128)}, f32[512,128]{1,0:T(8,128)S(1)}, u32[]{:S(2)}, u32[]{:S(2)}) collective-permute-start(f32[512,128]{1,0:T(8,128)} %bitcast.18), channel_id=1, source_target_pairs={{0,1},{1,0},{2,3},{3,2},{4,5},{5,4},{6,7},{7,6},{8,9},{9,8},{10,11... | collective-permute-start | bytes 786440 | tf_op jit(solution)/shard_map/ppermute | solution.py:181
  7.0 18.9 %copy-start = (f32[32,8,2,128]{3,2,1,0:T(2,128)S(1)}, f32[32,8,2,128]{3,2,1,0:T(2,128)}, u32[]{:S(2)}) copy-start(f32[32,8,2,128]{3,2,1,0:T(2,128)} %param.3) | copy-start | bytes 786436
  7.0 18.9 %copy-start.2 = (f32[32,8,2,128]{3,2,1,0:T(2,128)S(1)}, f32[32,8,2,128]{3,2,1,0:T(2,128)}, u32[]{:S(2)}) copy-start(f32[32,8,2,128]{3,2,1,0:T(2,128)} %param.4) | copy-start | bytes 786436
  8.3 6.2 %collective-permute-start.2 = (f32[256,128]{1,0:T(8,128)S(1)}, f32[256,128]{1,0:T(8,128)S(1)}, u32[]{:S(2)}, u32[]{:S(2)}) collective-permute-start(f32[256,128]{1,0:T(8,128)S(1)} %bitcast.25), channel_id=1, source_target_pairs={{0,4},{4,0},{8,12},{12,8},{16,20},{20,16},{24,28},{28,24},{32,36},... | collective-permute-start | bytes 393224 | tf_op jit(solution)/shard_map/ppermute | solution.py:165
  10.0 14.4 %collective-permute-start.3 = (f32[256,128]{1,0:T(8,128)S(1)}, f32[256,128]{1,0:T(8,128)S(1)}, u32[]{:S(2)}, u32[]{:S(2)}) collective-permute-start(f32[256,128]{1,0:T(8,128)S(1)} %bitcast.24), channel_id=1, source_target_pairs={{4,8},{12,16},{20,24},{28,32},{36,40},{44,48},{52,56},{60,64},{68,... | collective-permute-start | bytes 393224 | tf_op jit(solution)/shard_map/ppermute | solution.py:166
  24.4 1.5 %collective-permute-start.4 = (f32[512,128]{1,0:T(8,128)S(1)}, f32[512,128]{1,0:T(8,128)S(1)}, u32[]{:S(2)}, u32[]{:S(2)}) collective-permute-start(f32[512,128]{1,0:T(8,128)S(1)} %collective-permute-done.1.refs_5_.refs_3_), channel_id=1, source_target_pairs={{0,1},{1,0},{2,3},{3,2},{4,5},{5,4},{6,7},{7,6},{8,9},{9,8},{10,11... | collective-permute-start | bytes 786440 | tf_op jit(solution)/shard_map/ppermute | solution.py:186
  29.3 4.5 %copy-start.1 = (f32[3,3,3,32,128]{4,3,2,1,0:T(8,128)S(1)}, f32[3,3,3,32,128]{4,3,2,1,0:T(8,128)}, u32[]{:S(2)}) copy-start(f32[3,3,3,32,128]{4,3,2,1,0:T(8,128)} %param.5) | copy-start | bytes 1327108
  29.3 15.5 %all-to-all-start = ((f32[16,27,2,128]{3,2,1,0:T(2,128)}), f32[16,27,2,128]{3,2,1,0:T(2,128)S(1)}, u32[]{:S(2)}, u32[]{:S(2)}) async-start(f32[16,27,2,128]{3,2,1,0:T(2,128)} %bitcast.10), calls=%async_computation | async-start | bytes 884736 | tf_op jit(solution)/shard_map/all_to_all | solution.py:136
  35.9 21.3 %collective-permute-start.5 = (f32[256,128]{1,0:T(8,128)S(1)}, f32[256,128]{1,0:T(8,128)S(1)}, u32[]{:S(2)}, u32[]{:S(2)}) collective-permute-start(f32[256,128]{1,0:T(8,128)S(1)} %get-tuple-element.30), channel_id=1, source_target_pairs={{0,4},{4,0},{8,12},{12,8},{16,20},{20,16},{24,28},{28,24},{32,36},... | collective-permute-start | bytes 393224 | tf_op jit(solution)/shard_map/ppermute | solution.py:165
  37.9 19.3 %collective-permute-start.6 = (f32[256,128]{1,0:T(8,128)S(1)}, f32[256,128]{1,0:T(8,128)S(1)}, u32[]{:S(2)}, u32[]{:S(2)}) collective-permute-start(f32[256,128]{1,0:T(8,128)S(1)} %get-tuple-element.31), channel_id=1, source_target_pairs={{4,8},{12,16},{20,24},{28,32},{36,40},{44,48},{52,56},{60,64},{68,... | collective-permute-start | bytes 393224 | tf_op jit(solution)/shard_map/ppermute | solution.py:166
  44.9 4.3 %collective-permute-start.9 = (f32[27,2,128]{2,1,0:T(2,128)S(1)}, f32[27,2,128]{2,1,0:T(2,128)S(1)}, u32[]{:S(2)}, u32[]{:S(2)}) collective-permute-start(f32[27,2,128]{2,1,0:T(2,128)S(1)} %reduce_sum.9.a), channel_id=1, source_target_pairs={{0,48},{4,52},{8,56},{12,60},{16,32},{20,36},{24,40},{28,44},{32,1... | collective-permute-start | bytes 82952 | tf_op jit(solution)/shard_map/ppermute | solution.py:146
  46.5 4.8 %collective-permute-start.8 = (f32[27,2,128]{2,1,0:T(2,128)S(1)}, f32[27,2,128]{2,1,0:T(2,128)S(1)}, u32[]{:S(2)}, u32[]{:S(2)}) collective-permute-start(f32[27,2,128]{2,1,0:T(2,128)S(1)} %reduce_sum.9.a), channel_id=1, source_target_pairs={{0,32},{4,36},{8,40},{12,44},{16,48},{20,52},{24,56},{28,60},{32,0... | collective-permute-start | bytes 82952 | tf_op jit(solution)/shard_map/ppermute | solution.py:146
  48.7 3.9 %collective-permute-start.7 = (f32[27,2,128]{2,1,0:T(2,128)S(1)}, f32[27,2,128]{2,1,0:T(2,128)S(1)}, u32[]{:S(2)}, u32[]{:S(2)}) collective-permute-start(f32[27,2,128]{2,1,0:T(2,128)S(1)} %reduce_sum.9.a), channel_id=1, source_target_pairs={{0,16},{4,20},{8,24},{12,28},{16,0},{20,4},{24,8},{28,12},{32,48},... | collective-permute-start | bytes 82952 | tf_op jit(solution)/shard_map/ppermute | solution.py:146
  53.4 13.2 %all-to-all-start.1 = ((f32[16,27,2,128]{3,2,1,0:T(2,128)}), f32[16,27,2,128]{3,2,1,0:T(2,128)S(1)}, u32[]{:S(2)}, u32[]{:S(2)}) async-start(f32[16,27,2,128]{3,2,1,0:T(2,128)} %spread_kernel.1), calls=%async_computation.1 | async-start | bytes 884736 | tf_op jit(solution)/shard_map/all_to_all | solution.py:156

commit v4 on v3

--- a/solution.py
+++ b/solution.py
@@ -143,7 +143,7 @@
 
 
 def gathered(value):
-    parts = [value] + [lax.ppermute(value, "space", z_pairs(step)) for step in (1, 2, 3)]
+    parts = [value] + [lax.ppermute(value, "space", z_pairs(step)) for step in (1, 3, 2)]
     pieces = pl.pallas_call(
         spread_kernel,
         out_shape=jax.ShapeDtypeStruct((AXES * AXES,) + value.shape, F32),

time: 67.8 us -> 67.6 us (level)
    ppermute x3, waiting for transfers between devices: 3.34 us -> 2.25 us  [gathered(): lax.ppermute(value, 'space', z_pairs(step))]
where the time goes in v4:
time: 67.6 us; the launch traced here: 67.3 us
  starting transfers between devices  32.7 us (48%)
  waiting for transfers between devices  24.3 us (36%)
  Pallas kernels  6.28 us (9%)
  other arithmetic  2.5 us (4%)
  local copies, waits for them, and re-layouts  0.77 us (1%)
  between operations  0.74 us (1%)
    ppermute x2, waiting for transfers between devices, swap_halo(): b = lax.ppermute(jnp.where(odd, last, first), 'space', outer)  9.85 us
    ppermute x2, starting transfers between devices, swap_halo(): b = lax.ppermute(jnp.where(odd, last, first), 'space', outer)  9.59 us
    all_to_all x1, waiting for transfers between devices, gathered(): lax.all_to_all(pieces, 'space', 0, 0, axis_index_groups=groups_over_xy())  8.92 us
    ppermute x1, starting transfers between devices, per_device(): g2 = lax.ppermute(g0, 'chan', across)  6.38 us
    all_to_all x1, starting transfers between devices, scattered(): lax.all_to_all(value, 'space', 0, 0, axis_index_groups=groups_over_xy())  4.54 us
    ppermute x3, starting transfers between devices, gathered(): lax.ppermute(value, 'space', z_pairs(step))  4.47 us
    all_to_all x1, starting transfers between devices, gathered(): lax.all_to_all(pieces, 'space', 0, 0, axis_index_groups=groups_over_xy())  4.01 us
    ppermute x2, starting transfers between devices, swap_halo(): a = lax.ppermute(jnp.where(odd, first, last), 'space', inner)  3.67 us
  transfers between devices with their start and end apart: 12, of which 6 were waited for; matrix products, arithmetic and copies ran while one was open for 4% of the time, Pallas kernels for 4%

profile of v4, /device:TPU:32, one launch (start us, length us, event | category | flops | bytes accessed | tf_op | source)
XLA Modules:
  0.0 67.3 jit_solution(2213206377542818996)
XLA Ops:
  0.6 6.4 %collective-permute-start.1 = (f32[512,128]{1,0:T(8,128)}, f32[512,128]{1,0:T(8,128)S(1)}, u32[]{:S(2)}, u32[]{:S(2)}) collective-permute-start(f32[512,128]{1,0:T(8,128)} %bitcast.17), channel_id=1, source_target_pairs={{0,2},{1,3},{2,0},{3,1},{4,6},{5,7},{6,4},{7,5},{8,10},{9,11},{10,... | collective-permute-start | bytes 786440 | tf_op jit(solution)/shard_map/ppermute | solution.py:180
  7.0 0.0 collective-permute-start
  7.0 0.0 copy-start
  7.0 0.0 copy-start.2
  7.0 1.3 %broadcast_select_fusion = (f32[32,8,1,128]{3,2,1,0:T(1,128)S(1)}, f32[32,8,1,128]{3,2,1,0:T(1,128)S(1)}) fusion(pred[]{:T(512)S(6)} %eq.7, f32[32,8,2,128]{3,2,1,0:T(2,128)} %param.3), kind=kLoop, calls=%fused_computation.1 | loop fusion | flops 65536 | bytes 524289 | tf_op jit(solution)/shard_map/jit(_where)/select_n | solution.py:166
  8.3 1.7 %collective-permute-start.2 = (f32[256,128]{1,0:T(8,128)S(1)}, f32[256,128]{1,0:T(8,128)S(1)}, u32[]{:S(2)}, u32[]{:S(2)}) collective-permute-start(f32[256,128]{1,0:T(8,128)S(1)} %bitcast.25), channel_id=1, source_target_pairs={{0,4},{4,0},{8,12},{12,8},{16,20},{20,16},{24,28},{28,24},{32,36},... | collective-permute-start | bytes 393224 | tf_op jit(solution)/shard_map/ppermute | solution.py:165
  10.0 4.5 %collective-permute-start.3 = (f32[256,128]{1,0:T(8,128)S(1)}, f32[256,128]{1,0:T(8,128)S(1)}, u32[]{:S(2)}, u32[]{:S(2)}) collective-permute-start(f32[256,128]{1,0:T(8,128)S(1)} %bitcast.24), channel_id=1, source_target_pairs={{4,8},{12,16},{20,24},{28,32},{36,40},{44,48},{52,56},{60,64},{68,... | collective-permute-start | bytes 393224 | tf_op jit(solution)/shard_map/ppermute | solution.py:166
  14.5 0.0 collective-permute-done.2.refs_1_
  14.5 9.8 %collective-permute-done.3.refs_2_ = f32[256,128]{1,0:T(8,128)S(1)} collective-permute-done((f32[256,128]{1,0:T(8,128)S(1)}, f32[256,128]{1,0:T(8,128)S(1)}, u32[]{:S(2)}, u32[]{:S(2)}) %collective-permute-start.3) | collective-permute-done | bytes 131104 | tf_op jit(solution)/shard_map/ppermute | solution.py:166
  24.4 0.0 collective-permute-done.1.refs_5_.refs_3_
  24.4 0.0 collective-permute-done.refs_4_.refs_2_
  24.4 0.0 collective-permute-start.4
  24.4 1.5 %collective-permute-done.4.refs_6_.refs_4_ = f32[512,128]{1,0:T(8,128)S(1)} collective-permute-done((f32[512,128]{1,0:T(8,128)S(1)}, f32[512,128]{1,0:T(8,128)S(1)}, u32[]{:S(2)}, u32[]{:S(2)}) %collective-permute-start.4) | collective-permute-done | bytes 262176 | tf_op jit(solution)/shard_map/ppermute | solution.py:186
  25.9 0.0 copy-done
  25.9 0.0 copy-done.2
  25.9 3.3 %weight_kernel.1 = f32[864,128]{1,0:T(8,128)} custom-call(f32[512,128]{1,0:T(8,128)S(1)} %bitcast.15, f32[256,128]{1,0:T(8,128)S(1)} %collective-permute-done.2.refs_1_, f32[256,128]{1,0:T(8,128)S(1)} %collective-permute-done.3.refs_2_, f32[512,128]{1,0:T(8,128)S(1)} %bitcast.19, f32[512,128]{1,0:T(8,128)S(1)} %collective-permute-done.refs_4_.refs_2_, ...), custom_call_target="tpu_custom_call" | custom-call | flops 1358954496 | bytes 2097152 | tf_op jit(solution)/shard_map/weight_kernel/pallas_call | solution.py:192
  29.3 0.0 copy-start.1
  29.3 4.5 %all-to-all-start = ((f32[16,27,2,128]{3,2,1,0:T(2,128)}), f32[16,27,2,128]{3,2,1,0:T(2,128)S(1)}, u32[]{:S(2)}, u32[]{:S(2)}) async-start(f32[16,27,2,128]{3,2,1,0:T(2,128)} %bitcast.10), calls=%async_computation | async-start | bytes 884736 | tf_op jit(solution)/shard_map/all_to_all | solution.py:136
  33.8 0.0 copy-done.1
  33.8 2.1 %input_kernel.1 = (f32[512,128]{1,0:T(8,128)S(1)}, f32[256,128]{1,0:T(8,128)S(1)}, f32[256,128]{1,0:T(8,128)S(1)}) custom-call(f32[864,128]{1,0:T(8,128)S(1)} %bitcast.16, f32[512,128]{1,0:T(8,128)S(1)} %bitcast.20, f32[512,128]{1,0:T(8,128)S(1)} %collective-permute-done.refs_4_.refs_2_, f32[512,128]{1,0:T(8,128)S(1)} %collective-permute-done.1.refs_5_.refs_3_, ...), custom_call_target="tpu_custom_call" | custom-call | flops 1358954496 | bytes 2097152 | tf_op jit(solution)/shard_map/input_kernel/pallas_call | solution.py:210
  35.9 2.0 %collective-permute-start.5 = (f32[256,128]{1,0:T(8,128)S(1)}, f32[256,128]{1,0:T(8,128)S(1)}, u32[]{:S(2)}, u32[]{:S(2)}) collective-permute-start(f32[256,128]{1,0:T(8,128)S(1)} %get-tuple-element.30), channel_id=1, source_target_pairs={{0,4},{4,0},{8,12},{12,8},{16,20},{20,16},{24,28},{28,24},{32,36},... | collective-permute-start | bytes 393224 | tf_op jit(solution)/shard_map/ppermute | solution.py:165
  37.9 5.1 %collective-permute-start.6 = (f32[256,128]{1,0:T(8,128)S(1)}, f32[256,128]{1,0:T(8,128)S(1)}, u32[]{:S(2)}, u32[]{:S(2)}) collective-permute-start(f32[256,128]{1,0:T(8,128)S(1)} %get-tuple-element.31), channel_id=1, source_target_pairs={{4,8},{12,16},{20,24},{28,32},{36,40},{44,48},{52,56},{60,64},{68,... | collective-permute-start | bytes 393224 | tf_op jit(solution)/shard_map/ppermute | solution.py:166
  43.0 1.8 %all-to-all-done = f32[16,27,2,128]{3,2,1,0:T(2,128)S(1)} async-done(((f32[16,27,2,128]{3,2,1,0:T(2,128)}), f32[16,27,2,128]{3,2,1,0:T(2,128)S(1)}, u32[]{:S(2)}, u32[]{:S(2)}) %all-to-all-start) | async-done | bytes 442400 | tf_op jit(solution)/shard_map/all_to_all | solution.py:136
  44.8 0.1 reduce_sum.9.a
  44.9 2.8 %collective-permute-start.9 = (f32[27,2,128]{2,1,0:T(2,128)S(1)}, f32[27,2,128]{2,1,0:T(2,128)S(1)}, u32[]{:S(2)}, u32[]{:S(2)}) collective-permute-start(f32[27,2,128]{2,1,0:T(2,128)S(1)} %reduce_sum.9.a), channel_id=1, source_target_pairs={{0,32},{4,36},{8,40},{12,44},{16,48},{20,52},{24,56},{28,60},{32,0... | collective-permute-start | bytes 82952 | tf_op jit(solution)/shard_map/ppermute | solution.py:146
  47.8 0.0 collective-permute-start.8
  47.8 1.6 %collective-permute-start.7 = (f32[27,2,128]{2,1,0:T(2,128)S(1)}, f32[27,2,128]{2,1,0:T(2,128)S(1)}, u32[]{:S(2)}, u32[]{:S(2)}) collective-permute-start(f32[27,2,128]{2,1,0:T(2,128)S(1)} %reduce_sum.9.a), channel_id=1, source_target_pairs={{0,16},{4,20},{8,24},{12,28},{16,0},{20,4},{24,8},{28,12},{32,48},... | collective-permute-start | bytes 82952 | tf_op jit(solution)/shard_map/ppermute | solution.py:146
  49.4 0.5 collective-permute-done.9.d
  49.9 1.7 %collective-permute-done.8.c = f32[27,2,128]{2,1,0:T(2,128)S(1)} collective-permute-done((f32[27,2,128]{2,1,0:T(2,128)S(1)}, f32[27,2,128]{2,1,0:T(2,128)S(1)}, u32[]{:S(2)}, u32[]{:S(2)}) %collective-permute-start.8) | collective-permute-done | bytes 27680 | tf_op jit(solution)/shard_map/ppermute | solution.py:146
  51.6 0.0 collective-permute-done.7.b
  51.7 0.9 %spread_kernel.1 = f32[16,27,2,128]{3,2,1,0:T(2,128)} custom-call(f32[27,2,128]{2,1,0:T(2,128)S(1)} %reduce_sum.9.a, f32[27,2,128]{2,1,0:T(2,128)S(1)} %collective-permute-done.7.b, f32[27,2,128]{2,1,0:T(2,128)S(1)} %collective-permute-done.8.c, f32[27,2,128]{2,1,0:T(2,128)S(1)} %collective-permute-done.9.d), custom_call_target="tpu_custom_call" | custom-call | flops 65536 | bytes 524288 | tf_op jit(solution)/shard_map/spread_kernel/pallas_call | solution.py:147
  52.5 4.0 %all-to-all-start.1 = ((f32[16,27,2,128]{3,2,1,0:T(2,128)}), f32[16,27,2,128]{3,2,1,0:T(2,128)S(1)}, u32[]{:S(2)}, u32[]{:S(2)}) async-start(f32[16,27,2,128]{3,2,1,0:T(2,128)} %spread_kernel.1), calls=%async_computation.1 | async-start | bytes 884736 | tf_op jit(solution)/shard_map/all_to_all | solution.py:156
  56.6 0.0 collective-permute-done.5
  56.6 0.0 collective-permute-done.6
  56.6 1.0 %maximum_add_fusion = f32[32,8,2,128]{3,2,1,0:T(2,128)} fusion(f32[32,8,2,128]{3,2,1,0:T(2,128)S(1)} %bitcast.14, f32[32,8,1,128]{3,2,1,0:T(1,128)S(1)} %bitcast.23, f32[32,8,1,128]{3,2,1,0:T(1,128)S(1)} %bitcast.22), kind=kLoop, calls=%fused_computation | loop fusion | flops 131072 | bytes 786432 | tf_op jit(solution)/shard_map/add | solution.py:230
  57.6 8.9 %all-to-all-done.1 = f32[16,27,2,128]{3,2,1,0:T(2,128)S(1)} async-done(((f32[16,27,2,128]{3,2,1,0:T(2,128)}), f32[16,27,2,128]{3,2,1,0:T(2,128)S(1)}, u32[]{:S(2)}, u32[]{:S(2)}) %all-to-all-start.1) | async-done | bytes 442400 | tf_op jit(solution)/shard_map/all_to_all | solution.py:156
  66.5 0.8 %copy.8 = f32[3,3,3,32,128]{4,3,2,1,0:T(8,128)} copy(f32[3,3,3,32,128]{4,3,2,1,0:T(8,128)S(1)} %bitcast.21) | data formatting | bytes 884736
  (2 shorter events, 0.0 us)
Async XLA Ops:
  0.6 23.8 %collective-permute-start.1 = (f32[512,128]{1,0:T(8,128)}, f32[512,128]{1,0:T(8,128)S(1)}, u32[]{:S(2)}, u32[]{:S(2)}) collective-permute-start(f32[512,128]{1,0:T(8,128)} %bitcast.17), channel_id=1, source_target_pairs={{0,2},{1,3},{2,0},{3,1},{4,6},{5,7},{6,4},{7,5},{8,10},{9,11},{10,... | collective-permute-start | bytes 786440 | tf_op jit(solution)/shard_map/ppermute | solution.py:180
  7.0 17.4 %collective-permute-start = (f32[512,128]{1,0:T(8,128)}, f32[512,128]{1,0:T(8,128)S(1)}, u32[]{:S(2)}, u32[]{:S(2)}) collective-permute-start(f32[512,128]{1,0:T(8,128)} %bitcast.18), channel_id=1, source_target_pairs={{0,1},{1,0},{2,3},{3,2},{4,5},{5,4},{6,7},{7,6},{8,9},{9,8},{10,11... | collective-permute-start | bytes 786440 | tf_op jit(solution)/shard_map/ppermute | solution.py:181
  7.0 18.9 %copy-start = (f32[32,8,2,128]{3,2,1,0:T(2,128)S(1)}, f32[32,8,2,128]{3,2,1,0:T(2,128)}, u32[]{:S(2)}) copy-start(f32[32,8,2,128]{3,2,1,0:T(2,128)} %param.3) | copy-start | bytes 786436
  7.0 18.9 %copy-start.2 = (f32[32,8,2,128]{3,2,1,0:T(2,128)S(1)}, f32[32,8,2,128]{3,2,1,0:T(2,128)}, u32[]{:S(2)}) copy-start(f32[32,8,2,128]{3,2,1,0:T(2,128)} %param.4) | copy-start | bytes 786436
  8.3 6.2 %collective-permute-start.2 = (f32[256,128]{1,0:T(8,128)S(1)}, f32[256,128]{1,0:T(8,128)S(1)}, u32[]{:S(2)}, u32[]{:S(2)}) collective-permute-start(f32[256,128]{1,0:T(8,128)S(1)} %bitcast.25), channel_id=1, source_target_pairs={{0,4},{4,0},{8,12},{12,8},{16,20},{20,16},{24,28},{28,24},{32,36},... | collective-permute-start | bytes 393224 | tf_op jit(solution)/shard_map/ppermute | solution.py:165
  10.0 14.4 %collective-permute-start.3 = (f32[256,128]{1,0:T(8,128)S(1)}, f32[256,128]{1,0:T(8,128)S(1)}, u32[]{:S(2)}, u32[]{:S(2)}) collective-permute-start(f32[256,128]{1,0:T(8,128)S(1)} %bitcast.24), channel_id=1, source_target_pairs={{4,8},{12,16},{20,24},{28,32},{36,40},{44,48},{52,56},{60,64},{68,... | collective-permute-start | bytes 393224 | tf_op jit(solution)/shard_map/ppermute | solution.py:166
  24.4 1.5 %collective-permute-start.4 = (f32[512,128]{1,0:T(8,128)S(1)}, f32[512,128]{1,0:T(8,128)S(1)}, u32[]{:S(2)}, u32[]{:S(2)}) collective-permute-start(f32[512,128]{1,0:T(8,128)S(1)} %collective-permute-done.1.refs_5_.refs_3_), channel_id=1, source_target_pairs={{0,1},{1,0},{2,3},{3,2},{4,5},{5,4},{6,7},{7,6},{8,9},{9,8},{10,11... | collective-permute-start | bytes 786440 | tf_op jit(solution)/shard_map/ppermute | solution.py:186
  29.3 4.5 %copy-start.1 = (f32[3,3,3,32,128]{4,3,2,1,0:T(8,128)S(1)}, f32[3,3,3,32,128]{4,3,2,1,0:T(8,128)}, u32[]{:S(2)}) copy-start(f32[3,3,3,32,128]{4,3,2,1,0:T(8,128)} %param.5) | copy-start | bytes 1327108
  29.3 15.5 %all-to-all-start = ((f32[16,27,2,128]{3,2,1,0:T(2,128)}), f32[16,27,2,128]{3,2,1,0:T(2,128)S(1)}, u32[]{:S(2)}, u32[]{:S(2)}) async-start(f32[16,27,2,128]{3,2,1,0:T(2,128)} %bitcast.10), calls=%async_computation | async-start | bytes 884736 | tf_op jit(solution)/shard_map/all_to_all | solution.py:136
  35.9 20.6 %collective-permute-start.5 = (f32[256,128]{1,0:T(8,128)S(1)}, f32[256,128]{1,0:T(8,128)S(1)}, u32[]{:S(2)}, u32[]{:S(2)}) collective-permute-start(f32[256,128]{1,0:T(8,128)S(1)} %get-tuple-element.30), channel_id=1, source_target_pairs={{0,4},{4,0},{8,12},{12,8},{16,20},{20,16},{24,28},{28,24},{32,36},... | collective-permute-start | bytes 393224 | tf_op jit(solution)/shard_map/ppermute | solution.py:165
  37.9 18.6 %collective-permute-start.6 = (f32[256,128]{1,0:T(8,128)S(1)}, f32[256,128]{1,0:T(8,128)S(1)}, u32[]{:S(2)}, u32[]{:S(2)}) collective-permute-start(f32[256,128]{1,0:T(8,128)S(1)} %get-tuple-element.31), channel_id=1, source_target_pairs={{4,8},{12,16},{20,24},{28,32},{36,40},{44,48},{52,56},{60,64},{68,... | collective-permute-start | bytes 393224 | tf_op jit(solution)/shard_map/ppermute | solution.py:166
  44.9 4.9 %collective-permute-start.9 = (f32[27,2,128]{2,1,0:T(2,128)S(1)}, f32[27,2,128]{2,1,0:T(2,128)S(1)}, u32[]{:S(2)}, u32[]{:S(2)}) collective-permute-start(f32[27,2,128]{2,1,0:T(2,128)S(1)} %reduce_sum.9.a), channel_id=1, source_target_pairs={{0,32},{4,36},{8,40},{12,44},{16,48},{20,52},{24,56},{28,60},{32,0... | collective-permute-start | bytes 82952 | tf_op jit(solution)/shard_map/ppermute | solution.py:146
  47.8 3.9 %collective-permute-start.8 = (f32[27,2,128]{2,1,0:T(2,128)S(1)}, f32[27,2,128]{2,1,0:T(2,128)S(1)}, u32[]{:S(2)}, u32[]{:S(2)}) collective-permute-start(f32[27,2,128]{2,1,0:T(2,128)S(1)} %reduce_sum.9.a), channel_id=1, source_target_pairs={{0,48},{4,52},{8,56},{12,60},{16,32},{20,36},{24,40},{28,44},{32,1... | collective-permute-start | bytes 82952 | tf_op jit(solution)/shard_map/ppermute | solution.py:146
  47.8 3.9 %collective-permute-start.7 = (f32[27,2,128]{2,1,0:T(2,128)S(1)}, f32[27,2,128]{2,1,0:T(2,128)S(1)}, u32[]{:S(2)}, u32[]{:S(2)}) collective-permute-start(f32[27,2,128]{2,1,0:T(2,128)S(1)} %reduce_sum.9.a), channel_id=1, source_target_pairs={{0,16},{4,20},{8,24},{12,28},{16,0},{20,4},{24,8},{28,12},{32,48},... | collective-permute-start | bytes 82952 | tf_op jit(solution)/shard_map/ppermute | solution.py:146
  52.5 14.0 %all-to-all-start.1 = ((f32[16,27,2,128]{3,2,1,0:T(2,128)}), f32[16,27,2,128]{3,2,1,0:T(2,128)S(1)}, u32[]{:S(2)}, u32[]{:S(2)}) async-start(f32[16,27,2,128]{3,2,1,0:T(2,128)} %spread_kernel.1), calls=%async_computation.1 | async-start | bytes 884736 | tf_op jit(solution)/shard_map/all_to_all | solution.py:156

commit v5 on v4

--- a/solution.py
+++ b/solution.py
@@ -167,6 +167,10 @@
     return a, b, odd
 
 
+def keep_kernel(value, out):
+    out[...] = value[...]
+
+
 def per_device(inputs, out_grad, weights):
     channels, planes, rows, cols = inputs.shape
     filters = weights.shape[4]
@@ -182,8 +186,17 @@
     near, far, odd = swap_halo(
         inputs[:, :, 0, :].reshape(-1, cols), inputs[:, :, 1, :].reshape(-1, cols)
     )
-    g1, g2, near, far = lax.optimization_barrier((g1, g2, near, far))
+    g1, g2, near = lax.optimization_barrier((g1, g2, near))
     g3 = lax.ppermute(g2, "chan", beside)
+    far = pl.pallas_call(
+        keep_kernel,
+        out_shape=jax.ShapeDtypeStruct(far.shape, F32),
+        in_specs=[pl.BlockSpec(memory_space=pltpu.VMEM)],
+        out_specs=pl.BlockSpec(memory_space=pltpu.VMEM),
+        compiler_params=pltpu.CompilerParams(vmem_limit_bytes=2 * 1024 * 1024),
+        cost_estimate=pl.CostEstimate(flops=3 * 10**9, bytes_accessed=2**18, transcendentals=0),
+        name="keep_kernel",
+    )(far)
     cells = planes * rows * cols
 
     def vmem(n):

time: 67.6 us -> 66.8 us (0.988)
  the two profiles are of different devices: /device:TPU:32 before, /device:TPU:128 now
where the time goes in v5:
time: 66.8 us; the launch traced here: 66.5 us
  waiting for transfers between devices  33.1 us (50%)
  starting transfers between devices  23.2 us (35%)
  Pallas kernels  6.29 us (9%)
  other arithmetic  2.43 us (4%)
  local copies, waits for them, and re-layouts  0.77 us (1%)
  between operations  0.74 us (1%)
    ppermute x1, waiting for transfers between devices, per_device(): g2 = lax.ppermute(g0, 'chan', across)  9.39 us
    all_to_all x1, waiting for transfers between devices, gathered(): lax.all_to_all(pieces, 'space', 0, 0, axis_index_groups=groups_over_xy())  8.57 us
    all_to_all x1, starting transfers between devices, scattered(): lax.all_to_all(value, 'space', 0, 0, axis_index_groups=groups_over_xy())  7.69 us
    ppermute x3, starting transfers between devices, gathered(): lax.ppermute(value, 'space', z_pairs(step))  6.57 us
    all_to_all x1, waiting for transfers between devices, scattered(): lax.all_to_all(value, 'space', 0, 0, axis_index_groups=groups_over_xy())  5.84 us
    ppermute x2, waiting for transfers between devices, swap_halo(): a = lax.ppermute(jnp.where(odd, first, last), 'space', inner)  3.88 us
    ppermute x3, waiting for transfers between devices, gathered(): lax.ppermute(value, 'space', z_pairs(step))  3.86 us
    all_to_all x1, starting transfers between devices, gathered(): lax.all_to_all(pieces, 'space', 0, 0, axis_index_groups=groups_over_xy())  3.56 us
  transfers between devices with their start and end apart: 12, of which 7 were waited for; matrix products, arithmetic and copies ran while one was open for 4% of the time, Pallas kernels for 4%

profile of v5, /device:TPU:128, one launch (start us, length us, event | category | flops | bytes accessed | tf_op | source)
XLA Modules:
  0.0 66.5 jit_solution(6494337234392368054)
XLA Ops:
  0.6 0.6 collective-permute-start.1
  1.2 0.0 collective-permute-start
  1.2 1.3 %broadcast_select_fusion = (f32[32,8,1,128]{3,2,1,0:T(1,128)S(1)}, f32[32,8,1,128]{3,2,1,0:T(1,128)S(1)}) fusion(pred[]{:T(512)S(6)} %eq.7, f32[32,8,2,128]{3,2,1,0:T(2,128)} %param.3), kind=kLoop, calls=%fused_computation.1 | loop fusion | flops 65536 | bytes 524289 | tf_op jit(solution)/shard_map/jit(_where)/select_n | solution.py:166
  2.5 1.3 %collective-permute-start.2 = (f32[256,128]{1,0:T(8,128)S(1)}, f32[256,128]{1,0:T(8,128)S(1)}, u32[]{:S(2)}, u32[]{:S(2)}) collective-permute-start(f32[256,128]{1,0:T(8,128)S(1)} %bitcast.25), channel_id=1, source_target_pairs={{0,4},{4,0},{8,12},{12,8},{16,20},{20,16},{24,28},{28,24},{32,36},... | collective-permute-start | bytes 393224 | tf_op jit(solution)/shard_map/ppermute | solution.py:165
  3.8 0.0 copy-start
  3.8 0.0 copy-start.2
  3.8 0.8 %collective-permute-start.3 = (f32[256,128]{1,0:T(8,128)S(1)}, f32[256,128]{1,0:T(8,128)S(1)}, u32[]{:S(2)}, u32[]{:S(2)}) collective-permute-start(f32[256,128]{1,0:T(8,128)S(1)} %bitcast.24), channel_id=1, source_target_pairs={{4,8},{12,16},{20,24},{28,32},{36,40},{44,48},{52,56},{60,64},{68,... | collective-permute-start | bytes 393224 | tf_op jit(solution)/shard_map/ppermute | solution.py:166
  4.6 3.9 %collective-permute-done.2.refs_1_ = f32[256,128]{1,0:T(8,128)S(1)} collective-permute-done((f32[256,128]{1,0:T(8,128)S(1)}, f32[256,128]{1,0:T(8,128)S(1)}, u32[]{:S(2)}, u32[]{:S(2)}) %collective-permute-start.2) | collective-permute-done | bytes 131104 | tf_op jit(solution)/shard_map/ppermute | solution.py:165
  8.5 9.4 %collective-permute-done.1.refs_5_.refs_3_ = f32[512,128]{1,0:T(8,128)S(1)} collective-permute-done((f32[512,128]{1,0:T(8,128)}, f32[512,128]{1,0:T(8,128)S(1)}, u32[]{:S(2)}, u32[]{:S(2)}) %collective-permute-start.1) | collective-permute-done | bytes 262176 | tf_op jit(solution)/shard_map/ppermute | solution.py:184
  17.8 0.0 collective-permute-done.refs_4_.refs_2_
  17.9 0.0 collective-permute-start.4
  17.9 0.0 collective-permute-done.3.value
  17.9 1.5 %collective-permute-done.4.refs_6_.refs_4_ = f32[512,128]{1,0:T(8,128)S(1)} collective-permute-done((f32[512,128]{1,0:T(8,128)S(1)}, f32[512,128]{1,0:T(8,128)S(1)}, u32[]{:S(2)}, u32[]{:S(2)}) %collective-permute-start.4) | collective-permute-done | bytes 262176 | tf_op jit(solution)/shard_map/ppermute | solution.py:190
  19.4 0.0 copy-done
  19.4 0.0 copy-done.2
  19.4 3.3 %weight_kernel.1 = f32[864,128]{1,0:T(8,128)} custom-call(f32[512,128]{1,0:T(8,128)S(1)} %bitcast.15, f32[256,128]{1,0:T(8,128)S(1)} %collective-permute-done.2.refs_1_, f32[256,128]{1,0:T(8,128)S(1)} %keep_kernel.1.refs_2_, f32[512,128]{1,0:T(8,128)S(1)} %bitcast.19, f32[512,128]{1,0:T(8,128)S(1)} %collective-permute-done.refs_4_.refs_2_, ...), custom_call_target="tpu_custom_call" | custom-call | flops 1358954496 | bytes 2097152 | tf_op jit(solution)/shard_map/weight_kernel/pallas_call | solution.py:205
  22.7 0.0 copy-start.1
  22.7 7.7 %all-to-all-start = ((f32[16,27,2,128]{3,2,1,0:T(2,128)}), f32[16,27,2,128]{3,2,1,0:T(2,128)S(1)}, u32[]{:S(2)}, u32[]{:S(2)}) async-start(f32[16,27,2,128]{3,2,1,0:T(2,128)} %bitcast.10), calls=%async_computation | async-start | bytes 884736 | tf_op jit(solution)/shard_map/all_to_all | solution.py:136
  30.4 0.0 copy-done.1
  30.4 2.1 %input_kernel.1 = (f32[512,128]{1,0:T(8,128)S(1)}, f32[256,128]{1,0:T(8,128)S(1)}, f32[256,128]{1,0:T(8,128)S(1)}) custom-call(f32[864,128]{1,0:T(8,128)S(1)} %bitcast.16, f32[512,128]{1,0:T(8,128)S(1)} %bitcast.20, f32[512,128]{1,0:T(8,128)S(1)} %collective-permute-done.refs_4_.refs_2_, f32[512,128]{1,0:T(8,128)S(1)} %collective-permute-done.1.refs_5_.refs_3_, ...), custom_call_target="tpu_custom_call" | custom-call | flops 1358954496 | bytes 2097152 | tf_op jit(solution)/shard_map/input_kernel/pallas_call | solution.py:223
  32.5 2.0 %collective-permute-start.5 = (f32[256,128]{1,0:T(8,128)S(1)}, f32[256,128]{1,0:T(8,128)S(1)}, u32[]{:S(2)}, u32[]{:S(2)}) collective-permute-start(f32[256,128]{1,0:T(8,128)S(1)} %get-tuple-element.28), channel_id=1, source_target_pairs={{0,4},{4,0},{8,12},{12,8},{16,20},{20,16},{24,28},{28,24},{32,36},... | collective-permute-start | bytes 393224 | tf_op jit(solution)/shard_map/ppermute | solution.py:165
  34.6 0.7 collective-permute-start.6
  35.2 5.8 %all-to-all-done = f32[16,27,2,128]{3,2,1,0:T(2,128)S(1)} async-done(((f32[16,27,2,128]{3,2,1,0:T(2,128)}), f32[16,27,2,128]{3,2,1,0:T(2,128)S(1)}, u32[]{:S(2)}, u32[]{:S(2)}) %all-to-all-start) | async-done | bytes 442400 | tf_op jit(solution)/shard_map/all_to_all | solution.py:136
  41.1 0.1 reduce_sum.9.a
  41.2 2.5 %collective-permute-start.9 = (f32[27,2,128]{2,1,0:T(2,128)S(1)}, f32[27,2,128]{2,1,0:T(2,128)S(1)}, u32[]{:S(2)}, u32[]{:S(2)}) collective-permute-start(f32[27,2,128]{2,1,0:T(2,128)S(1)} %reduce_sum.9.a), channel_id=1, source_target_pairs={{0,32},{4,36},{8,40},{12,44},{16,48},{20,52},{24,56},{28,60},{32,0... | collective-permute-start | bytes 82952 | tf_op jit(solution)/shard_map/ppermute | solution.py:146
  43.7 4.1 %collective-permute-start.8 = (f32[27,2,128]{2,1,0:T(2,128)S(1)}, f32[27,2,128]{2,1,0:T(2,128)S(1)}, u32[]{:S(2)}, u32[]{:S(2)}) collective-permute-start(f32[27,2,128]{2,1,0:T(2,128)S(1)} %reduce_sum.9.a), channel_id=1, source_target_pairs={{0,48},{4,52},{8,56},{12,60},{16,32},{20,36},{24,40},{28,44},{32,1... | collective-permute-start | bytes 82952 | tf_op jit(solution)/shard_map/ppermute | solution.py:146
  47.8 0.0 collective-permute-start.7
  47.8 0.0 collective-permute-done.9.d
  47.8 2.1 %collective-permute-done.8.c = f32[27,2,128]{2,1,0:T(2,128)S(1)} collective-permute-done((f32[27,2,128]{2,1,0:T(2,128)S(1)}, f32[27,2,128]{2,1,0:T(2,128)S(1)}, u32[]{:S(2)}, u32[]{:S(2)}) %collective-permute-start.8) | collective-permute-done | bytes 27680 | tf_op jit(solution)/shard_map/ppermute | solution.py:146
  49.9 1.7 %collective-permute-done.7.b = f32[27,2,128]{2,1,0:T(2,128)S(1)} collective-permute-done((f32[27,2,128]{2,1,0:T(2,128)S(1)}, f32[27,2,128]{2,1,0:T(2,128)S(1)}, u32[]{:S(2)}, u32[]{:S(2)}) %collective-permute-start.7) | collective-permute-done | bytes 27680 | tf_op jit(solution)/shard_map/ppermute | solution.py:146
  51.6 0.9 %spread_kernel.1 = f32[16,27,2,128]{3,2,1,0:T(2,128)} custom-call(f32[27,2,128]{2,1,0:T(2,128)S(1)} %reduce_sum.9.a, f32[27,2,128]{2,1,0:T(2,128)S(1)} %collective-permute-done.7.b, f32[27,2,128]{2,1,0:T(2,128)S(1)} %collective-permute-done.8.c, f32[27,2,128]{2,1,0:T(2,128)S(1)} %collective-permute-done.9.d), custom_call_target="tpu_custom_call" | custom-call | flops 65536 | bytes 524288 | tf_op jit(solution)/shard_map/spread_kernel/pallas_call | solution.py:147
  52.5 3.6 %all-to-all-start.1 = ((f32[16,27,2,128]{3,2,1,0:T(2,128)}), f32[16,27,2,128]{3,2,1,0:T(2,128)S(1)}, u32[]{:S(2)}, u32[]{:S(2)}) async-start(f32[16,27,2,128]{3,2,1,0:T(2,128)} %spread_kernel.1), calls=%async_computation.1 | async-start | bytes 884736 | tf_op jit(solution)/shard_map/all_to_all | solution.py:156
  56.1 0.0 collective-permute-done.5
  56.1 0.0 collective-permute-done.6
  56.1 1.0 %maximum_add_fusion = f32[32,8,2,128]{3,2,1,0:T(2,128)} fusion(f32[32,8,2,128]{3,2,1,0:T(2,128)S(1)} %bitcast.14, f32[32,8,1,128]{3,2,1,0:T(1,128)S(1)} %bitcast.23, f32[32,8,1,128]{3,2,1,0:T(1,128)S(1)} %bitcast.22), kind=kLoop, calls=%fused_computation | loop fusion | flops 131072 | bytes 786432 | tf_op jit(solution)/shard_map/add | solution.py:243
  57.1 8.6 %all-to-all-done.1 = f32[16,27,2,128]{3,2,1,0:T(2,128)S(1)} async-done(((f32[16,27,2,128]{3,2,1,0:T(2,128)}), f32[16,27,2,128]{3,2,1,0:T(2,128)S(1)}, u32[]{:S(2)}, u32[]{:S(2)}) %all-to-all-start.1) | async-done | bytes 442400 | tf_op jit(solution)/shard_map/all_to_all | solution.py:156
  65.7 0.8 %copy.8 = f32[3,3,3,32,128]{4,3,2,1,0:T(8,128)} copy(f32[3,3,3,32,128]{4,3,2,1,0:T(8,128)S(1)} %bitcast.21) | data formatting | bytes 884736
  (3 shorter events, 0.1 us)
Async XLA Ops:
  0.6 17.2 %collective-permute-start.1 = (f32[512,128]{1,0:T(8,128)}, f32[512,128]{1,0:T(8,128)S(1)}, u32[]{:S(2)}, u32[]{:S(2)}) collective-permute-start(f32[512,128]{1,0:T(8,128)} %bitcast.17), channel_id=1, source_target_pairs={{0,2},{1,3},{2,0},{3,1},{4,6},{5,7},{6,4},{7,5},{8,10},{9,11},{10,... | collective-permute-start | bytes 786440 | tf_op jit(solution)/shard_map/ppermute | solution.py:184
  1.2 16.7 %collective-permute-start = (f32[512,128]{1,0:T(8,128)}, f32[512,128]{1,0:T(8,128)S(1)}, u32[]{:S(2)}, u32[]{:S(2)}) collective-permute-start(f32[512,128]{1,0:T(8,128)} %bitcast.18), channel_id=1, source_target_pairs={{0,1},{1,0},{2,3},{3,2},{4,5},{5,4},{6,7},{7,6},{8,9},{9,8},{10,11... | collective-permute-start | bytes 786440 | tf_op jit(solution)/shard_map/ppermute | solution.py:185
  2.5 6.0 %collective-permute-start.2 = (f32[256,128]{1,0:T(8,128)S(1)}, f32[256,128]{1,0:T(8,128)S(1)}, u32[]{:S(2)}, u32[]{:S(2)}) collective-permute-start(f32[256,128]{1,0:T(8,128)S(1)} %bitcast.25), channel_id=1, source_target_pairs={{0,4},{4,0},{8,12},{12,8},{16,20},{20,16},{24,28},{28,24},{32,36},... | collective-permute-start | bytes 393224 | tf_op jit(solution)/shard_map/ppermute | solution.py:165
  3.8 15.6 %copy-start = (f32[32,8,2,128]{3,2,1,0:T(2,128)S(1)}, f32[32,8,2,128]{3,2,1,0:T(2,128)}, u32[]{:S(2)}) copy-start(f32[32,8,2,128]{3,2,1,0:T(2,128)} %param.3) | copy-start | bytes 786436
  3.8 15.6 %copy-start.2 = (f32[32,8,2,128]{3,2,1,0:T(2,128)S(1)}, f32[32,8,2,128]{3,2,1,0:T(2,128)}, u32[]{:S(2)}) copy-start(f32[32,8,2,128]{3,2,1,0:T(2,128)} %param.4) | copy-start | bytes 786436
  3.8 14.1 %collective-permute-start.3 = (f32[256,128]{1,0:T(8,128)S(1)}, f32[256,128]{1,0:T(8,128)S(1)}, u32[]{:S(2)}, u32[]{:S(2)}) collective-permute-start(f32[256,128]{1,0:T(8,128)S(1)} %bitcast.24), channel_id=1, source_target_pairs={{4,8},{12,16},{20,24},{28,32},{36,40},{44,48},{52,56},{60,64},{68,... | collective-permute-start | bytes 393224 | tf_op jit(solution)/shard_map/ppermute | solution.py:166
  17.9 1.5 %collective-permute-start.4 = (f32[512,128]{1,0:T(8,128)S(1)}, f32[512,128]{1,0:T(8,128)S(1)}, u32[]{:S(2)}, u32[]{:S(2)}) collective-permute-start(f32[512,128]{1,0:T(8,128)S(1)} %collective-permute-done.1.refs_5_.refs_3_), channel_id=1, source_target_pairs={{0,1},{1,0},{2,3},{3,2},{4,5},{5,4},{6,7},{7,6},{8,9},{9,8},{10,11... | collective-permute-start | bytes 786440 | tf_op jit(solution)/shard_map/ppermute | solution.py:190
  22.7 7.7 %copy-start.1 = (f32[3,3,3,32,128]{4,3,2,1,0:T(8,128)S(1)}, f32[3,3,3,32,128]{4,3,2,1,0:T(8,128)}, u32[]{:S(2)}) copy-start(f32[3,3,3,32,128]{4,3,2,1,0:T(8,128)} %param.5) | copy-start | bytes 1327108
  22.7 18.3 %all-to-all-start = ((f32[16,27,2,128]{3,2,1,0:T(2,128)}), f32[16,27,2,128]{3,2,1,0:T(2,128)S(1)}, u32[]{:S(2)}, u32[]{:S(2)}) async-start(f32[16,27,2,128]{3,2,1,0:T(2,128)} %bitcast.10), calls=%async_computation | async-start | bytes 884736 | tf_op jit(solution)/shard_map/all_to_all | solution.py:136
  32.5 23.5 %collective-permute-start.5 = (f32[256,128]{1,0:T(8,128)S(1)}, f32[256,128]{1,0:T(8,128)S(1)}, u32[]{:S(2)}, u32[]{:S(2)}) collective-permute-start(f32[256,128]{1,0:T(8,128)S(1)} %get-tuple-element.28), channel_id=1, source_target_pairs={{0,4},{4,0},{8,12},{12,8},{16,20},{20,16},{24,28},{28,24},{32,36},... | collective-permute-start | bytes 393224 | tf_op jit(solution)/shard_map/ppermute | solution.py:165
  34.6 21.5 %collective-permute-start.6 = (f32[256,128]{1,0:T(8,128)S(1)}, f32[256,128]{1,0:T(8,128)S(1)}, u32[]{:S(2)}, u32[]{:S(2)}) collective-permute-start(f32[256,128]{1,0:T(8,128)S(1)} %get-tuple-element.29), channel_id=1, source_target_pairs={{4,8},{12,16},{20,24},{28,32},{36,40},{44,48},{52,56},{60,64},{68,... | collective-permute-start | bytes 393224 | tf_op jit(solution)/shard_map/ppermute | solution.py:166
  41.2 6.6 %collective-permute-start.9 = (f32[27,2,128]{2,1,0:T(2,128)S(1)}, f32[27,2,128]{2,1,0:T(2,128)S(1)}, u32[]{:S(2)}, u32[]{:S(2)}) collective-permute-start(f32[27,2,128]{2,1,0:T(2,128)S(1)} %reduce_sum.9.a), channel_id=1, source_target_pairs={{0,32},{4,36},{8,40},{12,44},{16,48},{20,52},{24,56},{28,60},{32,0... | collective-permute-start | bytes 82952 | tf_op jit(solution)/shard_map/ppermute | solution.py:146
  43.7 6.2 %collective-permute-start.8 = (f32[27,2,128]{2,1,0:T(2,128)S(1)}, f32[27,2,128]{2,1,0:T(2,128)S(1)}, u32[]{:S(2)}, u32[]{:S(2)}) collective-permute-start(f32[27,2,128]{2,1,0:T(2,128)S(1)} %reduce_sum.9.a), channel_id=1, source_target_pairs={{0,48},{4,52},{8,56},{12,60},{16,32},{20,36},{24,40},{28,44},{32,1... | collective-permute-start | bytes 82952 | tf_op jit(solution)/shard_map/ppermute | solution.py:146
  47.8 3.9 %collective-permute-start.7 = (f32[27,2,128]{2,1,0:T(2,128)S(1)}, f32[27,2,128]{2,1,0:T(2,128)S(1)}, u32[]{:S(2)}, u32[]{:S(2)}) collective-permute-start(f32[27,2,128]{2,1,0:T(2,128)S(1)} %reduce_sum.9.a), channel_id=1, source_target_pairs={{0,16},{4,20},{8,24},{12,28},{16,0},{20,4},{24,8},{28,12},{32,48},... | collective-permute-start | bytes 82952 | tf_op jit(solution)/shard_map/ppermute | solution.py:146
  52.5 13.2 %all-to-all-start.1 = ((f32[16,27,2,128]{3,2,1,0:T(2,128)}), f32[16,27,2,128]{3,2,1,0:T(2,128)S(1)}, u32[]{:S(2)}, u32[]{:S(2)}) async-start(f32[16,27,2,128]{3,2,1,0:T(2,128)} %spread_kernel.1), calls=%async_computation.1 | async-start | bytes 884736 | tf_op jit(solution)/shard_map/all_to_all | solution.py:156

commit v6 on v5

--- a/solution.py
+++ b/solution.py
@@ -143,7 +143,7 @@
 
 
 def gathered(value):
-    parts = [value] + [lax.ppermute(value, "space", z_pairs(step)) for step in (1, 3, 2)]
+    parts = [value] + [lax.ppermute(value, "space", z_pairs(step)) for step in (1, 2, 3)]
     pieces = pl.pallas_call(
         spread_kernel,
         out_shape=jax.ShapeDtypeStruct((AXES * AXES,) + value.shape, F32),

time: 66.8 us -> 66.2 us (level)
  the two profiles are of different devices: /device:TPU:128 before, /device:TPU:32 now
where the time goes in v6:
time: 66.2 us; the launch traced here: 65.9 us
  starting transfers between devices  33 us (50%)
  waiting for transfers between devices  22.6 us (34%)
  Pallas kernels  6.29 us (10%)
  other arithmetic  2.43 us (4%)
  local copies, waits for them, and re-layouts  0.77 us (1%)
  between operations  0.76 us (1%)
    ppermute x2, starting transfers between devices, swap_halo(): b = lax.ppermute(jnp.where(odd, last, first), 'space', outer)  9.72 us
    all_to_all x1, waiting for transfers between devices, gathered(): lax.all_to_all(pieces, 'space', 0, 0, axis_index_groups=groups_over_xy())  8.31 us
    ppermute x1, starting transfers between devices, per_device(): g2 = lax.ppermute(g0, 'chan', across)  6.38 us
    ppermute x1, waiting for transfers between devices, per_device(): g2 = lax.ppermute(g0, 'chan', across)  5.36 us
    ppermute x3, starting transfers between devices, gathered(): lax.ppermute(value, 'space', z_pairs(step))  4.57 us
    all_to_all x1, starting transfers between devices, scattered(): lax.all_to_all(value, 'space', 0, 0, axis_index_groups=groups_over_xy())  4.53 us
    ppermute x2, waiting for transfers between devices, swap_halo(): b = lax.ppermute(jnp.where(odd, last, first), 'space', outer)  4.41 us
    all_to_all x1, starting transfers between devices, gathered(): lax.all_to_all(pieces, 'space', 0, 0, axis_index_groups=groups_over_xy())  4.09 us
  transfers between devices with their start and end apart: 12, of which 6 were waited for; matrix products, arithmetic and copies ran while one was open for 4% of the time, Pallas kernels for 4%

profile of v6, /device:TPU:32, one launch (start us, length us, event | category | flops | bytes accessed | tf_op | source)
XLA Modules:
  0.0 65.9 jit_solution(16678470123080379557)
XLA Ops:
  0.6 6.4 %collective-permute-start.1 = (f32[512,128]{1,0:T(8,128)}, f32[512,128]{1,0:T(8,128)S(1)}, u32[]{:S(2)}, u32[]{:S(2)}) collective-permute-start(f32[512,128]{1,0:T(8,128)} %bitcast.17), channel_id=1, source_target_pairs={{0,2},{1,3},{2,0},{3,1},{4,6},{5,7},{6,4},{7,5},{8,10},{9,11},{10,... | collective-permute-start | bytes 786440 | tf_op jit(solution)/shard_map/ppermute | solution.py:184
  7.0 0.0 collective-permute-start
  7.0 1.3 %broadcast_select_fusion = (f32[32,8,1,128]{3,2,1,0:T(1,128)S(1)}, f32[32,8,1,128]{3,2,1,0:T(1,128)S(1)}) fusion(pred[]{:T(512)S(6)} %eq.7, f32[32,8,2,128]{3,2,1,0:T(2,128)} %param.3), kind=kLoop, calls=%fused_computation.1 | loop fusion | flops 65536 | bytes 524289 | tf_op jit(solution)/shard_map/jit(_where)/select_n | solution.py:166
  8.3 1.7 %collective-permute-start.2 = (f32[256,128]{1,0:T(8,128)S(1)}, f32[256,128]{1,0:T(8,128)S(1)}, u32[]{:S(2)}, u32[]{:S(2)}) collective-permute-start(f32[256,128]{1,0:T(8,128)S(1)} %bitcast.25), channel_id=1, source_target_pairs={{0,4},{4,0},{8,12},{12,8},{16,20},{20,16},{24,28},{28,24},{32,36},... | collective-permute-start | bytes 393224 | tf_op jit(solution)/shard_map/ppermute | solution.py:165
  9.9 0.0 copy-start
  9.9 0.0 copy-start.2
  9.9 4.7 %collective-permute-start.3 = (f32[256,128]{1,0:T(8,128)S(1)}, f32[256,128]{1,0:T(8,128)S(1)}, u32[]{:S(2)}, u32[]{:S(2)}) collective-permute-start(f32[256,128]{1,0:T(8,128)S(1)} %bitcast.24), channel_id=1, source_target_pairs={{4,8},{12,16},{20,24},{28,32},{36,40},{44,48},{52,56},{60,64},{68,... | collective-permute-start | bytes 393224 | tf_op jit(solution)/shard_map/ppermute | solution.py:166
  14.6 0.0 collective-permute-done.2.refs_1_
  14.6 5.4 %collective-permute-done.1.refs_5_.refs_3_ = f32[512,128]{1,0:T(8,128)S(1)} collective-permute-done((f32[512,128]{1,0:T(8,128)}, f32[512,128]{1,0:T(8,128)S(1)}, u32[]{:S(2)}, u32[]{:S(2)}) %collective-permute-start.1) | collective-permute-done | bytes 262176 | tf_op jit(solution)/shard_map/ppermute | solution.py:184
  20.0 0.0 collective-permute-done.refs_4_.refs_2_
  20.0 0.0 collective-permute-start.4
  20.0 4.4 %collective-permute-done.3.value = f32[256,128]{1,0:T(8,128)S(1)} collective-permute-done((f32[256,128]{1,0:T(8,128)S(1)}, f32[256,128]{1,0:T(8,128)S(1)}, u32[]{:S(2)}, u32[]{:S(2)}) %collective-permute-start.3) | collective-permute-done | bytes 131104 | tf_op jit(solution)/shard_map/ppermute | solution.py:166
  24.4 0.0 collective-permute-done.4.refs_6_.refs_4_
  24.4 0.0 copy-done
  24.4 0.0 copy-done.2
  24.4 3.3 %weight_kernel.1 = f32[864,128]{1,0:T(8,128)} custom-call(f32[512,128]{1,0:T(8,128)S(1)} %bitcast.15, f32[256,128]{1,0:T(8,128)S(1)} %collective-permute-done.2.refs_1_, f32[256,128]{1,0:T(8,128)S(1)} %keep_kernel.1.refs_2_, f32[512,128]{1,0:T(8,128)S(1)} %bitcast.19, f32[512,128]{1,0:T(8,128)S(1)} %collective-permute-done.refs_4_.refs_2_, ...), custom_call_target="tpu_custom_call" | custom-call | flops 1358954496 | bytes 2097152 | tf_op jit(solution)/shard_map/weight_kernel/pallas_call | solution.py:205
  27.8 0.0 copy-start.1
  27.8 4.5 %all-to-all-start = ((f32[16,27,2,128]{3,2,1,0:T(2,128)}), f32[16,27,2,128]{3,2,1,0:T(2,128)S(1)}, u32[]{:S(2)}, u32[]{:S(2)}) async-start(f32[16,27,2,128]{3,2,1,0:T(2,128)} %bitcast.10), calls=%async_computation | async-start | bytes 884736 | tf_op jit(solution)/shard_map/all_to_all | solution.py:136
  32.3 0.0 copy-done.1
  32.3 2.1 %input_kernel.1 = (f32[512,128]{1,0:T(8,128)S(1)}, f32[256,128]{1,0:T(8,128)S(1)}, f32[256,128]{1,0:T(8,128)S(1)}) custom-call(f32[864,128]{1,0:T(8,128)S(1)} %bitcast.16, f32[512,128]{1,0:T(8,128)S(1)} %bitcast.20, f32[512,128]{1,0:T(8,128)S(1)} %collective-permute-done.refs_4_.refs_2_, f32[512,128]{1,0:T(8,128)S(1)} %collective-permute-done.1.refs_5_.refs_3_, ...), custom_call_target="tpu_custom_call" | custom-call | flops 1358954496 | bytes 2097152 | tf_op jit(solution)/shard_map/input_kernel/pallas_call | solution.py:223
  34.4 2.0 %collective-permute-start.5 = (f32[256,128]{1,0:T(8,128)S(1)}, f32[256,128]{1,0:T(8,128)S(1)}, u32[]{:S(2)}, u32[]{:S(2)}) collective-permute-start(f32[256,128]{1,0:T(8,128)S(1)} %get-tuple-element.28), channel_id=1, source_target_pairs={{0,4},{4,0},{8,12},{12,8},{16,20},{20,16},{24,28},{28,24},{32,36},... | collective-permute-start | bytes 393224 | tf_op jit(solution)/shard_map/ppermute | solution.py:165
  36.4 5.1 %collective-permute-start.6 = (f32[256,128]{1,0:T(8,128)S(1)}, f32[256,128]{1,0:T(8,128)S(1)}, u32[]{:S(2)}, u32[]{:S(2)}) collective-permute-start(f32[256,128]{1,0:T(8,128)S(1)} %get-tuple-element.29), channel_id=1, source_target_pairs={{4,8},{12,16},{20,24},{28,32},{36,40},{44,48},{52,56},{60,64},{68,... | collective-permute-start | bytes 393224 | tf_op jit(solution)/shard_map/ppermute | solution.py:166
  41.5 1.4 %all-to-all-done = f32[16,27,2,128]{3,2,1,0:T(2,128)S(1)} async-done(((f32[16,27,2,128]{3,2,1,0:T(2,128)}), f32[16,27,2,128]{3,2,1,0:T(2,128)S(1)}, u32[]{:S(2)}, u32[]{:S(2)}) %all-to-all-start) | async-done | bytes 442400 | tf_op jit(solution)/shard_map/all_to_all | solution.py:136
  42.9 0.1 reduce_sum.9.a
  43.0 1.9 %collective-permute-start.9 = (f32[27,2,128]{2,1,0:T(2,128)S(1)}, f32[27,2,128]{2,1,0:T(2,128)S(1)}, u32[]{:S(2)}, u32[]{:S(2)}) collective-permute-start(f32[27,2,128]{2,1,0:T(2,128)S(1)} %reduce_sum.9.a), channel_id=1, source_target_pairs={{0,48},{4,52},{8,56},{12,60},{16,32},{20,36},{24,40},{28,44},{32,1... | collective-permute-start | bytes 82952 | tf_op jit(solution)/shard_map/ppermute | solution.py:146
  44.9 2.0 %collective-permute-start.8 = (f32[27,2,128]{2,1,0:T(2,128)S(1)}, f32[27,2,128]{2,1,0:T(2,128)S(1)}, u32[]{:S(2)}, u32[]{:S(2)}) collective-permute-start(f32[27,2,128]{2,1,0:T(2,128)S(1)} %reduce_sum.9.a), channel_id=1, source_target_pairs={{0,32},{4,36},{8,40},{12,44},{16,48},{20,52},{24,56},{28,60},{32,0... | collective-permute-start | bytes 82952 | tf_op jit(solution)/shard_map/ppermute | solution.py:146
  46.9 0.7 %collective-permute-start.7 = (f32[27,2,128]{2,1,0:T(2,128)S(1)}, f32[27,2,128]{2,1,0:T(2,128)S(1)}, u32[]{:S(2)}, u32[]{:S(2)}) collective-permute-start(f32[27,2,128]{2,1,0:T(2,128)S(1)} %reduce_sum.9.a), channel_id=1, source_target_pairs={{0,16},{4,20},{8,24},{12,28},{16,0},{20,4},{24,8},{28,12},{32,48},... | collective-permute-start | bytes 82952 | tf_op jit(solution)/shard_map/ppermute | solution.py:146
  47.6 0.0 collective-permute-done.9.d
  47.6 2.1 %collective-permute-done.8.c = f32[27,2,128]{2,1,0:T(2,128)S(1)} collective-permute-done((f32[27,2,128]{2,1,0:T(2,128)S(1)}, f32[27,2,128]{2,1,0:T(2,128)S(1)}, u32[]{:S(2)}, u32[]{:S(2)}) %collective-permute-start.8) | collective-permute-done | bytes 27680 | tf_op jit(solution)/shard_map/ppermute | solution.py:146
  49.7 1.1 %collective-permute-done.7.b = f32[27,2,128]{2,1,0:T(2,128)S(1)} collective-permute-done((f32[27,2,128]{2,1,0:T(2,128)S(1)}, f32[27,2,128]{2,1,0:T(2,128)S(1)}, u32[]{:S(2)}, u32[]{:S(2)}) %collective-permute-start.7) | collective-permute-done | bytes 27680 | tf_op jit(solution)/shard_map/ppermute | solution.py:146
  50.8 0.9 %spread_kernel.1 = f32[16,27,2,128]{3,2,1,0:T(2,128)} custom-call(f32[27,2,128]{2,1,0:T(2,128)S(1)} %reduce_sum.9.a, f32[27,2,128]{2,1,0:T(2,128)S(1)} %collective-permute-done.7.b, f32[27,2,128]{2,1,0:T(2,128)S(1)} %collective-permute-done.8.c, f32[27,2,128]{2,1,0:T(2,128)S(1)} %collective-permute-done.9.d), custom_call_target="tpu_custom_call" | custom-call | flops 65536 | bytes 524288 | tf_op jit(solution)/shard_map/spread_kernel/pallas_call | solution.py:147
  51.6 4.1 %all-to-all-start.1 = ((f32[16,27,2,128]{3,2,1,0:T(2,128)}), f32[16,27,2,128]{3,2,1,0:T(2,128)S(1)}, u32[]{:S(2)}, u32[]{:S(2)}) async-start(f32[16,27,2,128]{3,2,1,0:T(2,128)} %spread_kernel.1), calls=%async_computation.1 | async-start | bytes 884736 | tf_op jit(solution)/shard_map/all_to_all | solution.py:156
  55.7 0.0 collective-permute-done.5
  55.8 0.0 collective-permute-done.6
  55.8 1.0 %maximum_add_fusion = f32[32,8,2,128]{3,2,1,0:T(2,128)} fusion(f32[32,8,2,128]{3,2,1,0:T(2,128)S(1)} %bitcast.14, f32[32,8,1,128]{3,2,1,0:T(1,128)S(1)} %bitcast.23, f32[32,8,1,128]{3,2,1,0:T(1,128)S(1)} %bitcast.22), kind=kLoop, calls=%fused_computation | loop fusion | flops 131072 | bytes 786432 | tf_op jit(solution)/shard_map/add | solution.py:243
  56.8 8.3 %all-to-all-done.1 = f32[16,27,2,128]{3,2,1,0:T(2,128)S(1)} async-done(((f32[16,27,2,128]{3,2,1,0:T(2,128)}), f32[16,27,2,128]{3,2,1,0:T(2,128)S(1)}, u32[]{:S(2)}, u32[]{:S(2)}) %all-to-all-start.1) | async-done | bytes 442400 | tf_op jit(solution)/shard_map/all_to_all | solution.py:156
  65.1 0.8 %copy.8 = f32[3,3,3,32,128]{4,3,2,1,0:T(8,128)} copy(f32[3,3,3,32,128]{4,3,2,1,0:T(8,128)S(1)} %bitcast.21) | data formatting | bytes 884736
  (3 shorter events, 0.1 us)
Async XLA Ops:
  0.6 19.3 %collective-permute-start.1 = (f32[512,128]{1,0:T(8,128)}, f32[512,128]{1,0:T(8,128)S(1)}, u32[]{:S(2)}, u32[]{:S(2)}) collective-permute-start(f32[512,128]{1,0:T(8,128)} %bitcast.17), channel_id=1, source_target_pairs={{0,2},{1,3},{2,0},{3,1},{4,6},{5,7},{6,4},{7,5},{8,10},{9,11},{10,... | collective-permute-start | bytes 786440 | tf_op jit(solution)/shard_map/ppermute | solution.py:184
  7.0 13.0 %collective-permute-start = (f32[512,128]{1,0:T(8,128)}, f32[512,128]{1,0:T(8,128)S(1)}, u32[]{:S(2)}, u32[]{:S(2)}) collective-permute-start(f32[512,128]{1,0:T(8,128)} %bitcast.18), channel_id=1, source_target_pairs={{0,1},{1,0},{2,3},{3,2},{4,5},{5,4},{6,7},{7,6},{8,9},{9,8},{10,11... | collective-permute-start | bytes 786440 | tf_op jit(solution)/shard_map/ppermute | solution.py:185
  8.3 6.3 %collective-permute-start.2 = (f32[256,128]{1,0:T(8,128)S(1)}, f32[256,128]{1,0:T(8,128)S(1)}, u32[]{:S(2)}, u32[]{:S(2)}) collective-permute-start(f32[256,128]{1,0:T(8,128)S(1)} %bitcast.25), channel_id=1, source_target_pairs={{0,4},{4,0},{8,12},{12,8},{16,20},{20,16},{24,28},{28,24},{32,36},... | collective-permute-start | bytes 393224 | tf_op jit(solution)/shard_map/ppermute | solution.py:165
  9.9 14.5 %copy-start = (f32[32,8,2,128]{3,2,1,0:T(2,128)S(1)}, f32[32,8,2,128]{3,2,1,0:T(2,128)}, u32[]{:S(2)}) copy-start(f32[32,8,2,128]{3,2,1,0:T(2,128)} %param.3) | copy-start | bytes 786436
  9.9 14.5 %copy-start.2 = (f32[32,8,2,128]{3,2,1,0:T(2,128)S(1)}, f32[32,8,2,128]{3,2,1,0:T(2,128)}, u32[]{:S(2)}) copy-start(f32[32,8,2,128]{3,2,1,0:T(2,128)} %param.4) | copy-start | bytes 786436
  9.9 14.4 %collective-permute-start.3 = (f32[256,128]{1,0:T(8,128)S(1)}, f32[256,128]{1,0:T(8,128)S(1)}, u32[]{:S(2)}, u32[]{:S(2)}) collective-permute-start(f32[256,128]{1,0:T(8,128)S(1)} %bitcast.24), channel_id=1, source_target_pairs={{4,8},{12,16},{20,24},{28,32},{36,40},{44,48},{52,56},{60,64},{68,... | collective-permute-start | bytes 393224 | tf_op jit(solution)/shard_map/ppermute | solution.py:166
  20.0 4.4 %collective-permute-start.4 = (f32[512,128]{1,0:T(8,128)S(1)}, f32[512,128]{1,0:T(8,128)S(1)}, u32[]{:S(2)}, u32[]{:S(2)}) collective-permute-start(f32[512,128]{1,0:T(8,128)S(1)} %collective-permute-done.1.refs_5_.refs_3_), channel_id=1, source_target_pairs={{0,1},{1,0},{2,3},{3,2},{4,5},{5,4},{6,7},{7,6},{8,9},{9,8},{10,11... | collective-permute-start | bytes 786440 | tf_op jit(solution)/shard_map/ppermute | solution.py:190
  27.8 4.5 %copy-start.1 = (f32[3,3,3,32,128]{4,3,2,1,0:T(8,128)S(1)}, f32[3,3,3,32,128]{4,3,2,1,0:T(8,128)}, u32[]{:S(2)}) copy-start(f32[3,3,3,32,128]{4,3,2,1,0:T(8,128)} %param.5) | copy-start | bytes 1327108
  27.8 15.1 %all-to-all-start = ((f32[16,27,2,128]{3,2,1,0:T(2,128)}), f32[16,27,2,128]{3,2,1,0:T(2,128)S(1)}, u32[]{:S(2)}, u32[]{:S(2)}) async-start(f32[16,27,2,128]{3,2,1,0:T(2,128)} %bitcast.10), calls=%async_computation | async-start | bytes 884736 | tf_op jit(solution)/shard_map/all_to_all | solution.py:136
  34.4 21.3 %collective-permute-start.5 = (f32[256,128]{1,0:T(8,128)S(1)}, f32[256,128]{1,0:T(8,128)S(1)}, u32[]{:S(2)}, u32[]{:S(2)}) collective-permute-start(f32[256,128]{1,0:T(8,128)S(1)} %get-tuple-element.28), channel_id=1, source_target_pairs={{0,4},{4,0},{8,12},{12,8},{16,20},{20,16},{24,28},{28,24},{32,36},... | collective-permute-start | bytes 393224 | tf_op jit(solution)/shard_map/ppermute | solution.py:165
  36.4 19.3 %collective-permute-start.6 = (f32[256,128]{1,0:T(8,128)S(1)}, f32[256,128]{1,0:T(8,128)S(1)}, u32[]{:S(2)}, u32[]{:S(2)}) collective-permute-start(f32[256,128]{1,0:T(8,128)S(1)} %get-tuple-element.29), channel_id=1, source_target_pairs={{4,8},{12,16},{20,24},{28,32},{36,40},{44,48},{52,56},{60,64},{68,... | collective-permute-start | bytes 393224 | tf_op jit(solution)/shard_map/ppermute | solution.py:166
  43.0 4.6 %collective-permute-start.9 = (f32[27,2,128]{2,1,0:T(2,128)S(1)}, f32[27,2,128]{2,1,0:T(2,128)S(1)}, u32[]{:S(2)}, u32[]{:S(2)}) collective-permute-start(f32[27,2,128]{2,1,0:T(2,128)S(1)} %reduce_sum.9.a), channel_id=1, source_target_pairs={{0,48},{4,52},{8,56},{12,60},{16,32},{20,36},{24,40},{28,44},{32,1... | collective-permute-start | bytes 82952 | tf_op jit(solution)/shard_map/ppermute | solution.py:146
  44.9 4.8 %collective-permute-start.8 = (f32[27,2,128]{2,1,0:T(2,128)S(1)}, f32[27,2,128]{2,1,0:T(2,128)S(1)}, u32[]{:S(2)}, u32[]{:S(2)}) collective-permute-start(f32[27,2,128]{2,1,0:T(2,128)S(1)} %reduce_sum.9.a), channel_id=1, source_target_pairs={{0,32},{4,36},{8,40},{12,44},{16,48},{20,52},{24,56},{28,60},{32,0... | collective-permute-start | bytes 82952 | tf_op jit(solution)/shard_map/ppermute | solution.py:146
  46.9 3.9 %collective-permute-start.7 = (f32[27,2,128]{2,1,0:T(2,128)S(1)}, f32[27,2,128]{2,1,0:T(2,128)S(1)}, u32[]{:S(2)}, u32[]{:S(2)}) collective-permute-start(f32[27,2,128]{2,1,0:T(2,128)S(1)} %reduce_sum.9.a), channel_id=1, source_target_pairs={{0,16},{4,20},{8,24},{12,28},{16,0},{20,4},{24,8},{28,12},{32,48},... | collective-permute-start | bytes 82952 | tf_op jit(solution)/shard_map/ppermute | solution.py:146
  51.6 13.5 %all-to-all-start.1 = ((f32[16,27,2,128]{3,2,1,0:T(2,128)}), f32[16,27,2,128]{3,2,1,0:T(2,128)S(1)}, u32[]{:S(2)}, u32[]{:S(2)}) async-start(f32[16,27,2,128]{3,2,1,0:T(2,128)} %spread_kernel.1), calls=%async_computation.1 | async-start | bytes 884736 | tf_op jit(solution)/shard_map/all_to_all | solution.py:156

commit v7 on v3

--- a/solution.py
+++ b/solution.py
@@ -167,6 +167,11 @@
     return a, b, odd
 
 
+def keep_kernel(a, b, a_out, b_out):
+    a_out[...] = a[...]
+    b_out[...] = b[...]
+
+
 def per_device(inputs, out_grad, weights):
     channels, planes, rows, cols = inputs.shape
     filters = weights.shape[4]
@@ -182,8 +187,17 @@
     near, far, odd = swap_halo(
         inputs[:, :, 0, :].reshape(-1, cols), inputs[:, :, 1, :].reshape(-1, cols)
     )
-    g1, g2, near, far = lax.optimization_barrier((g1, g2, near, far))
+    g1, g2 = lax.optimization_barrier((g1, g2))
     g3 = lax.ppermute(g2, "chan", beside)
+    far, near = pl.pallas_call(
+        keep_kernel,
+        out_shape=(jax.ShapeDtypeStruct(far.shape, F32),) * 2,
+        in_specs=[pl.BlockSpec(memory_space=pltpu.VMEM)] * 2,
+        out_specs=(pl.BlockSpec(memory_space=pltpu.VMEM),) * 2,
+        compiler_params=pltpu.CompilerParams(vmem_limit_bytes=2 * 1024 * 1024),
+        cost_estimate=pl.CostEstimate(flops=3 * 10**9, bytes_accessed=2**18, transcendentals=0),
+        name="keep_kernel",
+    )(far, near)
     cells = planes * rows * cols
 
     def vmem(n):

time: 67.8 us -> 66.2 us (0.976)
  waiting for transfers between devices: 24.8 us -> 23.6 us
    ppermute x1, waiting for transfers between devices: 0.01 us -> 5.98 us  [per_device(): g2 = lax.ppermute(g0, 'chan', across)]
    ppermute x2, waiting for transfers between devices: 9.85 us -> 4.71 us  [swap_halo(): b = lax.ppermute(jnp.where(odd, last, first), 'space', outer)]
    ppermute x2, starting transfers between devices: 3.67 us -> 2.1 us  [swap_halo(): a = lax.ppermute(jnp.where(odd, first, last), 'space', inner)]
    ppermute x1, waiting for transfers between devices: 1.53 us -> 0.01 us  [per_device(): g3 = lax.ppermute(g2, 'chan', beside)]
    select_n x1 -> x0, other arithmetic: 1.32 us -> none  [swap_halo(): b = lax.ppermute(jnp.where(odd, last, first), 'space', outer)]
    select_n x1 -> x2, other arithmetic: 0.02 us -> 1.28 us  [swap_halo(): a = lax.ppermute(jnp.where(odd, first, last), 'space', inner)]
    ppermute x2, starting transfers between devices: 9.59 us -> 10.4 us  [swap_halo(): b = lax.ppermute(jnp.where(odd, last, first), 'space', outer)]
where the time goes in v7:
time: 66.2 us; the launch traced here: 65.9 us
  starting transfers between devices  32 us (48%)
  waiting for transfers between devices  23.6 us (36%)
  Pallas kernels  6.3 us (10%)
  other arithmetic  2.43 us (4%)
  local copies, waits for them, and re-layouts  0.78 us (1%)
  between operations  0.77 us (1%)
    ppermute x2, starting transfers between devices, swap_halo(): b = lax.ppermute(jnp.where(odd, last, first), 'space', outer)  10.4 us
    all_to_all x1, waiting for transfers between devices, gathered(): lax.all_to_all(pieces, 'space', 0, 0, axis_index_groups=groups_over_xy())  8.31 us
    ppermute x1, starting transfers between devices, per_device(): g2 = lax.ppermute(g0, 'chan', across)  6.38 us
    ppermute x1, waiting for transfers between devices, per_device(): g2 = lax.ppermute(g0, 'chan', across)  5.98 us
    ppermute x2, waiting for transfers between devices, swap_halo(): b = lax.ppermute(jnp.where(odd, last, first), 'space', outer)  4.71 us
    ppermute x3, starting transfers between devices, gathered(): lax.ppermute(value, 'space', z_pairs(step))  4.55 us
    all_to_all x1, starting transfers between devices, scattered(): lax.all_to_all(value, 'space', 0, 0, axis_index_groups=groups_over_xy())  4.54 us
    all_to_all x1, starting transfers between devices, gathered(): lax.all_to_all(pieces, 'space', 0, 0, axis_index_groups=groups_over_xy())  4.1 us
  transfers between devices with their start and end apart: 12, of which 6 were waited for; matrix products, arithmetic and copies ran while one was open for 4% of the time, Pallas kernels for 4%

profile of v7, /device:TPU:32, one launch (start us, length us, event | category | flops | bytes accessed | tf_op | source)
XLA Modules:
  0.0 65.9 jit_solution(1041235195366900187)
XLA Ops:
  0.6 6.4 %collective-permute-start.3 = (f32[512,128]{1,0:T(8,128)}, f32[512,128]{1,0:T(8,128)S(1)}, u32[]{:S(2)}, u32[]{:S(2)}) collective-permute-start(f32[512,128]{1,0:T(8,128)} %bitcast.17), channel_id=1, source_target_pairs={{0,2},{1,3},{2,0},{3,1},{4,6},{5,7},{6,4},{7,5},{8,10},{9,11},{10,... | collective-permute-start | bytes 786440 | tf_op jit(solution)/shard_map/ppermute | solution.py:185
  7.0 0.0 collective-permute-start.2
  7.0 1.3 %broadcast_select_fusion = (f32[32,8,1,128]{3,2,1,0:T(1,128)S(1)}, f32[32,8,1,128]{3,2,1,0:T(1,128)S(1)}) fusion(pred[]{:T(512)S(6)} %eq.7, f32[32,8,2,128]{3,2,1,0:T(2,128)} %param.3), kind=kLoop, calls=%fused_computation.1 | loop fusion | flops 65536 | bytes 524289 | tf_op jit(solution)/shard_map/jit(_where)/select_n | solution.py:165
  8.3 5.4 %collective-permute-start = (f32[256,128]{1,0:T(8,128)S(1)}, f32[256,128]{1,0:T(8,128)S(1)}, u32[]{:S(2)}, u32[]{:S(2)}) collective-permute-start(f32[256,128]{1,0:T(8,128)S(1)} %bitcast.25), channel_id=1, source_target_pairs={{4,8},{12,16},{20,24},{28,32},{36,40},{44,48},{52,56},{60,64},{68,... | collective-permute-start | bytes 393224 | tf_op jit(solution)/shard_map/ppermute | solution.py:166
  13.6 0.0 copy-start
  13.7 0.0 copy-start.2
  13.7 0.1 collective-permute-start.1
  13.8 6.0 %collective-permute-done.3.refs_5_.refs_3_ = f32[512,128]{1,0:T(8,128)S(1)} collective-permute-done((f32[512,128]{1,0:T(8,128)}, f32[512,128]{1,0:T(8,128)S(1)}, u32[]{:S(2)}, u32[]{:S(2)}) %collective-permute-start.3) | collective-permute-done | bytes 262176 | tf_op jit(solution)/shard_map/ppermute | solution.py:185
  19.8 0.0 collective-permute-done.2.refs_4_.refs_2_
  19.8 0.0 collective-permute-start.4
  19.8 4.7 %collective-permute-done.a = f32[256,128]{1,0:T(8,128)S(1)} collective-permute-done((f32[256,128]{1,0:T(8,128)S(1)}, f32[256,128]{1,0:T(8,128)S(1)}, u32[]{:S(2)}, u32[]{:S(2)}) %collective-permute-start) | collective-permute-done | bytes 131104 | tf_op jit(solution)/shard_map/ppermute | solution.py:166
  24.5 0.0 collective-permute-done.1.b
  24.5 0.0 collective-permute-done.4.refs_6_.refs_4_
  24.5 0.0 copy-done
  24.5 0.0 copy-done.2
  24.5 3.3 %weight_kernel.1 = f32[864,128]{1,0:T(8,128)} custom-call(f32[512,128]{1,0:T(8,128)S(1)} %bitcast.15, f32[256,128]{1,0:T(8,128)S(1)} %get-tuple-element.15.refs_1_, f32[256,128]{1,0:T(8,128)S(1)} %get-tuple-element.16.refs_2_, f32[512,128]{1,0:T(8,128)S(1)} %bitcast.19, f32[512,128]{1,0:T(8,128)S(1)} %collective-permute-done.2.refs_4_.refs_2_, ...), custom_call_target="tpu_custom_call" | custom-call | flops 1358954496 | bytes 2097152 | tf_op jit(solution)/shard_map/weight_kernel/pallas_call | solution.py:206
  27.9 0.0 copy-start.1
  27.9 4.5 %all-to-all-start = ((f32[16,27,2,128]{3,2,1,0:T(2,128)}), f32[16,27,2,128]{3,2,1,0:T(2,128)S(1)}, u32[]{:S(2)}, u32[]{:S(2)}) async-start(f32[16,27,2,128]{3,2,1,0:T(2,128)} %bitcast.10), calls=%async_computation | async-start | bytes 884736 | tf_op jit(solution)/shard_map/all_to_all | solution.py:136
  32.4 0.0 copy-done.1
  32.4 2.1 %input_kernel.1 = (f32[512,128]{1,0:T(8,128)S(1)}, f32[256,128]{1,0:T(8,128)S(1)}, f32[256,128]{1,0:T(8,128)S(1)}) custom-call(f32[864,128]{1,0:T(8,128)S(1)} %bitcast.16, f32[512,128]{1,0:T(8,128)S(1)} %bitcast.20, f32[512,128]{1,0:T(8,128)S(1)} %collective-permute-done.2.refs_4_.refs_2_, f32[512,128]{1,0:T(8,128)S(1)} %collective-permute-done.3.refs_5_.refs_3_, ...), custom_call_target="tpu_custom_call" | custom-call | flops 1358954496 | bytes 2097152 | tf_op jit(solution)/shard_map/input_kernel/pallas_call | solution.py:224
  34.5 2.0 %collective-permute-start.5 = (f32[256,128]{1,0:T(8,128)S(1)}, f32[256,128]{1,0:T(8,128)S(1)}, u32[]{:S(2)}, u32[]{:S(2)}) collective-permute-start(f32[256,128]{1,0:T(8,128)S(1)} %get-tuple-element.30), channel_id=1, source_target_pairs={{0,4},{4,0},{8,12},{12,8},{16,20},{20,16},{24,28},{28,24},{32,36},... | collective-permute-start | bytes 393224 | tf_op jit(solution)/shard_map/ppermute | solution.py:165
  36.5 5.0 %collective-permute-start.6 = (f32[256,128]{1,0:T(8,128)S(1)}, f32[256,128]{1,0:T(8,128)S(1)}, u32[]{:S(2)}, u32[]{:S(2)}) collective-permute-start(f32[256,128]{1,0:T(8,128)S(1)} %get-tuple-element.31), channel_id=1, source_target_pairs={{4,8},{12,16},{20,24},{28,32},{36,40},{44,48},{52,56},{60,64},{68,... | collective-permute-start | bytes 393224 | tf_op jit(solution)/shard_map/ppermute | solution.py:166
  41.5 1.4 %all-to-all-done = f32[16,27,2,128]{3,2,1,0:T(2,128)S(1)} async-done(((f32[16,27,2,128]{3,2,1,0:T(2,128)}), f32[16,27,2,128]{3,2,1,0:T(2,128)S(1)}, u32[]{:S(2)}, u32[]{:S(2)}) %all-to-all-start) | async-done | bytes 442400 | tf_op jit(solution)/shard_map/all_to_all | solution.py:136
  42.9 0.1 reduce_sum.9.a
  43.1 1.9 %collective-permute-start.9 = (f32[27,2,128]{2,1,0:T(2,128)S(1)}, f32[27,2,128]{2,1,0:T(2,128)S(1)}, u32[]{:S(2)}, u32[]{:S(2)}) collective-permute-start(f32[27,2,128]{2,1,0:T(2,128)S(1)} %reduce_sum.9.a), channel_id=1, source_target_pairs={{0,48},{4,52},{8,56},{12,60},{16,32},{20,36},{24,40},{28,44},{32,1... | collective-permute-start | bytes 82952 | tf_op jit(solution)/shard_map/ppermute | solution.py:146
  44.9 2.0 %collective-permute-start.8 = (f32[27,2,128]{2,1,0:T(2,128)S(1)}, f32[27,2,128]{2,1,0:T(2,128)S(1)}, u32[]{:S(2)}, u32[]{:S(2)}) collective-permute-start(f32[27,2,128]{2,1,0:T(2,128)S(1)} %reduce_sum.9.a), channel_id=1, source_target_pairs={{0,32},{4,36},{8,40},{12,44},{16,48},{20,52},{24,56},{28,60},{32,0... | collective-permute-start | bytes 82952 | tf_op jit(solution)/shard_map/ppermute | solution.py:146
  46.9 0.7 %collective-permute-start.7 = (f32[27,2,128]{2,1,0:T(2,128)S(1)}, f32[27,2,128]{2,1,0:T(2,128)S(1)}, u32[]{:S(2)}, u32[]{:S(2)}) collective-permute-start(f32[27,2,128]{2,1,0:T(2,128)S(1)} %reduce_sum.9.a), channel_id=1, source_target_pairs={{0,16},{4,20},{8,24},{12,28},{16,0},{20,4},{24,8},{28,12},{32,48},... | collective-permute-start | bytes 82952 | tf_op jit(solution)/shard_map/ppermute | solution.py:146
  47.6 0.0 collective-permute-done.9.d
  47.6 2.1 %collective-permute-done.8.c = f32[27,2,128]{2,1,0:T(2,128)S(1)} collective-permute-done((f32[27,2,128]{2,1,0:T(2,128)S(1)}, f32[27,2,128]{2,1,0:T(2,128)S(1)}, u32[]{:S(2)}, u32[]{:S(2)}) %collective-permute-start.8) | collective-permute-done | bytes 27680 | tf_op jit(solution)/shard_map/ppermute | solution.py:146
  49.7 1.1 %collective-permute-done.7.b = f32[27,2,128]{2,1,0:T(2,128)S(1)} collective-permute-done((f32[27,2,128]{2,1,0:T(2,128)S(1)}, f32[27,2,128]{2,1,0:T(2,128)S(1)}, u32[]{:S(2)}, u32[]{:S(2)}) %collective-permute-start.7) | collective-permute-done | bytes 27680 | tf_op jit(solution)/shard_map/ppermute | solution.py:146
  50.8 0.9 %spread_kernel.1 = f32[16,27,2,128]{3,2,1,0:T(2,128)} custom-call(f32[27,2,128]{2,1,0:T(2,128)S(1)} %reduce_sum.9.a, f32[27,2,128]{2,1,0:T(2,128)S(1)} %collective-permute-done.7.b, f32[27,2,128]{2,1,0:T(2,128)S(1)} %collective-permute-done.8.c, f32[27,2,128]{2,1,0:T(2,128)S(1)} %collective-permute-done.9.d), custom_call_target="tpu_custom_call" | custom-call | flops 65536 | bytes 524288 | tf_op jit(solution)/shard_map/spread_kernel/pallas_call | solution.py:147
  51.7 4.1 %all-to-all-start.1 = ((f32[16,27,2,128]{3,2,1,0:T(2,128)}), f32[16,27,2,128]{3,2,1,0:T(2,128)S(1)}, u32[]{:S(2)}, u32[]{:S(2)}) async-start(f32[16,27,2,128]{3,2,1,0:T(2,128)} %spread_kernel.1), calls=%async_computation.1 | async-start | bytes 884736 | tf_op jit(solution)/shard_map/all_to_all | solution.py:156
  55.8 0.0 collective-permute-done.5
  55.8 0.0 collective-permute-done.6
  55.8 1.0 %maximum_add_fusion = f32[32,8,2,128]{3,2,1,0:T(2,128)} fusion(f32[32,8,2,128]{3,2,1,0:T(2,128)S(1)} %bitcast.14, f32[32,8,1,128]{3,2,1,0:T(1,128)S(1)} %bitcast.23, f32[32,8,1,128]{3,2,1,0:T(1,128)S(1)} %bitcast.22), kind=kLoop, calls=%fused_computation | loop fusion | flops 131072 | bytes 786432 | tf_op jit(solution)/shard_map/add | solution.py:244
  56.8 8.3 %all-to-all-done.1 = f32[16,27,2,128]{3,2,1,0:T(2,128)S(1)} async-done(((f32[16,27,2,128]{3,2,1,0:T(2,128)}), f32[16,27,2,128]{3,2,1,0:T(2,128)S(1)}, u32[]{:S(2)}, u32[]{:S(2)}) %all-to-all-start.1) | async-done | bytes 442400 | tf_op jit(solution)/shard_map/all_to_all | solution.py:156
  65.1 0.8 %copy.8 = f32[3,3,3,32,128]{4,3,2,1,0:T(8,128)} copy(f32[3,3,3,32,128]{4,3,2,1,0:T(8,128)S(1)} %bitcast.21) | data formatting | bytes 884736
  (3 shorter events, 0.1 us)
Async XLA Ops:
  0.6 19.1 %collective-permute-start.3 = (f32[512,128]{1,0:T(8,128)}, f32[512,128]{1,0:T(8,128)S(1)}, u32[]{:S(2)}, u32[]{:S(2)}) collective-permute-start(f32[512,128]{1,0:T(8,128)} %bitcast.17), channel_id=1, source_target_pairs={{0,2},{1,3},{2,0},{3,1},{4,6},{5,7},{6,4},{7,5},{8,10},{9,11},{10,... | collective-permute-start | bytes 786440 | tf_op jit(solution)/shard_map/ppermute | solution.py:185
  7.0 12.7 %collective-permute-start.2 = (f32[512,128]{1,0:T(8,128)}, f32[512,128]{1,0:T(8,128)S(1)}, u32[]{:S(2)}, u32[]{:S(2)}) collective-permute-start(f32[512,128]{1,0:T(8,128)} %bitcast.18), channel_id=1, source_target_pairs={{0,1},{1,0},{2,3},{3,2},{4,5},{5,4},{6,7},{7,6},{8,9},{9,8},{10,11... | collective-permute-start | bytes 786440 | tf_op jit(solution)/shard_map/ppermute | solution.py:186
  8.3 16.2 %collective-permute-start = (f32[256,128]{1,0:T(8,128)S(1)}, f32[256,128]{1,0:T(8,128)S(1)}, u32[]{:S(2)}, u32[]{:S(2)}) collective-permute-start(f32[256,128]{1,0:T(8,128)S(1)} %bitcast.25), channel_id=1, source_target_pairs={{4,8},{12,16},{20,24},{28,32},{36,40},{44,48},{52,56},{60,64},{68,... | collective-permute-start | bytes 393224 | tf_op jit(solution)/shard_map/ppermute | solution.py:166
  13.6 10.9 %copy-start = (f32[32,8,2,128]{3,2,1,0:T(2,128)S(1)}, f32[32,8,2,128]{3,2,1,0:T(2,128)}, u32[]{:S(2)}) copy-start(f32[32,8,2,128]{3,2,1,0:T(2,128)} %param.3) | copy-start | bytes 786436
  13.7 10.9 %copy-start.2 = (f32[32,8,2,128]{3,2,1,0:T(2,128)S(1)}, f32[32,8,2,128]{3,2,1,0:T(2,128)}, u32[]{:S(2)}) copy-start(f32[32,8,2,128]{3,2,1,0:T(2,128)} %param.4) | copy-start | bytes 786436
  13.7 10.8 %collective-permute-start.1 = (f32[256,128]{1,0:T(8,128)S(1)}, f32[256,128]{1,0:T(8,128)S(1)}, u32[]{:S(2)}, u32[]{:S(2)}) collective-permute-start(f32[256,128]{1,0:T(8,128)S(1)} %bitcast.24), channel_id=1, source_target_pairs={{0,4},{4,0},{8,12},{12,8},{16,20},{20,16},{24,28},{28,24},{32,36},... | collective-permute-start | bytes 393224 | tf_op jit(solution)/shard_map/ppermute | solution.py:165
  19.8 4.7 %collective-permute-start.4 = (f32[512,128]{1,0:T(8,128)S(1)}, f32[512,128]{1,0:T(8,128)S(1)}, u32[]{:S(2)}, u32[]{:S(2)}) collective-permute-start(f32[512,128]{1,0:T(8,128)S(1)} %collective-permute-done.3.refs_5_.refs_3_), channel_id=1, source_target_pairs={{0,1},{1,0},{2,3},{3,2},{4,5},{5,4},{6,7},{7,6},{8,9},{9,8},{10,11... | collective-permute-start | bytes 786440 | tf_op jit(solution)/shard_map/ppermute | solution.py:191
  27.9 4.5 %copy-start.1 = (f32[3,3,3,32,128]{4,3,2,1,0:T(8,128)S(1)}, f32[3,3,3,32,128]{4,3,2,1,0:T(8,128)}, u32[]{:S(2)}) copy-start(f32[3,3,3,32,128]{4,3,2,1,0:T(8,128)} %param.5) | copy-start | bytes 1327108
  27.9 15.1 %all-to-all-start = ((f32[16,27,2,128]{3,2,1,0:T(2,128)}), f32[16,27,2,128]{3,2,1,0:T(2,128)S(1)}, u32[]{:S(2)}, u32[]{:S(2)}) async-start(f32[16,27,2,128]{3,2,1,0:T(2,128)} %bitcast.10), calls=%async_computation | async-start | bytes 884736 | tf_op jit(solution)/shard_map/all_to_all | solution.py:136
  34.5 21.2 %collective-permute-start.5 = (f32[256,128]{1,0:T(8,128)S(1)}, f32[256,128]{1,0:T(8,128)S(1)}, u32[]{:S(2)}, u32[]{:S(2)}) collective-permute-start(f32[256,128]{1,0:T(8,128)S(1)} %get-tuple-element.30), channel_id=1, source_target_pairs={{0,4},{4,0},{8,12},{12,8},{16,20},{20,16},{24,28},{28,24},{32,36},... | collective-permute-start | bytes 393224 | tf_op jit(solution)/shard_map/ppermute | solution.py:165
  36.5 19.2 %collective-permute-start.6 = (f32[256,128]{1,0:T(8,128)S(1)}, f32[256,128]{1,0:T(8,128)S(1)}, u32[]{:S(2)}, u32[]{:S(2)}) collective-permute-start(f32[256,128]{1,0:T(8,128)S(1)} %get-tuple-element.31), channel_id=1, source_target_pairs={{4,8},{12,16},{20,24},{28,32},{36,40},{44,48},{52,56},{60,64},{68,... | collective-permute-start | bytes 393224 | tf_op jit(solution)/shard_map/ppermute | solution.py:166
  43.1 4.6 %collective-permute-start.9 = (f32[27,2,128]{2,1,0:T(2,128)S(1)}, f32[27,2,128]{2,1,0:T(2,128)S(1)}, u32[]{:S(2)}, u32[]{:S(2)}) collective-permute-start(f32[27,2,128]{2,1,0:T(2,128)S(1)} %reduce_sum.9.a), channel_id=1, source_target_pairs={{0,48},{4,52},{8,56},{12,60},{16,32},{20,36},{24,40},{28,44},{32,1... | collective-permute-start | bytes 82952 | tf_op jit(solution)/shard_map/ppermute | solution.py:146
  44.9 4.8 %collective-permute-start.8 = (f32[27,2,128]{2,1,0:T(2,128)S(1)}, f32[27,2,128]{2,1,0:T(2,128)S(1)}, u32[]{:S(2)}, u32[]{:S(2)}) collective-permute-start(f32[27,2,128]{2,1,0:T(2,128)S(1)} %reduce_sum.9.a), channel_id=1, source_target_pairs={{0,32},{4,36},{8,40},{12,44},{16,48},{20,52},{24,56},{28,60},{32,0... | collective-permute-start | bytes 82952 | tf_op jit(solution)/shard_map/ppermute | solution.py:146
  46.9 3.9 %collective-permute-start.7 = (f32[27,2,128]{2,1,0:T(2,128)S(1)}, f32[27,2,128]{2,1,0:T(2,128)S(1)}, u32[]{:S(2)}, u32[]{:S(2)}) collective-permute-start(f32[27,2,128]{2,1,0:T(2,128)S(1)} %reduce_sum.9.a), channel_id=1, source_target_pairs={{0,16},{4,20},{8,24},{12,28},{16,0},{20,4},{24,8},{28,12},{32,48},... | collective-permute-start | bytes 82952 | tf_op jit(solution)/shard_map/ppermute | solution.py:146
  51.7 13.5 %all-to-all-start.1 = ((f32[16,27,2,128]{3,2,1,0:T(2,128)}), f32[16,27,2,128]{3,2,1,0:T(2,128)S(1)}, u32[]{:S(2)}, u32[]{:S(2)}) async-start(f32[16,27,2,128]{3,2,1,0:T(2,128)} %spread_kernel.1), calls=%async_computation.1 | async-start | bytes 884736 | tf_op jit(solution)/shard_map/all_to_all | solution.py:156

commit v8 on v6

--- a/solution.py
+++ b/solution.py
@@ -211,7 +211,7 @@
             pltpu.VMEM((6 * channels, (planes + 2) * 4 * cols), BF),
             pltpu.VMEM((2 * filters, cells), BF),
         ],
-        compiler_params=pltpu.CompilerParams(vmem_limit_bytes=48 * 1024 * 1024),
+        compiler_params=pltpu.CompilerParams(vmem_limit_bytes=16 * 1024 * 1024),
         cost_estimate=pl.CostEstimate(
             flops=6 * 27 * channels * filters * cells, bytes_accessed=2**21, transcendentals=0
         ),
@@ -229,7 +229,7 @@
             pltpu.VMEM((9 * channels, 9 * filters), BF),
             pltpu.VMEM((2 * filters, cells), BF),
         ],
-        compiler_params=pltpu.CompilerParams(vmem_limit_bytes=48 * 1024 * 1024),
+        compiler_params=pltpu.CompilerParams(vmem_limit_bytes=16 * 1024 * 1024),
         cost_estimate=pl.CostEstimate(
             flops=6 * 27 * channels * filters * cells, bytes_accessed=2**21, transcendentals=0
         ),

time: 66.2 us -> 66.2 us (level)
  no operation moved by 1% of the time
where the time goes in v8:
time: 66.2 us; the launch traced here: 65.9 us
  starting transfers between devices  33 us (50%)
  waiting for transfers between devices  22.6 us (34%)
  Pallas kernels  6.29 us (10%)
  other arithmetic  2.43 us (4%)
  local copies, waits for them, and re-layouts  0.77 us (1%)
  between operations  0.76 us (1%)
    ppermute x2, starting transfers between devices, swap_halo(): b = lax.ppermute(jnp.where(odd, last, first), 'space', outer)  9.72 us
    all_to_all x1, waiting for transfers between devices, gathered(): lax.all_to_all(pieces, 'space', 0, 0, axis_index_groups=groups_over_xy())  8.31 us
    ppermute x1, starting transfers between devices, per_device(): g2 = lax.ppermute(g0, 'chan', across)  6.38 us
    ppermute x1, waiting for transfers between devices, per_device(): g2 = lax.ppermute(g0, 'chan', across)  5.36 us
    ppermute x3, starting transfers between devices, gathered(): lax.ppermute(value, 'space', z_pairs(step))  4.57 us
    all_to_all x1, starting transfers between devices, scattered(): lax.all_to_all(value, 'space', 0, 0, axis_index_groups=groups_over_xy())  4.53 us
    ppermute x2, waiting for transfers between devices, swap_halo(): b = lax.ppermute(jnp.where(odd, last, first), 'space', outer)  4.41 us
    all_to_all x1, starting transfers between devices, gathered(): lax.all_to_all(pieces, 'space', 0, 0, axis_index_groups=groups_over_xy())  4.09 us
  transfers between devices with their start and end apart: 12, of which 6 were waited for; matrix products, arithmetic and copies ran while one was open for 4% of the time, Pallas kernels for 4%

profile of v8, /device:TPU:32, one launch (start us, length us, event | category | flops | bytes accessed | tf_op | source)
XLA Modules:
  0.0 65.9 jit_solution(2032214880819643321)
XLA Ops:
  0.6 6.4 %collective-permute-start.1 = (f32[512,128]{1,0:T(8,128)}, f32[512,128]{1,0:T(8,128)S(1)}, u32[]{:S(2)}, u32[]{:S(2)}) collective-permute-start(f32[512,128]{1,0:T(8,128)} %bitcast.17), channel_id=1, source_target_pairs={{0,2},{1,3},{2,0},{3,1},{4,6},{5,7},{6,4},{7,5},{8,10},{9,11},{10,... | collective-permute-start | bytes 786440 | tf_op jit(solution)/shard_map/ppermute | solution.py:184
  7.0 0.0 collective-permute-start
  7.0 1.3 %broadcast_select_fusion = (f32[32,8,1,128]{3,2,1,0:T(1,128)S(1)}, f32[32,8,1,128]{3,2,1,0:T(1,128)S(1)}) fusion(pred[]{:T(512)S(6)} %eq.7, f32[32,8,2,128]{3,2,1,0:T(2,128)} %param.3), kind=kLoop, calls=%fused_computation.1 | loop fusion | flops 65536 | bytes 524289 | tf_op jit(solution)/shard_map/jit(_where)/select_n | solution.py:166
  8.3 1.7 %collective-permute-start.2 = (f32[256,128]{1,0:T(8,128)S(1)}, f32[256,128]{1,0:T(8,128)S(1)}, u32[]{:S(2)}, u32[]{:S(2)}) collective-permute-start(f32[256,128]{1,0:T(8,128)S(1)} %bitcast.25), channel_id=1, source_target_pairs={{0,4},{4,0},{8,12},{12,8},{16,20},{20,16},{24,28},{28,24},{32,36},... | collective-permute-start | bytes 393224 | tf_op jit(solution)/shard_map/ppermute | solution.py:165
  9.9 0.0 copy-start
  9.9 0.0 copy-start.2
  9.9 4.7 %collective-permute-start.3 = (f32[256,128]{1,0:T(8,128)S(1)}, f32[256,128]{1,0:T(8,128)S(1)}, u32[]{:S(2)}, u32[]{:S(2)}) collective-permute-start(f32[256,128]{1,0:T(8,128)S(1)} %bitcast.24), channel_id=1, source_target_pairs={{4,8},{12,16},{20,24},{28,32},{36,40},{44,48},{52,56},{60,64},{68,... | collective-permute-start | bytes 393224 | tf_op jit(solution)/shard_map/ppermute | solution.py:166
  14.6 0.0 collective-permute-done.2.refs_1_
  14.6 5.4 %collective-permute-done.1.refs_5_.refs_3_ = f32[512,128]{1,0:T(8,128)S(1)} collective-permute-done((f32[512,128]{1,0:T(8,128)}, f32[512,128]{1,0:T(8,128)S(1)}, u32[]{:S(2)}, u32[]{:S(2)}) %collective-permute-start.1) | collective-permute-done | bytes 262176 | tf_op jit(solution)/shard_map/ppermute | solution.py:184
  20.0 0.0 collective-permute-done.refs_4_.refs_2_
  20.0 0.0 collective-permute-start.4
  20.0 4.4 %collective-permute-done.3.value = f32[256,128]{1,0:T(8,128)S(1)} collective-permute-done((f32[256,128]{1,0:T(8,128)S(1)}, f32[256,128]{1,0:T(8,128)S(1)}, u32[]{:S(2)}, u32[]{:S(2)}) %collective-permute-start.3) | collective-permute-done | bytes 131104 | tf_op jit(solution)/shard_map/ppermute | solution.py:166
  24.4 0.0 collective-permute-done.4.refs_6_.refs_4_
  24.4 0.0 copy-done
  24.4 0.0 copy-done.2
  24.4 3.3 %weight_kernel.1 = f32[864,128]{1,0:T(8,128)} custom-call(f32[512,128]{1,0:T(8,128)S(1)} %bitcast.15, f32[256,128]{1,0:T(8,128)S(1)} %collective-permute-done.2.refs_1_, f32[256,128]{1,0:T(8,128)S(1)} %keep_kernel.1.refs_2_, f32[512,128]{1,0:T(8,128)S(1)} %bitcast.19, f32[512,128]{1,0:T(8,128)S(1)} %collective-permute-done.refs_4_.refs_2_, ...), custom_call_target="tpu_custom_call" | custom-call | flops 1358954496 | bytes 2097152 | tf_op jit(solution)/shard_map/weight_kernel/pallas_call | solution.py:205
  27.8 0.0 copy-start.1
  27.8 4.5 %all-to-all-start = ((f32[16,27,2,128]{3,2,1,0:T(2,128)}), f32[16,27,2,128]{3,2,1,0:T(2,128)S(1)}, u32[]{:S(2)}, u32[]{:S(2)}) async-start(f32[16,27,2,128]{3,2,1,0:T(2,128)} %bitcast.10), calls=%async_computation | async-start | bytes 884736 | tf_op jit(solution)/shard_map/all_to_all | solution.py:136
  32.3 0.0 copy-done.1
  32.3 2.1 %input_kernel.1 = (f32[512,128]{1,0:T(8,128)S(1)}, f32[256,128]{1,0:T(8,128)S(1)}, f32[256,128]{1,0:T(8,128)S(1)}) custom-call(f32[864,128]{1,0:T(8,128)S(1)} %bitcast.16, f32[512,128]{1,0:T(8,128)S(1)} %bitcast.20, f32[512,128]{1,0:T(8,128)S(1)} %collective-permute-done.refs_4_.refs_2_, f32[512,128]{1,0:T(8,128)S(1)} %collective-permute-done.1.refs_5_.refs_3_, ...), custom_call_target="tpu_custom_call" | custom-call | flops 1358954496 | bytes 2097152 | tf_op jit(solution)/shard_map/input_kernel/pallas_call | solution.py:223
  34.4 2.0 %collective-permute-start.5 = (f32[256,128]{1,0:T(8,128)S(1)}, f32[256,128]{1,0:T(8,128)S(1)}, u32[]{:S(2)}, u32[]{:S(2)}) collective-permute-start(f32[256,128]{1,0:T(8,128)S(1)} %get-tuple-element.28), channel_id=1, source_target_pairs={{0,4},{4,0},{8,12},{12,8},{16,20},{20,16},{24,28},{28,24},{32,36},... | collective-permute-start | bytes 393224 | tf_op jit(solution)/shard_map/ppermute | solution.py:165
  36.4 5.1 %collective-permute-start.6 = (f32[256,128]{1,0:T(8,128)S(1)}, f32[256,128]{1,0:T(8,128)S(1)}, u32[]{:S(2)}, u32[]{:S(2)}) collective-permute-start(f32[256,128]{1,0:T(8,128)S(1)} %get-tuple-element.29), channel_id=1, source_target_pairs={{4,8},{12,16},{20,24},{28,32},{36,40},{44,48},{52,56},{60,64},{68,... | collective-permute-start | bytes 393224 | tf_op jit(solution)/shard_map/ppermute | solution.py:166
  41.5 1.4 %all-to-all-done = f32[16,27,2,128]{3,2,1,0:T(2,128)S(1)} async-done(((f32[16,27,2,128]{3,2,1,0:T(2,128)}), f32[16,27,2,128]{3,2,1,0:T(2,128)S(1)}, u32[]{:S(2)}, u32[]{:S(2)}) %all-to-all-start) | async-done | bytes 442400 | tf_op jit(solution)/shard_map/all_to_all | solution.py:136
  42.9 0.1 reduce_sum.9.a
  43.0 1.9 %collective-permute-start.9 = (f32[27,2,128]{2,1,0:T(2,128)S(1)}, f32[27,2,128]{2,1,0:T(2,128)S(1)}, u32[]{:S(2)}, u32[]{:S(2)}) collective-permute-start(f32[27,2,128]{2,1,0:T(2,128)S(1)} %reduce_sum.9.a), channel_id=1, source_target_pairs={{0,48},{4,52},{8,56},{12,60},{16,32},{20,36},{24,40},{28,44},{32,1... | collective-permute-start | bytes 82952 | tf_op jit(solution)/shard_map/ppermute | solution.py:146
  44.9 2.0 %collective-permute-start.8 = (f32[27,2,128]{2,1,0:T(2,128)S(1)}, f32[27,2,128]{2,1,0:T(2,128)S(1)}, u32[]{:S(2)}, u32[]{:S(2)}) collective-permute-start(f32[27,2,128]{2,1,0:T(2,128)S(1)} %reduce_sum.9.a), channel_id=1, source_target_pairs={{0,32},{4,36},{8,40},{12,44},{16,48},{20,52},{24,56},{28,60},{32,0... | collective-permute-start | bytes 82952 | tf_op jit(solution)/shard_map/ppermute | solution.py:146
  46.9 0.7 %collective-permute-start.7 = (f32[27,2,128]{2,1,0:T(2,128)S(1)}, f32[27,2,128]{2,1,0:T(2,128)S(1)}, u32[]{:S(2)}, u32[]{:S(2)}) collective-permute-start(f32[27,2,128]{2,1,0:T(2,128)S(1)} %reduce_sum.9.a), channel_id=1, source_target_pairs={{0,16},{4,20},{8,24},{12,28},{16,0},{20,4},{24,8},{28,12},{32,48},... | collective-permute-start | bytes 82952 | tf_op jit(solution)/shard_map/ppermute | solution.py:146
  47.6 0.0 collective-permute-done.9.d
  47.6 2.1 %collective-permute-done.8.c = f32[27,2,128]{2,1,0:T(2,128)S(1)} collective-permute-done((f32[27,2,128]{2,1,0:T(2,128)S(1)}, f32[27,2,128]{2,1,0:T(2,128)S(1)}, u32[]{:S(2)}, u32[]{:S(2)}) %collective-permute-start.8) | collective-permute-done | bytes 27680 | tf_op jit(solution)/shard_map/ppermute | solution.py:146
  49.7 1.1 %collective-permute-done.7.b = f32[27,2,128]{2,1,0:T(2,128)S(1)} collective-permute-done((f32[27,2,128]{2,1,0:T(2,128)S(1)}, f32[27,2,128]{2,1,0:T(2,128)S(1)}, u32[]{:S(2)}, u32[]{:S(2)}) %collective-permute-start.7) | collective-permute-done | bytes 27680 | tf_op jit(solution)/shard_map/ppermute | solution.py:146
  50.8 0.9 %spread_kernel.1 = f32[16,27,2,128]{3,2,1,0:T(2,128)} custom-call(f32[27,2,128]{2,1,0:T(2,128)S(1)} %reduce_sum.9.a, f32[27,2,128]{2,1,0:T(2,128)S(1)} %collective-permute-done.7.b, f32[27,2,128]{2,1,0:T(2,128)S(1)} %collective-permute-done.8.c, f32[27,2,128]{2,1,0:T(2,128)S(1)} %collective-permute-done.9.d), custom_call_target="tpu_custom_call" | custom-call | flops 65536 | bytes 524288 | tf_op jit(solution)/shard_map/spread_kernel/pallas_call | solution.py:147
  51.6 4.1 %all-to-all-start.1 = ((f32[16,27,2,128]{3,2,1,0:T(2,128)}), f32[16,27,2,128]{3,2,1,0:T(2,128)S(1)}, u32[]{:S(2)}, u32[]{:S(2)}) async-start(f32[16,27,2,128]{3,2,1,0:T(2,128)} %spread_kernel.1), calls=%async_computation.1 | async-start | bytes 884736 | tf_op jit(solution)/shard_map/all_to_all | solution.py:156
  55.7 0.0 collective-permute-done.5
  55.8 0.0 collective-permute-done.6
  55.8 1.0 %maximum_add_fusion = f32[32,8,2,128]{3,2,1,0:T(2,128)} fusion(f32[32,8,2,128]{3,2,1,0:T(2,128)S(1)} %bitcast.14, f32[32,8,1,128]{3,2,1,0:T(1,128)S(1)} %bitcast.23, f32[32,8,1,128]{3,2,1,0:T(1,128)S(1)} %bitcast.22), kind=kLoop, calls=%fused_computation | loop fusion | flops 131072 | bytes 786432 | tf_op jit(solution)/shard_map/add | solution.py:243
  56.8 8.3 %all-to-all-done.1 = f32[16,27,2,128]{3,2,1,0:T(2,128)S(1)} async-done(((f32[16,27,2,128]{3,2,1,0:T(2,128)}), f32[16,27,2,128]{3,2,1,0:T(2,128)S(1)}, u32[]{:S(2)}, u32[]{:S(2)}) %all-to-all-start.1) | async-done | bytes 442400 | tf_op jit(solution)/shard_map/all_to_all | solution.py:156
  65.1 0.8 %copy.8 = f32[3,3,3,32,128]{4,3,2,1,0:T(8,128)} copy(f32[3,3,3,32,128]{4,3,2,1,0:T(8,128)S(1)} %bitcast.21) | data formatting | bytes 884736
  (3 shorter events, 0.1 us)
Async XLA Ops:
  0.6 19.3 %collective-permute-start.1 = (f32[512,128]{1,0:T(8,128)}, f32[512,128]{1,0:T(8,128)S(1)}, u32[]{:S(2)}, u32[]{:S(2)}) collective-permute-start(f32[512,128]{1,0:T(8,128)} %bitcast.17), channel_id=1, source_target_pairs={{0,2},{1,3},{2,0},{3,1},{4,6},{5,7},{6,4},{7,5},{8,10},{9,11},{10,... | collective-permute-start | bytes 786440 | tf_op jit(solution)/shard_map/ppermute | solution.py:184
  7.0 13.0 %collective-permute-start = (f32[512,128]{1,0:T(8,128)}, f32[512,128]{1,0:T(8,128)S(1)}, u32[]{:S(2)}, u32[]{:S(2)}) collective-permute-start(f32[512,128]{1,0:T(8,128)} %bitcast.18), channel_id=1, source_target_pairs={{0,1},{1,0},{2,3},{3,2},{4,5},{5,4},{6,7},{7,6},{8,9},{9,8},{10,11... | collective-permute-start | bytes 786440 | tf_op jit(solution)/shard_map/ppermute | solution.py:185
  8.3 6.3 %collective-permute-start.2 = (f32[256,128]{1,0:T(8,128)S(1)}, f32[256,128]{1,0:T(8,128)S(1)}, u32[]{:S(2)}, u32[]{:S(2)}) collective-permute-start(f32[256,128]{1,0:T(8,128)S(1)} %bitcast.25), channel_id=1, source_target_pairs={{0,4},{4,0},{8,12},{12,8},{16,20},{20,16},{24,28},{28,24},{32,36},... | collective-permute-start | bytes 393224 | tf_op jit(solution)/shard_map/ppermute | solution.py:165
  9.9 14.5 %copy-start = (f32[32,8,2,128]{3,2,1,0:T(2,128)S(1)}, f32[32,8,2,128]{3,2,1,0:T(2,128)}, u32[]{:S(2)}) copy-start(f32[32,8,2,128]{3,2,1,0:T(2,128)} %param.3) | copy-start | bytes 786436
  9.9 14.5 %copy-start.2 = (f32[32,8,2,128]{3,2,1,0:T(2,128)S(1)}, f32[32,8,2,128]{3,2,1,0:T(2,128)}, u32[]{:S(2)}) copy-start(f32[32,8,2,128]{3,2,1,0:T(2,128)} %param.4) | copy-start | bytes 786436
  9.9 14.4 %collective-permute-start.3 = (f32[256,128]{1,0:T(8,128)S(1)}, f32[256,128]{1,0:T(8,128)S(1)}, u32[]{:S(2)}, u32[]{:S(2)}) collective-permute-start(f32[256,128]{1,0:T(8,128)S(1)} %bitcast.24), channel_id=1, source_target_pairs={{4,8},{12,16},{20,24},{28,32},{36,40},{44,48},{52,56},{60,64},{68,... | collective-permute-start | bytes 393224 | tf_op jit(solution)/shard_map/ppermute | solution.py:166
  20.0 4.4 %collective-permute-start.4 = (f32[512,128]{1,0:T(8,128)S(1)}, f32[512,128]{1,0:T(8,128)S(1)}, u32[]{:S(2)}, u32[]{:S(2)}) collective-permute-start(f32[512,128]{1,0:T(8,128)S(1)} %collective-permute-done.1.refs_5_.refs_3_), channel_id=1, source_target_pairs={{0,1},{1,0},{2,3},{3,2},{4,5},{5,4},{6,7},{7,6},{8,9},{9,8},{10,11... | collective-permute-start | bytes 786440 | tf_op jit(solution)/shard_map/ppermute | solution.py:190
  27.8 4.5 %copy-start.1 = (f32[3,3,3,32,128]{4,3,2,1,0:T(8,128)S(1)}, f32[3,3,3,32,128]{4,3,2,1,0:T(8,128)}, u32[]{:S(2)}) copy-start(f32[3,3,3,32,128]{4,3,2,1,0:T(8,128)} %param.5) | copy-start | bytes 1327108
  27.8 15.1 %all-to-all-start = ((f32[16,27,2,128]{3,2,1,0:T(2,128)}), f32[16,27,2,128]{3,2,1,0:T(2,128)S(1)}, u32[]{:S(2)}, u32[]{:S(2)}) async-start(f32[16,27,2,128]{3,2,1,0:T(2,128)} %bitcast.10), calls=%async_computation | async-start | bytes 884736 | tf_op jit(solution)/shard_map/all_to_all | solution.py:136
  34.4 21.3 %collective-permute-start.5 = (f32[256,128]{1,0:T(8,128)S(1)}, f32[256,128]{1,0:T(8,128)S(1)}, u32[]{:S(2)}, u32[]{:S(2)}) collective-permute-start(f32[256,128]{1,0:T(8,128)S(1)} %get-tuple-element.28), channel_id=1, source_target_pairs={{0,4},{4,0},{8,12},{12,8},{16,20},{20,16},{24,28},{28,24},{32,36},... | collective-permute-start | bytes 393224 | tf_op jit(solution)/shard_map/ppermute | solution.py:165
  36.4 19.3 %collective-permute-start.6 = (f32[256,128]{1,0:T(8,128)S(1)}, f32[256,128]{1,0:T(8,128)S(1)}, u32[]{:S(2)}, u32[]{:S(2)}) collective-permute-start(f32[256,128]{1,0:T(8,128)S(1)} %get-tuple-element.29), channel_id=1, source_target_pairs={{4,8},{12,16},{20,24},{28,32},{36,40},{44,48},{52,56},{60,64},{68,... | collective-permute-start | bytes 393224 | tf_op jit(solution)/shard_map/ppermute | solution.py:166
  43.0 4.6 %collective-permute-start.9 = (f32[27,2,128]{2,1,0:T(2,128)S(1)}, f32[27,2,128]{2,1,0:T(2,128)S(1)}, u32[]{:S(2)}, u32[]{:S(2)}) collective-permute-start(f32[27,2,128]{2,1,0:T(2,128)S(1)} %reduce_sum.9.a), channel_id=1, source_target_pairs={{0,48},{4,52},{8,56},{12,60},{16,32},{20,36},{24,40},{28,44},{32,1... | collective-permute-start | bytes 82952 | tf_op jit(solution)/shard_map/ppermute | solution.py:146
  44.9 4.8 %collective-permute-start.8 = (f32[27,2,128]{2,1,0:T(2,128)S(1)}, f32[27,2,128]{2,1,0:T(2,128)S(1)}, u32[]{:S(2)}, u32[]{:S(2)}) collective-permute-start(f32[27,2,128]{2,1,0:T(2,128)S(1)} %reduce_sum.9.a), channel_id=1, source_target_pairs={{0,32},{4,36},{8,40},{12,44},{16,48},{20,52},{24,56},{28,60},{32,0... | collective-permute-start | bytes 82952 | tf_op jit(solution)/shard_map/ppermute | solution.py:146
  46.9 3.9 %collective-permute-start.7 = (f32[27,2,128]{2,1,0:T(2,128)S(1)}, f32[27,2,128]{2,1,0:T(2,128)S(1)}, u32[]{:S(2)}, u32[]{:S(2)}) collective-permute-start(f32[27,2,128]{2,1,0:T(2,128)S(1)} %reduce_sum.9.a), channel_id=1, source_target_pairs={{0,16},{4,20},{8,24},{12,28},{16,0},{20,4},{24,8},{28,12},{32,48},... | collective-permute-start | bytes 82952 | tf_op jit(solution)/shard_map/ppermute | solution.py:146
  51.6 13.5 %all-to-all-start.1 = ((f32[16,27,2,128]{3,2,1,0:T(2,128)}), f32[16,27,2,128]{3,2,1,0:T(2,128)S(1)}, u32[]{:S(2)}, u32[]{:S(2)}) async-start(f32[16,27,2,128]{3,2,1,0:T(2,128)} %spread_kernel.1), calls=%async_computation.1 | async-start | bytes 884736 | tf_op jit(solution)/shard_map/all_to_all | solution.py:156
